TPU v7x, 32 devices: a whole 2x2x4 slice. The times are simulated.
32 devices in a mesh: dp: 8 (over z, x), tensor: 4 (over y, core).
Axes of the slice: x: 2, y: 2, z: 4, core: 2. Of those that a mesh axis runs over, the one named last changes fastest.
Arguments:
- patch_rows: bfloat16 [256, 32, 768], P('tensor', 'dp'), may hold values from -6 to 6
- cotangent: bfloat16 [256, 32, 768], P('tensor', 'dp'), may hold values from -6 to 6
- mask_flags: int32 [256, 32], P('tensor', 'dp'), may hold values from 0 to 1, as said below
- pad_flags: int32 [256, 32], P(None, 'dp'), may hold values from 0 to 1, as said below
- buckets: int32 [256, 256], replicated, may hold values from 0 to 731, as said below
- mask_emb: bfloat16 [768], replicated, may hold values from -6 to 6
- ln1_gain: bfloat16 [2, 768], replicated, may hold values from 0.5 to 1.5
- ln1_bias: bfloat16 [2, 768], replicated, may hold values from -1.75 to 1.75
- w_qkv: bfloat16 [2, 3, 768, 768], P(None, None, None, 'tensor'), may hold values from -0.21875 to 0.21875
- qv_bias: bfloat16 [2, 2, 768], P(None, None, 'tensor'), may hold values from -3 to 3
- rel_table: bfloat16 [2, 12, 732], P(None, 'tensor'), may hold values from -6 to 6
- w_out: bfloat16 [2, 768, 768], P(None, 'tensor'), may hold values from -0.625 to 0.625
- out_bias: bfloat16 [2, 768], replicated, may hold values from -1.75 to 1.75
- ln2_gain: bfloat16 [2, 768], replicated, may hold values from 0.5 to 1.5
- ln2_bias: bfloat16 [2, 768], replicated, may hold values from -1.75 to 1.75
- w_up: bfloat16 [2, 768, 3072], P(None, None, 'tensor'), may hold values from -0.21875 to 0.21875
- up_bias: bfloat16 [2, 3072], P(None, 'tensor'), may hold values from -1.75 to 1.75
- w_down: bfloat16 [2, 3072, 768], P(None, 'tensor'), may hold values from -0.109375 to 0.109375
- down_bias: bfloat16 [2, 768], replicated, may hold values from -1.75 to 1.75
Outputs:
- layer_out: bfloat16 [256, 32, 768], P('tensor', 'dp')
- d_x: float32 [256, 32, 768], P('tensor', 'dp')
- d_mask_emb: float32 [768], replicated
- d_ln1_gain: float32 [2, 768], replicated
- d_ln1_bias: float32 [2, 768], replicated
- d_w_qkv: float32 [2, 3, 768, 768], P(None, None, None, 'tensor')
- d_qv_bias: float32 [2, 2, 768], P(None, None, 'tensor')
- d_rel_table: float32 [2, 12, 732], P(None, 'tensor')
- d_w_out: float32 [2, 768, 768], P(None, 'tensor')
- d_out_bias: float32 [2, 768], replicated
- d_ln2_gain: float32 [2, 768], replicated
- d_ln2_bias: float32 [2, 768], replicated
- d_w_up: float32 [2, 768, 3072], P(None, None, 'tensor')
- d_up_bias: float32 [2, 3072], P(None, 'tensor')
- d_w_down: float32 [2, 3072, 768], P(None, 'tensor')
- d_down_bias: float32 [2, 768], replicated
Inputs may be any that keep to these rules, and one draw needn't show every extreme that they name: `mask_flags`: each page has its own masking rate, drawn from 20 to 60 percent. `pad_flags`: in each page the rows from its patch count on are 1, the patch count between 160 and 197. `buckets`: the bucket depends only on the two rows' places in the 14 x 14 patch grid, or on class or padding rows.
All inputs are finite; a program needn't handle non-finite values.
Results may differ from a plain program's by a relative error of at most 0.025.
Values may be sent and summed in bfloat16 or wider, within the bound.
No kernel may reach another device: no remote copies, remote signals or barrier semaphores. Data moves between devices by JAX's collectives and lax.ppermute only.
A program may use at most 192 MiB of HBM per device.

v0:
```python
import jax
import jax.numpy as jnp
from jax import lax
from jax.sharding import PartitionSpec as P

HEAD_DIM = 64
BUCKETS = 732
LAYERS = 2


EPSILON = 1e-06


def norm_rows(values, norm_gain, norm_shift):
    center = values - jnp.mean(values, axis=-1, keepdims=True)
    spread = jnp.mean(center * center, axis=-1, keepdims=True)
    return center * lax.rsqrt(spread + EPSILON) * norm_gain + norm_shift


def gelu_tanh(values):
    return jax.nn.gelu(values, approximate=True)


def gather_product(local_rows, matrix, einsum_form):
    block_rows = lax.all_gather(local_rows, "tensor", axis=0, tiled=True)
    return (
        block_rows,
        jnp.einsum(einsum_form, block_rows, matrix, preferred_element_type=jnp.float32),
    )


def scatter_product(full_rows, matrix, einsum_form):
    return lax.psum_scatter(
        jnp.einsum(einsum_form, full_rows, matrix, preferred_element_type=jnp.float32).astype(
            jnp.bfloat16
        ),
        "tensor",
        scatter_dimension=0,
        tiled=True,
    ).astype(jnp.float32)


def attend_scores(query_rows, key_rows, rel_bias, key_bias):
    return (
        jnp.einsum("qphe,kphe->phqk", query_rows, key_rows, preferred_element_type=jnp.float32)
        + rel_bias[None]
        + key_bias
    )


def layer_forward(hidden, layer_weights, key_bias, buckets):
    (
        gain_one,
        shift_one,
        w_qkv,
        qv_bias,
        rel_table,
        w_out,
        out_bias,
        gain_two,
        shift_two,
        w_up,
        up_bias,
        w_down,
        down_bias,
    ) = layer_weights
    normed = norm_rows(hidden, gain_one, shift_one).astype(jnp.bfloat16)
    normed_all, projected = gather_product(normed, w_qkv, "spd,tde->spte")
    seq_rows, page_count, local_width = (normed_all.shape[0], normed_all.shape[1], w_qkv.shape[2])
    head_shape = (seq_rows, page_count, local_width // HEAD_DIM, HEAD_DIM)
    query_scale = HEAD_DIM ** (-0.5)
    query_rows = (
        ((projected[:, :, 0] + qv_bias[0]) * query_scale).astype(jnp.bfloat16).reshape(head_shape)
    )
    key_rows = projected[:, :, 1].astype(jnp.bfloat16).reshape(head_shape)
    value_rows = (projected[:, :, 2] + qv_bias[1]).astype(jnp.bfloat16).reshape(head_shape)
    rel_bias = rel_table[:, buckets]
    scores = attend_scores(query_rows, key_rows, rel_bias, key_bias)
    row_max = jnp.max(scores, axis=-1, keepdims=True)
    log_total = row_max + jnp.log(jnp.sum(jnp.exp(scores - row_max), axis=-1, keepdims=True))
    softmax_weights = jnp.exp(scores - log_total).astype(jnp.bfloat16)
    attended = jnp.einsum(
        "phqk,kphe->qphe", softmax_weights, value_rows, preferred_element_type=jnp.float32
    )
    attended = attended.reshape(seq_rows, page_count, local_width).astype(jnp.bfloat16)
    mixed = scatter_product(attended, w_out, "spe,ed->spd")
    after_mixer = hidden + mixed + out_bias
    normed_two = norm_rows(after_mixer, gain_two, shift_two).astype(jnp.bfloat16)
    normed_two_all, pre_act = gather_product(normed_two, w_up, "spd,df->spf")
    pre_act = pre_act + up_bias
    activated = gelu_tanh(pre_act).astype(jnp.bfloat16)
    layer_output = after_mixer + scatter_product(activated, w_down, "spf,fd->spd") + down_bias
    kept_values = (
        hidden,
        normed_all,
        query_rows,
        key_rows,
        value_rows,
        rel_bias,
        log_total,
        attended,
        after_mixer,
        normed_two_all,
        pre_act,
        activated,
    )
    return (layer_output, kept_values)


def layer_backward(grad_output, kept_values, layer_weights, key_bias, buckets):
    (
        gain_one,
        shift_one,
        w_qkv,
        qv_bias,
        rel_table,
        w_out,
        out_bias,
        gain_two,
        shift_two,
        w_up,
        up_bias,
        w_down,
        down_bias,
    ) = layer_weights
    (
        hidden,
        normed_all,
        query_rows,
        key_rows,
        value_rows,
        rel_bias,
        log_total,
        attended,
        after_mixer,
        normed_two_all,
        pre_act,
        activated,
    ) = kept_values
    seq_rows, page_count, local_width = attended.shape
    query_scale = HEAD_DIM ** (-0.5)
    grad_down_bias = jnp.sum(grad_output, axis=(0, 1))
    grad_low = grad_output.astype(jnp.bfloat16)
    grad_low_all, grad_act = gather_product(grad_low, w_down, "spd,fd->spf")
    grad_w_down = jnp.einsum(
        "spf,spd->fd", activated, grad_low_all, preferred_element_type=jnp.float32
    )
    unused_value, gelu_pull = jax.vjp(gelu_tanh, pre_act)
    grad_pre = gelu_pull(grad_act)[0].astype(jnp.bfloat16)
    grad_up_bias = jnp.sum(grad_pre.astype(jnp.float32), axis=(0, 1))
    grad_w_up = jnp.einsum(
        "spd,spf->df", normed_two_all, grad_pre, preferred_element_type=jnp.float32
    )
    grad_normed_two = scatter_product(grad_pre, w_up, "spf,df->spd")
    unused_value, norm_pull_two = jax.vjp(norm_rows, after_mixer, gain_two, shift_two)
    grad_mixer_norm, grad_gain_two, grad_shift_two = norm_pull_two(grad_normed_two)
    grad_mixer = grad_output + grad_mixer_norm
    grad_out_bias = jnp.sum(grad_mixer, axis=(0, 1))
    grad_mixer_low = grad_mixer.astype(jnp.bfloat16)
    grad_mixer_all, grad_attended = gather_product(grad_mixer_low, w_out, "spd,ed->spe")
    grad_w_out = jnp.einsum(
        "spe,spd->ed", attended, grad_mixer_all, preferred_element_type=jnp.float32
    )
    grad_heads = grad_attended.astype(jnp.bfloat16).reshape(query_rows.shape)
    scores = attend_scores(query_rows, key_rows, rel_bias, key_bias)
    softmax_full = jnp.exp(scores - log_total)
    softmax_weights = softmax_full.astype(jnp.bfloat16)
    grad_values = jnp.einsum(
        "phqk,qphe->kphe", softmax_weights, grad_heads, preferred_element_type=jnp.float32
    ).astype(jnp.bfloat16)
    grad_weights = jnp.einsum(
        "qphe,kphe->phqk", grad_heads, value_rows, preferred_element_type=jnp.float32
    )
    row_inner = jnp.sum(softmax_full * grad_weights, axis=-1, keepdims=True)
    grad_scores = (softmax_full * (grad_weights - row_inner)).astype(jnp.bfloat16)
    score_totals = jnp.sum(grad_scores.astype(jnp.float32), axis=0)
    head_count = score_totals.shape[0]
    grad_rel_table = jax.ops.segment_sum(
        score_totals.reshape(head_count, -1).T, buckets.reshape(-1), num_segments=BUCKETS
    ).T
    grad_queries = (
        jnp.einsum(
            "phqk,kphe->qphe", grad_scores, key_rows, preferred_element_type=jnp.float32
        ).astype(jnp.bfloat16)
        * query_scale
    )
    grad_keys = jnp.einsum(
        "phqk,qphe->kphe", grad_scores, query_rows, preferred_element_type=jnp.float32
    ).astype(jnp.bfloat16)
    flat_shape = (seq_rows, page_count, local_width)
    grad_projected = jnp.stack(
        [
            grad_queries.reshape(flat_shape),
            grad_keys.reshape(flat_shape),
            grad_values.reshape(flat_shape),
        ],
        axis=2,
    )
    grad_qv_bias = jnp.stack(
        [
            jnp.sum(grad_queries.reshape(flat_shape).astype(jnp.float32), axis=(0, 1)),
            jnp.sum(grad_values.reshape(flat_shape).astype(jnp.float32), axis=(0, 1)),
        ]
    )
    grad_w_qkv = jnp.einsum(
        "spd,spte->tde", normed_all, grad_projected, preferred_element_type=jnp.float32
    )
    grad_normed = scatter_product(grad_projected, w_qkv, "spte,tde->spd")
    unused_value, norm_pull_one = jax.vjp(norm_rows, hidden, gain_one, shift_one)
    grad_hidden_norm, grad_gain_one, grad_shift_one = norm_pull_one(grad_normed)
    grad_hidden = grad_mixer + grad_hidden_norm
    large_grads = (
        grad_w_qkv,
        grad_qv_bias,
        grad_rel_table,
        grad_w_out,
        grad_w_up,
        grad_up_bias,
        grad_w_down,
    )
    small_grads = (
        grad_gain_one,
        grad_shift_one,
        grad_out_bias,
        grad_gain_two,
        grad_shift_two,
        grad_down_bias,
    )
    return (grad_hidden, large_grads, small_grads)


def shards(
    patch_rows,
    cotangent,
    mask_flags,
    pad_flags,
    buckets,
    mask_emb,
    ln1_gain,
    ln1_bias,
    w_qkv,
    qv_bias,
    rel_table,
    w_out,
    out_bias,
    ln2_gain,
    ln2_bias,
    w_up,
    up_bias,
    w_down,
    down_bias,
):
    masked = (mask_flags == 1)[..., None]
    hidden = jnp.where(masked, mask_emb.astype(jnp.float32), patch_rows.astype(jnp.float32))
    key_bias = jnp.where(pad_flags == 1, -1000000000.0, 0.0).astype(jnp.float32).T[:, None, None, :]

    def weights_of(layer_index):
        return (
            ln1_gain[layer_index].astype(jnp.float32),
            ln1_bias[layer_index].astype(jnp.float32),
            w_qkv[layer_index],
            qv_bias[layer_index].astype(jnp.float32),
            rel_table[layer_index].astype(jnp.float32),
            w_out[layer_index],
            out_bias[layer_index].astype(jnp.float32),
            ln2_gain[layer_index].astype(jnp.float32),
            ln2_bias[layer_index].astype(jnp.float32),
            w_up[layer_index],
            up_bias[layer_index].astype(jnp.float32),
            w_down[layer_index],
            down_bias[layer_index].astype(jnp.float32),
        )

    layer_inputs = []
    stash_list = []
    for layer_index in range(LAYERS):
        layer_inputs.append(hidden)
        hidden, kept_values = layer_forward(hidden, weights_of(layer_index), key_bias, buckets)
        stash_list.append(kept_values)
    result = hidden.astype(jnp.bfloat16)
    grad_hidden = cotangent.astype(jnp.float32)
    large_list = [None] * LAYERS
    small_list = [None] * LAYERS
    for layer_index in reversed(range(LAYERS)):
        layer_weights = weights_of(layer_index)
        kept_values = stash_list[layer_index]
        grad_hidden, large_grads, small_grads = layer_backward(
            grad_hidden, kept_values, layer_weights, key_bias, buckets
        )
        large_list[layer_index] = large_grads
        small_list[layer_index] = small_grads
    stacked_large = tuple((jnp.stack(members) for members in zip(*large_list)))
    stacked_large = lax.psum(stacked_large, "dp")
    stacked_small = tuple((jnp.stack(members) for members in zip(*small_list)))
    mask_grad = jnp.sum(jnp.where(masked, grad_hidden, 0.0), axis=(0, 1))
    summed_small = lax.psum(stacked_small + (mask_grad,), ("dp", "tensor"))
    grad_input = jnp.where(masked, 0.0, grad_hidden)
    grad_w_qkv, grad_qv_bias, grad_rel_table, grad_w_out, grad_w_up, grad_up_bias, grad_w_down = (
        stacked_large
    )
    (
        grad_gain_one,
        grad_shift_one,
        grad_out_bias,
        grad_gain_two,
        grad_shift_two,
        grad_down_bias,
        grad_mask,
    ) = summed_small
    return (
        result,
        grad_input,
        grad_mask,
        grad_gain_one,
        grad_shift_one,
        grad_w_qkv,
        grad_qv_bias,
        grad_rel_table,
        grad_w_out,
        grad_out_bias,
        grad_gain_two,
        grad_shift_two,
        grad_w_up,
        grad_up_bias,
        grad_w_down,
        grad_down_bias,
    )


def solution(mesh):
    placed = (
        P("tensor", "dp", None),
        P("tensor", "dp", None),
        P("tensor", "dp"),
        P(None, "dp"),
        P(),
        P(),
        P(),
        P(),
        P(None, None, None, "tensor"),
        P(None, None, "tensor"),
        P(None, "tensor", None),
        P(None, "tensor", None),
        P(),
        P(),
        P(),
        P(None, None, "tensor"),
        P(None, "tensor"),
        P(None, "tensor", None),
        P(),
    )
    return jax.shard_map(
        shards,
        mesh=mesh,
        in_specs=placed,
        out_specs=(
            P("tensor", "dp", None),
            P("tensor", "dp", None),
            P(),
            P(),
            P(),
            P(None, None, None, "tensor"),
            P(None, None, "tensor"),
            P(None, "tensor", None),
            P(None, "tensor", None),
            P(),
            P(),
            P(),
            P(None, None, "tensor"),
            P(None, "tensor"),
            P(None, "tensor", None),
            P(),
        ),
        check_vma=False,
    )
```

profile of v0, /device:TPU:0, one launch (start us, length us, event | category | flops | bytes accessed | tf_op | source)
XLA Modules:
  0.0 1854.0 jit_solution(12692917503913096444)
XLA Ops:
  12.5 2.0 add_convert_fusion.6
  17.7 216.0 %gather_fusion = f32[65536,3]{1,0:T(8,128)} fusion(f32[3,732]{0,1:T(8,128)S(1)} %bitcast_convert_fusion.3, s32[65536]{0:T(1024)S(1)} %broadcast_clamp_fusion), kind=kCustom, calls=%fused_computation | custom fusion | bytes 1835008 | tf_op jit(solution)/shard_map/gather | solution.py:77
  233.7 19.1 %copy.94 = f32[256,256,3]{0,1,2:T(8,128)S(1)} copy(f32[256,256,3]{2,1,0:T(8,128)} %bitcast.222) | data formatting | bytes 1572864 | tf_op jit(solution)/shard_map/gather | solution.py:77
  252.9 2.8 fusion.24
  260.7 1.8 convolution_convert_fusion.5
  263.8 29.7 %reduce-scatter.9.cloned.1.call-done = bf16[64,4,768]{2,0,1:T(8,128)(2,1)} async-done(((bf16[256,4,768]{2,0,1:T(8,128)(2,1)}), bf16[64,4,768]{2,0,1:T(8,128)(2,1)}) %reduce-scatter.9.cloned.1.call-update) | async-done | bytes 393232 | tf_op jit(solution)/shard_map/reduce_scatter | solution.py:33
  296.2 2.1 add_convert_fusion.4
  299.0 19.1 %all-gather.11.cloned.1.call-done = bf16[256,4,768]{2,0,1:T(8,128)(2,1)} async-done(((bf16[64,4,768]{2,0,1:T(8,128)(2,1)}), bf16[256,4,768]{2,0,1:T(8,128)(2,1)}) %all-gather.11.cloned.1.call-update) | async-done | bytes 1572880 | tf_op jit(solution)/shard_map/all_gather | solution.py:25
  318.1 3.3 fusion.42
  323.1 3.3 convolution_convert_fusion.4
  327.1 27.7 %reduce-scatter.11.cloned.1.call-done = bf16[64,4,768]{2,0,1:T(8,128)(2,1)} async-done(((bf16[256,4,768]{2,0,1:T(8,128)(2,1)}), bf16[64,4,768]{2,0,1:T(8,128)(2,1)}) %reduce-scatter.11.cloned.1.call-update) | async-done | bytes 393232 | tf_op jit(solution)/shard_map/reduce_scatter | solution.py:33
  359.9 216.0 %gather_fusion.1 = f32[65536,3]{1,0:T(8,128)} fusion(f32[3,732]{0,1:T(8,128)S(1)} %bitcast_convert_fusion.2, s32[65536]{0:T(1024)S(1)} %broadcast_clamp_fusion), kind=kCustom, calls=%fused_computation.1 | custom fusion | bytes 1835008 | tf_op jit(solution)/shard_map/gather | solution.py:77
  575.8 19.7 %copy.97 = f32[256,256,3]{0,1,2:T(8,128)} copy(f32[256,256,3]{2,1,0:T(8,128)} %bitcast.221) | data formatting | bytes 1572864 | tf_op jit(solution)/shard_map/gather | solution.py:77
  595.5 2.5 fusion.20
  603.0 1.8 convolution_convert_fusion.3
  604.8 28.3 %reduce-scatter.13.cloned.1.call-done = bf16[64,4,768]{2,0,1:T(8,128)(2,1)} async-done(((bf16[256,4,768]{2,0,1:T(8,128)(2,1)}), bf16[64,4,768]{2,0,1:T(8,128)(2,1)}) %reduce-scatter.13.cloned.1.call-update) | async-done | bytes 393232 | tf_op jit(solution)/shard_map/reduce_scatter | solution.py:33
  637.7 1.8 copy.99
  639.5 17.9 all-gather.15.cloned.1.call-done
  657.5 4.8 fusion.37
  662.3 16.5 all-gather.17.cloned.1.call-done
  678.8 6.5 convert_reduce_fusion
  686.4 2.6 convolution_convert_fusion.1
  689.5 5.5 convolution_convert_fusion.2
  695.1 22.3 %reduce-scatter.17.cloned.1.call-done = bf16[64,4,768]{2,0,1:T(8,128)(2,1)} async-done(((bf16[256,4,768]{2,0,1:T(8,128)(2,1)}), bf16[64,4,768]{2,0,1:T(8,128)(2,1)}) %reduce-scatter.17.cloned.1.call-update) | async-done | bytes 393232 | tf_op jit(solution)/shard_map/reduce_scatter | solution.py:33
  717.4 2.1 convert_reduce_fusion.7
  720.8 2.3 fusion.68
  723.7 24.3 %reduce-scatter.15.cloned.1.call-done = bf16[64,4,768]{2,0,1:T(8,128)(2,1)} async-done(((bf16[256,4,768]{2,0,1:T(8,128)(2,1)}), bf16[64,4,768]{2,0,1:T(8,128)(2,1)}) %reduce-scatter.15.cloned.1.call-update) | async-done | bytes 393232 | tf_op jit(solution)/shard_map/reduce_scatter | solution.py:33
  748.0 3.3 fusion.118
  753.0 19.8 %all-gather.19.cloned.1.call-done = bf16[256,4,768]{2,0,1:T(8,128)(2,1)} async-done(((bf16[64,4,768]{2,0,1:T(8,128)(2,1)}), bf16[256,4,768]{2,0,1:T(8,128)(2,1)}) %all-gather.19.cloned.1.call-update) | async-done | bytes 1572880 | tf_op jit(solution)/shard_map/all_gather | solution.py:25
  772.7 2.2 convolution_convert_fusion.13
  775.0 2.7 convert_reduce_fusion.9
  779.1 1.9 convert_reduce_fusion.2
  783.5 2.6 bitcast_convert_fusion.1
  786.2 28.3 %reduce-scatter.19.cloned.1.call-done = bf16[64,4,768]{2,0,1:T(8,128)(2,1)} async-done(((bf16[256,4,768]{2,0,1:T(8,128)(2,1)}), bf16[64,4,768]{2,0,1:T(8,128)(2,1)}) %reduce-scatter.19.cloned.1.call-update) | async-done | bytes 393232 | tf_op jit(solution)/shard_map/reduce_scatter | solution.py:33
  814.5 1.8 convert_reduce_fusion.6
  816.3 2.1 fusion.69
  818.4 1.9 fusion.117
  821.4 19.6 %all-gather.21.cloned.1.call-done = bf16[256,4,768]{2,0,1:T(8,128)(2,1)} async-done(((bf16[64,4,768]{2,0,1:T(8,128)(2,1)}), bf16[256,4,768]{2,0,1:T(8,128)(2,1)}) %all-gather.21.cloned.1.call-update) | async-done | bytes 1572880 | tf_op jit(solution)/shard_map/all_gather | solution.py:25
  841.0 6.3 convert_reduce_fusion.1
  848.5 3.9 convolution_convert_fusion
  852.5 28.3 %reduce-scatter.21.cloned.1.call-done = bf16[64,4,768]{2,0,1:T(8,128)(2,1)} async-done(((bf16[256,4,768]{2,0,1:T(8,128)(2,1)}), bf16[64,4,768]{2,0,1:T(8,128)(2,1)}) %reduce-scatter.21.cloned.1.call-update) | async-done | bytes 393232 | tf_op jit(solution)/shard_map/reduce_scatter | solution.py:33
  880.8 2.0 convert_reduce_fusion.5
  882.8 2.3 fusion.70
  885.1 2.4 fusion.119
  887.7 5.9 convolution_bitcast_fusion
  893.5 13.9 all-gather.23.cloned.1.call-done
  907.4 2.2 convolution_convert_fusion.9
  909.7 2.7 convert_reduce_fusion.11
  913.7 2.0 convert_reduce_fusion.3
  917.4 2.7 bitcast_convert_fusion
  920.4 3.5 convolution_bitcast_fusion.2
  927.0 1.9 convolution_bitcast_fusion.1
  929.0 2.7 pad_maximum_fusion.1
  934.0 2.5 pad_maximum_fusion
  939.6 2.1 pad_maximum_fusion.2
  945.1 16.3 copy.116
  961.4 387.6 %scatter_custom_fusion.1 = f32[732,3]{1,0:T(8,128)S(1)} fusion(s32[65536]{0:T(1024)S(1)} %bitcast.275, f32[65536,3]{1,0:T(8,128)} %copy.116, f32[]{:T(128)} %constant.37.clone.1), kind=kCustom, calls=%fused_computation.191 | custom fusion | flops 196608 | bytes 9296 | tf_op jit(solution)/shard_map/scatter-add | solution.py:178
  1350.4 16.0 copy.114
  1366.4 387.3 %scatter_custom_fusion = f32[732,3]{1,0:T(8,128)S(1)} fusion(s32[65536]{0:T(1024)S(1)} %bitcast.276, f32[65536,3]{1,0:T(8,128)} %copy.114, f32[]{:T(128)} %constant.37.clone.1), kind=kCustom, calls=%fused_computation.193 | custom fusion | flops 196608 | bytes 9296 | tf_op jit(solution)/shard_map/scatter-add | solution.py:178
  1753.9 37.9 %all-reduce.1 = (f32[2,2,192]{2,1,0:T(2,128)}, f32[2,3,732]{2,0,1:T(2,128)}, f32[2,768]{1,0:T(2,128)}) all-reduce(f32[2,2,192]{2,1,0:T(2,128)S(1)} %pad_maximum_fusion.18, f32[2,3,732]{2,0,1:T(2,128)S(1)} %pad_maximum_fusion.10, f32[2,768]{1,0:T(2,128)S(1)} %pad_maximum_fusion.16), channel_id=1, replica_groups=mesh['dp'=8,'tensor'=4] {'dp'}, use_global_device_ids=true, to_apply=%region_43.44 | all-reduce | flops 6696 | bytes 53568 | tf_op jit(solution)/shard_map/psum | solution.py:293
  1797.7 38.2 %all-reduce = (f32[768]{0:T(1024)}, f32[2,768]{1,0:T(2,128)}, f32[2,768]{1,0:T(2,128)}, f32[2,768]{1,0:T(2,128)}, f32[2,768]{1,0:T(2,128)}, /*index=5*/f32[2,768]{1,0:T(2,128)}, f32[2,768]{1,0:T(2,128)}) all-reduce(f32[768]{0:T(1024)S(1)} %get-tuple-element.71, ...), channel_id=1, replica_groups=mesh['dp'=8,'tensor'=4] {'dp','tensor'}, use_global_device_ids=true, to_apply=%region_31.32 | all-reduce | flops 9984 | bytes 79872 | tf_op jit(solution)/shard_map/psum | solution.py:296
  1835.9 4.4 copy.178
  1841.3 2.4 copy.180
  1844.9 2.2 copy.181
  (422 shorter events, 70.6 us)
Async XLA Ops:
  7.2 245.7 %all-gather.9.cloned.1.call-start = ((), (), s32[]{:S(2)}) async-start(), calls=%async_computation.8 | async-start | bytes 1966080 | tf_op jit(solution)/shard_map/all_gather | solution.py:25
  7.9 346.8 %copy-start.55 = (pred[64,4]{0,1:T(4,128)(4,1)}, pred[64,4]{0,1:T(4,128)(4,1)S(1)}, u32[]{:S(2)}) copy-start(pred[64,4]{0,1:T(4,128)(4,1)S(1)} %broadcast_compare_fusion) | copy-start | bytes 772
  9.8 223.8 %copy-start.58 = (f32[64,4]{0,1:T(4,128)}, f32[64,4]{0,1:T(4,128)S(1)}, u32[]{:S(2)}) copy-start(f32[64,4]{0,1:T(4,128)S(1)} %broadcast_multiply_fusion.3) | copy-start | bytes 3076
  11.7 221.9 %copy-start.65 = (f32[64,4]{0,1:T(4,128)}, f32[64,4]{0,1:T(4,128)S(1)}, u32[]{:S(2)}) copy-start(f32[64,4]{0,1:T(4,128)S(1)} %fusion.100) | copy-start | bytes 3076
  14.6 278.9 %reduce-scatter.9.cloned.1.call-start = ((), (), s32[]{:S(2)}) async-start(), calls=%async_computation.9 | async-start | bytes 1966080 | tf_op jit(solution)/shard_map/reduce_scatter | solution.py:33
  17.2 241.1 %copy-start.99 = (f32[3,64]{1,0:T(4,128)}, f32[3,64]{1,0:T(4,128)S(1)}, u32[]{:S(2)}) copy-start(f32[3,64]{1,0:T(4,128)S(1)} %add.327) | copy-start | bytes 2308
  17.3 238.5 %copy-start.72 = (f32[3,64]{1,0:T(4,128)}, f32[3,64]{1,0:T(4,128)S(1)}, u32[]{:S(2)}) copy-start(f32[3,64]{1,0:T(4,128)S(1)} %add.330) | copy-start | bytes 2308
  233.7 19.1 %copy-start.108 = (s32[256,4]{0,1:T(4,128)S(1)}, s32[256,4]{0,1:T(4,128)}, u32[]{:S(2)}) copy-start(s32[256,4]{0,1:T(4,128)} %param.22) | copy-start | bytes 12292
  233.7 19.2 %copy-start.113 = (bf16[2,3,768,192]{2,3,1,0:T(8,128)(2,1)S(1)}, bf16[2,3,768,192]{2,3,1,0:T(8,128)(2,1)}, u32[]{:S(2)}) copy-start(bf16[2,3,768,192]{2,3,1,0:T(8,128)(2,1)} %param.27) | copy-start | bytes 5308420
  259.9 33.5 %copy-start = (bf16[64,4,768]{2,1,0:T(4,128)(2,1)S(1)}, bf16[64,4,768]{2,1,0:T(4,128)(2,1)}, u32[]{:S(2)}) copy-start(bf16[64,4,768]{2,1,0:T(4,128)(2,1)} %param.19) | copy-start | bytes 1179652
  260.7 37.7 %copy-start.95 = (bf16[2,768]{1,0:T(2,128)(2,1)S(1)}, bf16[2,768]{1,0:T(2,128)(2,1)}, u32[]{:S(2)}) copy-start(bf16[2,768]{1,0:T(2,128)(2,1)} %param.35) | copy-start | bytes 9220
  262.5 55.7 %all-gather.11.cloned.1.call-start = ((), (), s32[]{:S(2)}) async-start(), calls=%async_computation.10 | async-start | bytes 1966080 | tf_op jit(solution)/shard_map/all_gather | solution.py:25
  263.8 57.7 %copy-start.53 = (f32[768]{0:T(1024)}, f32[768]{0:T(1024)S(1)}, u32[]{:S(2)}) copy-start(f32[768]{0:T(1024)S(1)} %get-tuple-element.162) | copy-start | bytes 9220
  294.8 26.6 %copy-start.60 = (f32[64,4]{0,1:T(4,128)}, f32[64,4]{0,1:T(4,128)S(1)}, u32[]{:S(2)}) copy-start(f32[64,4]{0,1:T(4,128)S(1)} %broadcast_multiply_fusion.2) | copy-start | bytes 3076
  296.2 25.2 %copy-start.78 = (f32[64,4]{0,1:T(4,128)}, f32[64,4]{0,1:T(4,128)S(1)}, u32[]{:S(2)}) copy-start(f32[64,4]{0,1:T(4,128)S(1)} %multiply_reduce_fusion.4) | copy-start | bytes 3076
  296.2 25.2 %copy-start.67 = (f32[64,4]{0,1:T(4,128)}, f32[64,4]{0,1:T(4,128)S(1)}, u32[]{:S(2)}) copy-start(f32[64,4]{0,1:T(4,128)S(1)} %fusion.101) | copy-start | bytes 3076
  298.3 56.4 %reduce-scatter.11.cloned.1.call-start = ((), (), s32[]{:S(2)}) async-start(), calls=%async_computation.11 | async-start | bytes 1966080 | tf_op jit(solution)/shard_map/reduce_scatter | solution.py:33
  299.0 22.5 %copy-start.103 = (f32[768]{0:T(1024)}, f32[768]{0:T(1024)S(1)}, u32[]{:S(2)}) copy-start(f32[768]{0:T(1024)S(1)} %get-tuple-element.84) | copy-start | bytes 9220
  323.1 31.6 %copy-start.10 = (bf16[64,4,768]{2,0,1:T(8,128)(2,1)S(1)}, bf16[64,4,768]{2,0,1:T(8,128)(2,1)}, u32[]{:S(2)}) copy-start(bf16[64,4,768]{2,0,1:T(8,128)(2,1)} %reduce-scatter.9.cloned.1.call-done) | copy-start | bytes 1179652
  326.4 269.1 %all-gather.13.cloned.1.call-start = ((), (), s32[]{:S(2)}) async-start(), calls=%async_computation.12 | async-start | bytes 1966080 | tf_op jit(solution)/shard_map/all_gather | solution.py:25
  356.2 219.6 %copy-start.62 = (f32[64,4]{0,1:T(4,128)}, f32[64,4]{0,1:T(4,128)S(1)}, u32[]{:S(2)}) copy-start(f32[64,4]{0,1:T(4,128)S(1)} %broadcast_multiply_fusion.1) | copy-start | bytes 3076
  356.4 219.4 %copy-start.80 = (f32[64,4]{0,1:T(4,128)}, f32[64,4]{0,1:T(4,128)S(1)}, u32[]{:S(2)}) copy-start(f32[64,4]{0,1:T(4,128)S(1)} %multiply_reduce_fusion.3) | copy-start | bytes 3076
  356.5 219.4 %copy-start.69 = (f32[64,4]{0,1:T(4,128)}, f32[64,4]{0,1:T(4,128)S(1)}, u32[]{:S(2)}) copy-start(f32[64,4]{0,1:T(4,128)S(1)} %fusion.102) | copy-start | bytes 3076
  358.0 275.1 %reduce-scatter.13.cloned.1.call-start = ((), (), s32[]{:S(2)}) async-start(), calls=%async_computation.13 | async-start | bytes 1966080 | tf_op jit(solution)/shard_map/reduce_scatter | solution.py:33
  604.8 52.7 %all-gather.15.cloned.1.call-start = ((), (), s32[]{:S(2)}) async-start(), calls=%async_computation.14 | async-start | bytes 1966080 | tf_op jit(solution)/shard_map/all_gather | solution.py:25
  637.6 41.1 %all-gather.17.cloned.1.call-start = ((), (), s32[]{:S(2)}) async-start(), calls=%async_computation.16 | async-start | bytes 1966080 | tf_op jit(solution)/shard_map/all_gather | solution.py:25
  639.5 77.9 %reduce-scatter.17.cloned.1.call-start = ((), (), s32[]{:S(2)}) async-start(), calls=%async_computation.17 | async-start | bytes 1966080 | tf_op jit(solution)/shard_map/reduce_scatter | solution.py:33
  678.8 7.6 copy-start.112
  689.1 58.9 %reduce-scatter.15.cloned.1.call-start = ((), (), s32[]{:S(2)}) async-start(), calls=%async_computation.15 | async-start | bytes 1966080 | tf_op jit(solution)/shard_map/reduce_scatter | solution.py:33
  695.1 77.7 %all-gather.19.cloned.1.call-start = ((), (), s32[]{:S(2)}) async-start(), calls=%async_computation.18 | async-start | bytes 1966080 | tf_op jit(solution)/shard_map/all_gather | solution.py:25
  752.9 61.5 %reduce-scatter.19.cloned.1.call-start = ((), (), s32[]{:S(2)}) async-start(), calls=%async_computation.19 | async-start | bytes 1966080 | tf_op jit(solution)/shard_map/reduce_scatter | solution.py:33
  783.4 31.0 %copy-start.4 = (f32[64,4,768]{2,0,1:T(8,128)S(1)}, f32[64,4,768]{2,0,1:T(8,128)}, u32[]{:S(2)}) copy-start(f32[64,4,768]{2,0,1:T(8,128)} %copy-done.3) | copy-start | bytes 2359300
  783.5 31.0 %copy-start.63 = (f32[64,4]{0,1:T(4,128)S(1)}, f32[64,4]{0,1:T(4,128)}, u32[]{:S(2)}) copy-start(f32[64,4]{0,1:T(4,128)} %copy-done.62) | copy-start | bytes 3076
  783.5 32.9 %copy-start.81 = (f32[64,4]{0,1:T(4,128)S(1)}, f32[64,4]{0,1:T(4,128)}, u32[]{:S(2)}) copy-start(f32[64,4]{0,1:T(4,128)} %copy-done.80) | copy-start | bytes 3076
  783.5 32.9 %copy-start.70 = (f32[64,4]{0,1:T(4,128)S(1)}, f32[64,4]{0,1:T(4,128)}, u32[]{:S(2)}) copy-start(f32[64,4]{0,1:T(4,128)} %copy-done.69) | copy-start | bytes 3076
  786.1 32.3 %copy-start.13 = (f32[64,4,768]{2,0,1:T(8,128)S(1)}, f32[64,4,768]{2,0,1:T(8,128)}, u32[]{:S(2)}) copy-start(f32[64,4,768]{2,0,1:T(8,128)} %copy-done.12) | copy-start | bytes 2359300
  786.1 54.8 %copy-start.104 = (f32[768]{0:T(1024)S(1)}, f32[768]{0:T(1024)}, u32[]{:S(2)}) copy-start(f32[768]{0:T(1024)} %copy-done.103) | copy-start | bytes 9220
  786.1 54.8 %all-gather.21.cloned.1.call-start = ((), (), s32[]{:S(2)}) async-start(), calls=%async_computation.20 | async-start | bytes 1966080 | tf_op jit(solution)/shard_map/all_gather | solution.py:25
  821.1 59.6 %reduce-scatter.21.cloned.1.call-start = ((), (), s32[]{:S(2)}) async-start(), calls=%async_computation.21 | async-start | bytes 1966080 | tf_op jit(solution)/shard_map/reduce_scatter | solution.py:33
  848.5 32.3 %copy-start.11 = (bf16[64,4,768]{2,0,1:T(8,128)(2,1)S(1)}, bf16[64,4,768]{2,0,1:T(8,128)(2,1)}, u32[]{:S(2)}) copy-start(bf16[64,4,768]{2,0,1:T(8,128)(2,1)} %reduce-scatter.9.cloned.1.call-done) | copy-start | bytes 1179652
  848.5 32.3 %copy-start.54 = (f32[768]{0:T(1024)S(1)}, f32[768]{0:T(1024)}, u32[]{:S(2)}) copy-start(f32[768]{0:T(1024)} %copy-done.53) | copy-start | bytes 9220
  848.5 32.3 %copy-start.56 = (pred[64,4]{0,1:T(4,128)(4,1)S(1)}, pred[64,4]{0,1:T(4,128)(4,1)}, u32[]{:S(2)}) copy-start(pred[64,4]{0,1:T(4,128)(4,1)} %copy-done.55) | copy-start | bytes 772
  848.5 32.3 %copy-start.61 = (f32[64,4]{0,1:T(4,128)S(1)}, f32[64,4]{0,1:T(4,128)}, u32[]{:S(2)}) copy-start(f32[64,4]{0,1:T(4,128)} %copy-done.60) | copy-start | bytes 3076
  848.5 34.3 %copy-start.79 = (f32[64,4]{0,1:T(4,128)S(1)}, f32[64,4]{0,1:T(4,128)}, u32[]{:S(2)}) copy-start(f32[64,4]{0,1:T(4,128)} %copy-done.78) | copy-start | bytes 3076
  848.5 34.3 %copy-start.68 = (f32[64,4]{0,1:T(4,128)S(1)}, f32[64,4]{0,1:T(4,128)}, u32[]{:S(2)}) copy-start(f32[64,4]{0,1:T(4,128)} %copy-done.67) | copy-start | bytes 3076
  852.5 55.0 %all-gather.23.cloned.1.call-start = ((), (), s32[]{:S(2)}) async-start(), calls=%async_computation.22 | async-start | bytes 1966080 | tf_op jit(solution)/shard_map/all_gather | solution.py:25
  887.6 22.1 %copy-start.2 = (f32[4,3,256,256]{2,3,1,0:T(8,128)S(1)}, f32[4,3,256,256]{2,3,1,0:T(8,128)}, u32[]{:S(2)}) copy-start(f32[4,3,256,256]{2,3,1,0:T(8,128)} %copy-done.1) | copy-start | bytes 9437188
  887.6 904.2 %reduce-scatter.23.cloned.1.call-start = ((), (), s32[]{:S(2)}) async-start(), calls=%async_computation.23 | async-start | bytes 1966080 | tf_op jit(solution)/shard_map/reduce_scatter | solution.py:33
  893.5 18.9 %copy-start.100 = (f32[3,64]{1,0:T(4,128)S(1)}, f32[3,64]{1,0:T(4,128)}, u32[]{:S(2)}) copy-start(f32[3,64]{1,0:T(4,128)} %copy-done.99) | copy-start | bytes 2308
  920.1 915.8 %all-reduce.5.cloned.1.call-start = ((), (), s32[]{:S(2)}) async-start(), calls=%async_computation.24 | async-start | bytes 28311552 | tf_op jit(solution)/shard_map/psum | solution.py:293
  945.0 404.1 %copy-start.87 = (f32[768]{0:T(1024)S(1)}, f32[768]{0:T(1024)}, u32[]{:S(2)}) copy-start(f32[768]{0:T(1024)} %get-tuple-element.79) | copy-start | bytes 9220
  945.0 404.1 %copy-start.88 = (f32[768]{0:T(1024)S(1)}, f32[768]{0:T(1024)}, u32[]{:S(2)}) copy-start(f32[768]{0:T(1024)} %get-tuple-element.68) | copy-start | bytes 9220
  945.0 404.1 %copy-start.89 = (f32[768]{0:T(1024)S(1)}, f32[768]{0:T(1024)}, u32[]{:S(2)}) copy-start(f32[768]{0:T(1024)} %get-tuple-element.117) | copy-start | bytes 9220
  945.0 404.2 %copy-start.107 = (f32[768]{0:T(1024)S(1)}, f32[768]{0:T(1024)}, u32[]{:S(2)}) copy-start(f32[768]{0:T(1024)} %get-tuple-element.156) | copy-start | bytes 9220
  945.0 404.2 %copy-start.90 = (f32[768]{0:T(1024)S(1)}, f32[768]{0:T(1024)}, u32[]{:S(2)}) copy-start(f32[768]{0:T(1024)} %get-tuple-element.73) | copy-start | bytes 9220
  945.1 404.2 %copy-start.91 = (f32[768]{0:T(1024)S(1)}, f32[768]{0:T(1024)}, u32[]{:S(2)}) copy-start(f32[768]{0:T(1024)} %get-tuple-element.64) | copy-start | bytes 9220
  945.1 404.2 %copy-start.110 = (f32[3,64]{1,0:T(4,128)S(1)}, f32[3,64]{1,0:T(4,128)}, u32[]{:S(2)}) copy-start(f32[3,64]{1,0:T(4,128)} %get-tuple-element.150) | copy-start | bytes 2308
  945.1 404.3 %copy-start.23 = (f32[3,256,256]{1,2,0:T(8,128)S(1)}, f32[3,256,256]{1,2,0:T(8,128)}, u32[]{:S(2)}) copy-start(f32[3,256,256]{1,2,0:T(8,128)} %get-tuple-element.113) | copy-start | bytes 2359300
  945.1 404.6 %copy-start.98 = (f32[3,64]{1,0:T(4,128)S(1)}, f32[3,64]{1,0:T(4,128)}, u32[]{:S(2)}) copy-start(f32[3,64]{1,0:T(4,128)} %get-tuple-element.152) | copy-start | bytes 2308
  1350.3 441.5 %copy-start.52 = (f32[768]{0:T(1024)S(1)}, f32[768]{0:T(1024)}, u32[]{:S(2)}) copy-start(f32[768]{0:T(1024)} %copy-done.51) | copy-start | bytes 9220
  1350.3 441.5 %copy-start.59 = (f32[64,4]{0,1:T(4,128)S(1)}, f32[64,4]{0,1:T(4,128)}, u32[]{:S(2)}) copy-start(f32[64,4]{0,1:T(4,128)} %copy-done.58) | copy-start | bytes 3076
  1350.3 442.9 %copy-start.77 = (f32[64,4]{0,1:T(4,128)S(1)}, f32[64,4]{0,1:T(4,128)}, u32[]{:S(2)}) copy-start(f32[64,4]{0,1:T(4,128)} %copy-done.76) | copy-start | bytes 3076
  1350.3 442.9 %copy-start.66 = (f32[64,4]{0,1:T(4,128)S(1)}, f32[64,4]{0,1:T(4,128)}, u32[]{:S(2)}) copy-start(f32[64,4]{0,1:T(4,128)} %copy-done.65) | copy-start | bytes 3076
  1350.4 444.3 %copy-start.28 = (f32[64,4,768]{2,0,1:T(8,128)S(1)}, f32[64,4,768]{2,0,1:T(8,128)}, u32[]{:S(2)}) copy-start(f32[64,4,768]{2,0,1:T(8,128)} %get-tuple-element.122) | copy-start | bytes 2359300
  (86 other events, 212.7 us)
Sparse Core Ops, SparseCore 0:
  14.7 22.3 all-gather.8
  262.6 30.8 reduce-scatter.8
  298.5 19.6 all-gather.10
  326.5 28.1 reduce-scatter.10
  358.2 19.6 all-gather.12
  604.9 28.1 reduce-scatter.12
  637.8 19.6 all-gather.14
  659.1 19.6 all-gather.16
  689.2 28.1 reduce-scatter.16
  719.8 28.1 reduce-scatter.14
  753.0 19.6 all-gather.18
  786.3 28.1 reduce-scatter.18
  821.3 19.6 all-gather.20
  852.6 28.1 reduce-scatter.20
  887.7 19.6 all-gather.22
  920.2 28.1 reduce-scatter.22
  954.1 440.0 all-reduce.4
where the time goes:
time: 1860 us; the launch traced here: 1850 us
  other arithmetic  838 us (45%)
  local copies, waits for them, and re-layouts  541 us (29%)
  waiting for transfers between devices  296 us (16%)
  matrix products  85.4 us (5%)
  blocking collectives  76.1 us (4%)
    scatter-add x2, other arithmetic, layer_backward(): jax.ops.segment_sum(score_totals.reshape(head_count, -1).T, buckets.resha...  775 us
    gather x4, local copies, waits for them, and re-layouts, layer_forward(): rel_bias = rel_table[:, buckets]  471 us
    reduce_scatter x8, waiting for transfers between devices, scatter_product(): lax.psum_scatter(jnp.einsum(einsum_form, full_rows, matrix, preferred_ele...  189 us
    all_gather x8, waiting for transfers between devices, gather_product(): block_rows = lax.all_gather(local_rows, 'tensor', axis=0, tiled=True)  107 us
    psum x1, blocking collectives, shards(): summed_small = lax.psum(stacked_small + (mask_grad,), ('dp', 'tensor'))  38.2 us
    psum x1, blocking collectives, shards(): stacked_large = lax.psum(stacked_large, 'dp')  37.9 us
  transfers between devices with their start and end apart: 17, of which 13 were waited for; matrix products, arithmetic and copies ran while one was open for 72% of the time, Pallas kernels for 0%

commit v1 on v0

v1 whole, which is shorter than its diff:
```python
import functools

import jax
import jax.numpy as jnp
from jax import lax
from jax.experimental import pallas as pl
from jax.experimental.pallas import tpu as pltpu
from jax.sharding import PartitionSpec as P

HEAD_DIM = 64
BUCKETS = 732
LAYERS = 2
EPSILON = 1e-06
GROUPS = 1

BF = jnp.bfloat16
F32 = jnp.float32
CORE = [(i, i ^ 1) for i in range(4)]
CHIP = [(i, i ^ 2) for i in range(4)]
VMEM = pl.BlockSpec(memory_space=pltpu.VMEM)


def swap_core(values):
    return lax.ppermute(values, "tensor", CORE)


def swap_chip(values):
    return lax.ppermute(values, "tensor", CHIP)


def spread(own):
    far = swap_chip(own)
    near = swap_core(own)
    return [own, near, far, swap_core(far)]


def collect(partial):
    pair_far = partial[2] + swap_core(partial[3])
    arriving = swap_chip(pair_far)
    pair_own = partial[0].astype(F32) + swap_core(partial[1]).astype(F32)
    return pair_own + arriving.astype(F32)


def own_order(values, axis, member):
    low, high = member & 1, member >> 1

    def taken(source, order):
        return jnp.concatenate([lax.slice_in_dim(source, i, i + 1, axis=axis) for i in order], axis)

    values = jnp.where(low == 1, taken(values, (1, 0, 3, 2)), values)
    return jnp.where(high == 1, taken(values, (2, 3, 0, 1)), values)


def bias_kernel(table_ref, index_ref, out_ref):
    tables, chunks, lanes = table_ref.shape

    def rows_step(step, carry):
        rows = pl.ds(pl.multiple_of(step * 16, 16), 16)
        for half in range(2):
            columns = slice(half * 128, half * 128 + 128)
            index = index_ref[rows, columns]
            lane, chunk = index & 127, index >> 7
            here = [chunk == c for c in range(chunks)]
            for member in range(tables):
                total = jnp.zeros((16, 128), F32)
                for c in range(chunks):
                    line = jnp.broadcast_to(table_ref[member, c : c + 1, :], (16, 128))
                    total = jnp.where(here[c], jnp.take_along_axis(line, lane, axis=1), total)
                out_ref[member, rows, columns] = total.astype(out_ref.dtype)
        return carry

    lax.fori_loop(0, index_ref.shape[0] // 16, rows_step, 0)


def bias_of_buckets(tables, buckets):
    count, entries = tables.shape
    chunks = (entries + 127) // 128
    padded = jnp.pad(tables.astype(F32), ((0, 0), (0, chunks * 128 - entries)))
    return pl.pallas_call(
        bias_kernel,
        out_shape=jax.ShapeDtypeStruct((count,) + buckets.shape, BF),
        in_specs=[VMEM, VMEM],
        out_specs=VMEM,
        name="bias_of_buckets",
        cost_estimate=pl.CostEstimate(flops=10_000_000, bytes_accessed=1_500_000, transcendentals=0),
    )(padded.reshape(count, chunks, 128), buckets)


def bucket_kernel(values_ref, index_ref, out_ref):
    heads, size, width = values_ref.shape
    chunk = 8

    def step(i, total):
        start = pl.multiple_of(i * chunk, chunk)
        index = index_ref[pl.ds(start, chunk), :]
        left, right = [], []
        for r in range(chunk):
            row = index[r : r + 1, :]
            at_high = lax.broadcasted_iota(jnp.int32, (24, width), 0) == (row >> 5)
            at_low = lax.broadcasted_iota(jnp.int32, (32, width), 0) == (row & 31)
            right.append(jnp.where(at_low, 1.0, 0.0).astype(BF))
            left.append(
                jnp.concatenate(
                    [
                        jnp.where(at_high, values_ref[h, pl.ds(start + r, 1), :], 0.0).astype(BF)
                        for h in range(heads)
                    ],
                    0,
                )
            )
        return total + lax.dot_general(
            jnp.concatenate(left, 1),
            jnp.concatenate(right, 1),
            (((1,), (1,)), ((), ())),
            preferred_element_type=F32,
        )

    out_ref[...] = lax.fori_loop(0, size // chunk, step, jnp.zeros((heads * 24, 32), F32))


def sum_by_bucket(values, buckets):
    heads = values.shape[0]
    out = pl.pallas_call(
        bucket_kernel,
        out_shape=jax.ShapeDtypeStruct((heads * 24, 32), F32),
        in_specs=[VMEM, VMEM],
        out_specs=VMEM,
        name="sum_by_bucket",
        cost_estimate=pl.CostEstimate(flops=2_000_000_000, bytes_accessed=1_000_000, transcendentals=0),
    )(values, buckets)
    return out.reshape(heads, 768)


def norm_stats(values):
    mean = jnp.mean(values, axis=-1, keepdims=True)
    center = values - mean
    inverse = lax.rsqrt(jnp.mean(center * center, axis=-1, keepdims=True) + EPSILON)
    return center * inverse, inverse


def norm_rows(values, gain, shift):
    normal, unused = norm_stats(values)
    return (normal * gain + shift).astype(BF)


def norm_back(grad, values, gain):
    normal, inverse = norm_stats(values)
    scaled = grad * gain
    inner = scaled - jnp.mean(scaled, -1, keepdims=True) - normal * jnp.mean(scaled * normal, -1, keepdims=True)
    return inner * inverse, jnp.sum(grad * normal, axis=(0, 1)), jnp.sum(grad, axis=(0, 1))


def dot(form, left, right):
    return jnp.einsum(form, left, right, preferred_element_type=F32)


def joined(blocks):
    return jnp.concatenate(blocks, axis=1)


def parted(values):
    return jnp.split(values, 4, axis=1)


def gelu_tanh(values):
    return jax.nn.gelu(values, approximate=True)


def scores_of(queries, keys, rel_bias, key_bias):
    return dot("pqhe,pkhe->phqk", queries, keys) + rel_bias[None].astype(F32) + key_bias


def attention_in(own, w, key_bias):
    rows_all = joined(spread(own))
    pages, length, unused = rows_all.shape
    projected = dot("psd,tde->pste", rows_all, w["w_qkv"])
    shape = (pages, length, -1, HEAD_DIM)
    q = ((projected[:, :, 0] + w["qv_bias"][0]) * HEAD_DIM**-0.5).astype(BF).reshape(shape)
    k = projected[:, :, 1].astype(BF).reshape(shape)
    v = (projected[:, :, 2] + w["qv_bias"][1]).astype(BF).reshape(shape)
    scores = scores_of(q, k, w["rel_bias"], key_bias)
    row_max = jnp.max(scores, axis=-1, keepdims=True)
    log_total = row_max + jnp.log(jnp.sum(jnp.exp(scores - row_max), axis=-1, keepdims=True))
    weights = jnp.exp(scores - log_total).astype(BF)
    o = dot("phqk,pkhe->pqhe", weights, v).reshape(pages, length, -1).astype(BF)
    mixed = dot("pse,ed->psd", o, w["w_out"]).astype(BF)
    return mixed, (rows_all, q, k, v, log_total, o)


def attention_back(grad_all, kept, w, key_bias):
    rows_all, q, k, v, log_total, o = kept
    go = dot("psd,ed->pse", grad_all, w["w_out"]).astype(BF).reshape(q.shape)
    p = jnp.exp(scores_of(q, k, w["rel_bias"], key_bias) - log_total)
    gv = dot("phqk,pqhe->pkhe", p.astype(BF), go).astype(BF)
    gp = dot("pqhe,pkhe->phqk", go, v)
    gs = (p * (gp - jnp.sum(p * gp, axis=-1, keepdims=True))).astype(BF)
    totals = jnp.sum(gs.astype(F32), axis=0)
    gq = dot("phqk,pkhe->pqhe", gs, k).astype(BF) * HEAD_DIM**-0.5
    gk = dot("phqk,pqhe->pkhe", gs, q).astype(BF)
    flat = o.shape
    stacked = jnp.concatenate([gq.reshape(flat), gk.reshape(flat), gv.reshape(flat)], axis=-1)
    w_joined = jnp.concatenate([w["w_qkv"][i] for i in range(3)], axis=-1)
    ga = dot("pse,de->psd", stacked, w_joined).astype(BF)
    return ga, stacked, totals


def butterfly_reduce(values, bits, place):
    order = []
    for bit in bits:
        half = values.shape[0] // 2
        mine = (place >> bit) & 1
        first, second = values[:half], values[half:]
        keep = jnp.where(mine == 1, second, first)
        send = jnp.where(mine == 1, first, second)
        got = lax.ppermute(send, "dp", [(i, i ^ (1 << bit)) for i in range(1 << len(bits))])
        values = keep + got
    return values


def butterfly_gather(values, bits, place):
    for bit in reversed(bits):
        mine = (place >> bit) & 1
        got = lax.ppermute(values, "dp", [(i, i ^ (1 << bit)) for i in range(1 << len(bits))])
        values = jnp.concatenate(
            [jnp.where(mine == 1, got, values), jnp.where(mine == 1, values, got)], axis=0
        )
    return values


def sum_pages(values, bits, place):
    return butterfly_gather(butterfly_reduce(values, bits, place), bits, place)


def sum_small(values, axis, bits):
    for bit in bits:
        values = values + lax.ppermute(values, axis, [(i, i ^ (1 << bit)) for i in range(1 << len(bits))])
    return values


def shards(
    n_dp,
    patch_rows,
    cotangent,
    mask_flags,
    pad_flags,
    buckets,
    mask_emb,
    ln1_gain,
    ln1_bias,
    w_qkv,
    qv_bias,
    rel_table,
    w_out,
    out_bias,
    ln2_gain,
    ln2_bias,
    w_up,
    up_bias,
    w_down,
    down_bias,
):
    member = lax.axis_index("tensor")
    place = lax.axis_index("dp")
    bits = list(range(n_dp.bit_length() - 1))
    positions, pages, width = patch_rows.shape
    per_group = pages // GROUPS
    heads = rel_table.shape[1]

    length = buckets.shape[0]
    ordered = own_order(buckets.reshape(4, positions, 4, positions), 0, member)
    ordered = own_order(ordered, 2, member).reshape(length, length)
    pads = own_order(pad_flags.reshape(4, positions, pages), 0, member).reshape(length, pages)
    key_bias = jnp.where(pads == 1, -1000000000.0, 0.0).astype(F32).T[:, None, None, :]
    rel_bias = bias_of_buckets(rel_table.reshape(LAYERS * heads, BUCKETS), ordered)
    rel_bias = rel_bias.reshape(LAYERS, heads, length, length)

    def by_page(values):
        return jnp.swapaxes(values, 0, 1)

    masked = by_page(mask_flags == 1)[..., None]
    rows = by_page(patch_rows).astype(F32)
    hidden_all = jnp.where(masked, mask_emb.astype(F32), rows)
    cotangent = by_page(cotangent)

    def weights_of(layer):
        return {
            "ln1_gain": ln1_gain[layer].astype(F32),
            "ln1_bias": ln1_bias[layer].astype(F32),
            "w_qkv": w_qkv[layer],
            "qv_bias": qv_bias[layer].astype(F32),
            "rel_bias": rel_bias[layer],
            "w_out": w_out[layer],
            "out_bias": out_bias[layer].astype(F32),
            "ln2_gain": ln2_gain[layer].astype(F32),
            "ln2_bias": ln2_bias[layer].astype(F32),
            "w_up": w_up[layer],
            "up_bias": up_bias[layer].astype(F32),
            "w_down": w_down[layer],
            "down_bias": down_bias[layer].astype(F32),
        }

    groups = range(GROUPS)

    def part(values, g):
        return values[g * per_group : (g + 1) * per_group]

    weights = [weights_of(layer) for layer in range(LAYERS)]
    hidden = [part(hidden_all, g) for g in groups]
    pads_of = [part(key_bias, g) for g in groups]
    last_grad = [joined(spread(part(cotangent, g))) for g in groups]
    kept = []
    for layer in range(LAYERS):
        w = weights[layer]
        saved = []
        for g in groups:
            own = norm_rows(hidden[g], w["ln1_gain"], w["ln1_bias"])
            mixed, kept_attention = attention_in(own, w, pads_of[g])
            middle = hidden[g] + collect(parted(mixed)) + w["out_bias"]
            own = norm_rows(middle, w["ln2_gain"], w["ln2_bias"])
            rows_two = joined(spread(own))
            u = dot("psd,df->psf", rows_two, w["w_up"]) + w["up_bias"]
            z = gelu_tanh(u).astype(BF)
            down = dot("psf,fd->psd", z, w["w_down"]).astype(BF)
            saved.append((hidden[g], kept_attention, middle, rows_two, u, z))
            hidden[g] = middle + collect(parted(down)) + w["down_bias"]
        kept.append(saved)
    result = jnp.concatenate([h.astype(BF) for h in hidden], axis=0)

    grads = [part(cotangent, g).astype(F32) for g in groups]
    large = [None] * LAYERS
    slim = [None] * LAYERS
    small = [None] * LAYERS
    for layer in reversed(range(LAYERS)):
        w = weights[layer]
        d_down_bias = sum(jnp.sum(grads[g], axis=(0, 1)) for g in groups)
        stage = []
        d_up_bias = 0.0
        for g in groups:
            before, kept_attention, middle, rows_two, u, z = kept[layer][g]
            gm = last_grad[g] if layer == LAYERS - 1 else joined(spread(grads[g].astype(BF)))
            gz = dot("psd,fd->psf", gm, w["w_down"])
            unused, pull = jax.vjp(gelu_tanh, u)
            gu = pull(gz)[0].astype(BF)
            d_up_bias = d_up_bias + jnp.sum(gu.astype(F32), axis=(0, 1))
            gc = dot("psf,df->psd", gu, w["w_up"]).astype(BF)
            stage.append((gm, gu, collect(parted(gc))))
        d_w_down = sum(dot("psf,psd->fd", kept[layer][g][5], stage[g][0]) for g in groups)
        d_w_up = sum(dot("psd,psf->df", kept[layer][g][3], stage[g][1]) for g in groups)
        d_ln2_gain = d_ln2_bias = d_out_bias = 0.0
        second = []
        for g in groups:
            before, kept_attention, middle, rows_two, u, z = kept[layer][g]
            inner, d_gain, d_shift = norm_back(stage[g][2], middle, w["ln2_gain"])
            g1 = grads[g] + inner
            d_ln2_gain, d_ln2_bias = d_ln2_gain + d_gain, d_ln2_bias + d_shift
            d_out_bias = d_out_bias + jnp.sum(g1, axis=(0, 1))
            gr = joined(spread(g1.astype(BF)))
            ga, stacked, totals = attention_back(gr, kept_attention, w, pads_of[g])
            second.append((g1, gr, stacked, totals, collect(parted(ga))))
        mlp_sum = sum_pages(jnp.concatenate([d_w_down, d_w_up], axis=0).astype(BF), bits, place)
        d_w_out = sum(dot("pse,psd->ed", kept[layer][g][1][5], second[g][1]) for g in groups)
        d_w_qkv = sum(dot("pse,psd->ed", second[g][2], kept[layer][g][1][0]) for g in groups)
        attention_sum = sum_pages(jnp.concatenate([d_w_out, d_w_qkv], axis=0).astype(BF), bits, place)
        d_rel = sum_by_bucket(sum(second[g][3] for g in groups), ordered)[:, :BUCKETS]
        flat_sum = sum(jnp.sum(second[g][2].astype(F32), axis=(0, 1)) for g in groups)
        d_ln1_gain = d_ln1_bias = 0.0
        for g in groups:
            inner, d_gain, d_shift = norm_back(second[g][4], kept[layer][g][0], w["ln1_gain"])
            grads[g] = second[g][0] + inner
            d_ln1_gain, d_ln1_bias = d_ln1_gain + d_gain, d_ln1_bias + d_shift
        large[layer] = (mlp_sum, attention_sum)
        slim[layer] = jnp.concatenate([d_rel.reshape(-1), flat_sum, d_up_bias])
        small[layer] = [d_ln1_gain, d_ln1_bias, d_out_bias, d_ln2_gain, d_ln2_bias, d_down_bias]

    grad_hidden = jnp.concatenate(grads, axis=0)
    mask_grad = jnp.sum(jnp.where(masked, grad_hidden, 0.0), axis=(0, 1))
    grad_input = jnp.where(masked, 0.0, grad_hidden)
    lanes = jnp.concatenate([v for layer in range(LAYERS) for v in small[layer]] + [mask_grad])
    lanes = sum_small(lanes, "tensor", [0, 1])
    slim_size = slim[0].shape[0]
    whole = sum_small(jnp.concatenate(slim + [lanes]), "dp", bits)
    slim_sum = [whole[i * slim_size : (i + 1) * slim_size] for i in range(LAYERS)]
    small_sum = whole[LAYERS * slim_size :].reshape(-1, width)
    local = heads * HEAD_DIM
    rel_size = heads * BUCKETS

    def stacked_small(i):
        return jnp.stack([small_sum[layer * 6 + i] for layer in range(LAYERS)])

    return (
        by_page(result),
        by_page(grad_input),
        small_sum[-1],
        stacked_small(0),
        stacked_small(1),
        jnp.stack(
            [
                jnp.swapaxes(large[i][1][local:].astype(F32).reshape(3, local, width), 1, 2)
                for i in range(LAYERS)
            ]
        ),
        jnp.stack(
            [
                slim_sum[i][rel_size : rel_size + 3 * local].reshape(3, local)[::2]
                for i in range(LAYERS)
            ]
        ),
        jnp.stack([slim_sum[i][:rel_size].reshape(heads, BUCKETS) for i in range(LAYERS)]),
        jnp.stack([large[i][1][:local].astype(F32) for i in range(LAYERS)]),
        stacked_small(2),
        stacked_small(3),
        stacked_small(4),
        jnp.stack([large[i][0][width:].astype(F32) for i in range(LAYERS)]),
        jnp.stack([slim_sum[i][rel_size + 3 * local :] for i in range(LAYERS)]),
        jnp.stack([large[i][0][:width].astype(F32) for i in range(LAYERS)]),
        stacked_small(5),
    )


def solution(mesh):
    placed = (
        P("tensor", "dp", None),
        P("tensor", "dp", None),
        P("tensor", "dp"),
        P(None, "dp"),
        P(),
        P(),
        P(),
        P(),
        P(None, None, None, "tensor"),
        P(None, None, "tensor"),
        P(None, "tensor", None),
        P(None, "tensor", None),
        P(),
        P(),
        P(),
        P(None, None, "tensor"),
        P(None, "tensor"),
        P(None, "tensor", None),
        P(),
    )
    return jax.shard_map(
        functools.partial(shards, mesh.shape["dp"]),
        mesh=mesh,
        in_specs=placed,
        out_specs=(
            P("tensor", "dp", None),
            P("tensor", "dp", None),
            P(),
            P(),
            P(),
            P(None, None, None, "tensor"),
            P(None, None, "tensor"),
            P(None, "tensor", None),
            P(None, "tensor", None),
            P(),
            P(),
            P(),
            P(None, None, "tensor"),
            P(None, "tensor"),
            P(None, "tensor", None),
            P(),
        ),
        check_vma=False,
    )
```

time: 1860 us -> 508 us (0.27)
  other arithmetic: 838 us -> 77.9 us
  local copies, waits for them, and re-layouts: 541 us -> 45.1 us
  blocking collectives: 76.1 us -> 0 us
  waiting for transfers between devices: 296 us -> 229 us
  starting transfers between devices: 1.71 us -> 56 us
  Pallas kernels: 0 us -> 25 us
  matrix products: 85.4 us -> 65.7 us
    scatter-add x2 -> x0, other arithmetic: 775 us -> none  [layer_backward(): jax.ops.segment_sum(score_totals.reshape(head_count, -1).T, buckets.resha...]
    gather x4 -> x0, local copies, waits for them, and re-layouts: 471 us -> none  [layer_forward(): rel_bias = rel_table[:, buckets]]
    ppermute x0 -> x77, waiting for transfers between devices: none -> 229 us  [the longest x16 104 us: swap_chip(): return lax.ppermute(values, 'tensor', CHIP)]
    reduce_scatter x8 -> x0, waiting for transfers between devices: 189 us -> none  [scatter_product(): lax.psum_scatter(jnp.einsum(einsum_form, full_rows, matrix, preferred_ele...]
    all_gather x8 -> x0, waiting for transfers between devices: 107 us -> none  [gather_product(): block_rows = lax.all_gather(local_rows, 'tensor', axis=0, tiled=True)]
    psum x2 -> x0, blocking collectives: 76.1 us -> none  [the longest x1 38.2 us: shards(): summed_small = lax.psum(stacked_small + (mask_grad,), ('dp', 'tensor'))]
    ppermute x0 -> x77, starting transfers between devices: none -> 56 us  [the longest x12 18.1 us: butterfly_reduce(): lax.ppermute(send, 'dp', [(i, i ^ 1 << bit) for i in range(1 << len(bits))])]
    transpose x2 -> x0, local copies, waits for them, and re-layouts: 32.3 us -> none  [layer_backward(): score_totals.reshape(head_count, -1)]
  transfers between devices with their start and end apart: 17 -> 77, of which waited for: 13 -> 31; matrix products, arithmetic and copies ran while one was open for 72% -> 29% of each run, Pallas kernels for 0% -> 5%
where the time goes in v1:
time: 508 us; the launch traced here: 502 us
  waiting for transfers between devices  229 us (45%)
  other arithmetic  77.9 us (15%)
  matrix products  65.7 us (13%)
  starting transfers between devices  56 us (11%)
  local copies, waits for them, and re-layouts  45.1 us (9%)
  Pallas kernels  25 us (5%)
    ppermute x16, waiting for transfers between devices, swap_chip(): return lax.ppermute(values, 'tensor', CHIP)  104 us
    ppermute x12, waiting for transfers between devices, butterfly_gather(): lax.ppermute(values, 'dp', [(i, i ^ 1 << bit) for i in range(1 << len(bit...  81.5 us
    dot_general x36, matrix products, dot(): return jnp.einsum(form, left, right, preferred_element_type=F32)  65.7 us
    ppermute x12, waiting for transfers between devices, butterfly_reduce(): lax.ppermute(send, 'dp', [(i, i ^ 1 << bit) for i in range(1 << len(bits))])  26.4 us
    pallas_call x2, Pallas kernels, sum_by_bucket(): pl.pallas_call(bucket_kernel, out_shape=jax.ShapeDtypeStruct((heads * 24,...  19.4 us
    ppermute x12, starting transfers between devices, butterfly_reduce(): lax.ppermute(send, 'dp', [(i, i ^ 1 << bit) for i in range(1 << len(bits))])  18.1 us
    unnamed x352, local copies, waits for them, and re-layouts  16.3 us
    ppermute x12, starting transfers between devices, butterfly_gather(): lax.ppermute(values, 'dp', [(i, i ^ 1 << bit) for i in range(1 << len(bit...  16.3 us
  transfers between devices with their start and end apart: 77, of which 31 were waited for; matrix products, arithmetic and copies ran while one was open for 29% of the time, Pallas kernels for 5%

profile of v1, /device:TPU:0, one launch (start us, length us, event | category | flops | bytes accessed | tf_op | source)
XLA Modules:
  0.0 501.9 jit_solution(1419697014123502991)
XLA Ops:
  6.0 2.0 fusion.66
  8.0 3.0 collective-permute-start.1
  21.3 5.6 %bias_of_buckets.1 = bf16[6,256,256]{2,1,0:T(8,128)(2,1)} custom-call(f32[6,6,128]{2,1,0:T(8,128)} %reshape.411.table_ref, s32[256,256]{1,0:T(8,128)} %select_select_fusion.index_ref), custom_call_target="tpu_custom_call" | custom-call | flops 10000000 | bytes 1500000 | tf_op jit(solution)/shard_map/bias_of_buckets/pallas_call | solution.py:79
  27.4 2.1 slice_convert_fusion.2
  30.7 2.5 fusion.20
  42.0 9.3 %collective-permute-done.5 = bf16[4,64,768]{2,1,0:T(8,128)(2,1)S(1)} collective-permute-done((bf16[4,64,768]{2,1,0:T(8,128)(2,1)S(1)}, bf16[4,64,768]{2,1,0:T(8,128)(2,1)S(1)}, u32[]{:S(2)}, u32[]{:S(2)}) %collective-permute-start.5) | collective-permute-done | bytes 393248 | tf_op jit(solution)/shard_map/ppermute | solution.py:28
  52.5 10.0 %collective-permute-done.7 = bf16[4,64,768]{2,1,0:T(8,128)(2,1)S(1)} collective-permute-done((bf16[4,64,768]{2,1,0:T(8,128)(2,1)S(1)}, bf16[4,64,768]{2,1,0:T(8,128)(2,1)S(1)}, u32[]{:S(2)}, u32[]{:S(2)}) %collective-permute-start.7) | collective-permute-done | bytes 393248 | tf_op jit(solution)/shard_map/ppermute | solution.py:28
  65.8 2.1 convolution_convert_fusion.6
  71.1 9.9 %collective-permute-done.11 = bf16[4,64,768]{2,1,0:T(8,128)(2,1)S(1)} collective-permute-done((bf16[4,64,768]{2,1,0:T(8,128)(2,1)S(1)}, bf16[4,64,768]{2,1,0:T(8,128)(2,1)S(1)}, u32[]{:S(2)}, u32[]{:S(2)}) %collective-permute-start.11) | collective-permute-done | bytes 393248 | tf_op jit(solution)/shard_map/ppermute | solution.py:28
  83.7 10.0 %collective-permute-done.13 = bf16[4,64,768]{2,1,0:T(8,128)(2,1)} collective-permute-done((bf16[4,64,768]{2,1,0:T(8,128)(2,1)}, bf16[4,64,768]{2,1,0:T(8,128)(2,1)}, u32[]{:S(2)}, u32[]{:S(2)}) %collective-permute-start.13) | collective-permute-done | bytes 393248 | tf_op jit(solution)/shard_map/ppermute | solution.py:28
  96.5 2.3 copy.77
  98.8 2.8 fusion.18
  109.3 10.8 %collective-permute-done.17 = bf16[4,64,768]{2,1,0:T(8,128)(2,1)S(1)} collective-permute-done((bf16[4,64,768]{2,1,0:T(8,128)(2,1)S(1)}, bf16[4,64,768]{2,1,0:T(8,128)(2,1)S(1)}, u32[]{:S(2)}, u32[]{:S(2)}) %collective-permute-start.17) | collective-permute-done | bytes 393248 | tf_op jit(solution)/shard_map/ppermute | solution.py:28
  125.1 9.5 %collective-permute-done.19 = bf16[4,64,768]{2,1,0:T(8,128)(2,1)} collective-permute-done((bf16[4,64,768]{2,1,0:T(8,128)(2,1)}, bf16[4,64,768]{2,1,0:T(8,128)(2,1)}, u32[]{:S(2)}, u32[]{:S(2)}) %collective-permute-start.19) | collective-permute-done | bytes 393248 | tf_op jit(solution)/shard_map/ppermute | solution.py:28
  135.2 6.4 %collective-permute-done.25 = bf16[4,64,768]{2,1,0:T(8,128)(2,1)} collective-permute-done((bf16[4,64,768]{2,1,0:T(8,128)(2,1)}, bf16[4,64,768]{2,1,0:T(8,128)(2,1)}, u32[]{:S(2)}, u32[]{:S(2)}) %collective-permute-start.25) | collective-permute-done | bytes 393248 | tf_op jit(solution)/shard_map/ppermute | solution.py:28
  141.6 3.2 fusion.29
  144.8 2.1 convolution_convert_fusion.4
  147.6 5.0 convert_reduce_fusion
  154.7 2.8 bitcast_convert_fusion.1
  158.5 4.6 broadcast_select_fusion
  166.2 3.6 collective-permute-done.29
  170.8 7.0 %collective-permute-done.23 = bf16[4,64,768]{2,1,0:T(8,128)(2,1)S(1)} collective-permute-done((bf16[4,64,768]{2,1,0:T(8,128)(2,1)S(1)}, bf16[4,64,768]{2,1,0:T(8,128)(2,1)S(1)}, u32[]{:S(2)}, u32[]{:S(2)}) %collective-permute-start.23) | collective-permute-done | bytes 393248 | tf_op jit(solution)/shard_map/ppermute | solution.py:28
  177.8 2.0 fusion.116
  182.1 2.8 slice_bitcast_fusion.4
  186.0 6.6 %collective-permute-done.31 = bf16[4,64,768]{2,1,0:T(8,128)(2,1)} collective-permute-done((bf16[4,64,768]{2,1,0:T(8,128)(2,1)}, bf16[4,64,768]{2,1,0:T(8,128)(2,1)}, u32[]{:S(2)}, u32[]{:S(2)}) %collective-permute-start.31) | collective-permute-done | bytes 393248 | tf_op jit(solution)/shard_map/ppermute | solution.py:28
  196.8 1.8 convolution_convert_fusion.15
  201.1 1.9 convert_reduce_fusion.1
  204.4 1.7 fusion.23
  206.1 2.5 bitcast_convert_fusion.4
  210.6 2.3 copy.87.values_ref
  214.4 2.9 convolution_convert_fusion.1
  222.2 2.6 collective-permute-start.73
  224.8 9.7 %sum_by_bucket.3 = f32[72,32]{1,0:T(8,128)} custom-call(f32[3,256,256]{2,1,0:T(8,128)} %copy.87.values_ref, s32[256,256]{1,0:T(8,128)} %select_select_fusion.index_ref), custom_call_target="tpu_custom_call" | custom-call | flops 2000000000 | bytes 1000000 | tf_op jit(solution)/shard_map/sum_by_bucket/pallas_call | solution.py:123
  236.4 2.2 collective-permute-done.73
  241.3 3.4 collective-permute-start.60
  244.6 10.9 %collective-permute-done.74 = bf16[192,768]{1,0:T(8,128)(2,1)S(1)} collective-permute-done((bf16[192,768]{1,0:T(8,128)(2,1)S(1)}, bf16[192,768]{1,0:T(8,128)(2,1)S(1)}, u32[]{:S(2)}, u32[]{:S(2)}) %collective-permute-start.74) | collective-permute-done | bytes 294944 | tf_op jit(solution)/shard_map/ppermute | solution.py:223
  257.0 1.8 pad_maximum_fusion.19
  260.0 2.2 collective-permute-start.61
  262.2 13.0 %collective-permute-done.61 = bf16[96,768]{1,0:T(8,128)(2,1)S(1)} collective-permute-done((bf16[96,768]{1,0:T(8,128)(2,1)S(1)}, bf16[96,768]{1,0:T(8,128)(2,1)S(1)}, u32[]{:S(2)}, u32[]{:S(2)}) %collective-permute-start.61) | collective-permute-done | bytes 147488 | tf_op jit(solution)/shard_map/ppermute | solution.py:215
  275.9 3.4 collective-permute-start.62
  287.3 5.1 %collective-permute-done.37 = bf16[4,64,768]{2,1,0:T(8,128)(2,1)} collective-permute-done((bf16[4,64,768]{2,1,0:T(8,128)(2,1)}, bf16[4,64,768]{2,1,0:T(8,128)(2,1)}, u32[]{:S(2)}, u32[]{:S(2)}) %collective-permute-start.37) | collective-permute-done | bytes 393248 | tf_op jit(solution)/shard_map/ppermute | solution.py:28
  296.9 4.8 convert_reduce_fusion.2
  304.8 3.1 broadcast_select_fusion.1
  311.2 24.3 %collective-permute-done.64 = bf16[384,768]{1,0:T(8,128)(2,1)S(1)} collective-permute-done((bf16[384,768]{1,0:T(8,128)(2,1)S(1)}, bf16[384,768]{1,0:T(8,128)(2,1)S(1)}, u32[]{:S(2)}, u32[]{:S(2)}) %collective-permute-start.64) | collective-permute-done | bytes 589856 | tf_op jit(solution)/shard_map/ppermute | solution.py:223
  340.4 1.8 select_bitcast_fusion
  342.2 7.0 %collective-permute-done.43 = bf16[4,64,768]{2,1,0:T(8,128)(2,1)S(1)} collective-permute-done((bf16[4,64,768]{2,1,0:T(8,128)(2,1)S(1)}, bf16[4,64,768]{2,1,0:T(8,128)(2,1)S(1)}, u32[]{:S(2)}, u32[]{:S(2)}) %collective-permute-start.43) | collective-permute-done | bytes 393248 | tf_op jit(solution)/shard_map/ppermute | solution.py:28
  349.2 11.2 %collective-permute-done.65 = bf16[768,768]{1,0:T(8,128)(2,1)S(1)} collective-permute-done((bf16[768,768]{1,0:T(8,128)(2,1)S(1)}, bf16[768,768]{1,0:T(8,128)(2,1)S(1)}, u32[]{:S(2)}, u32[]{:S(2)}) %collective-permute-start.65) | collective-permute-done | bytes 1179680 | tf_op jit(solution)/shard_map/ppermute | solution.py:215
  363.2 1.7 convolution_convert_fusion.8
  366.2 1.9 convert_reduce_fusion.3
  370.7 1.9 fusion.22
  372.6 2.3 bitcast_convert_fusion.5
  379.5 9.6 %sum_by_bucket.2 = f32[72,32]{1,0:T(8,128)} custom-call(f32[3,256,256]{2,1,0:T(8,128)} %copy.86.values_ref, s32[256,256]{1,0:T(8,128)} %select_select_fusion.index_ref), custom_call_target="tpu_custom_call" | custom-call | flops 2000000000 | bytes 1000000 | tf_op jit(solution)/shard_map/sum_by_bucket/pallas_call | solution.py:123
  396.3 8.7 %collective-permute-done.47 = bf16[4,64,768]{2,1,0:T(8,128)(2,1)S(1)} collective-permute-done((bf16[4,64,768]{2,1,0:T(8,128)(2,1)S(1)}, bf16[4,64,768]{2,1,0:T(8,128)(2,1)S(1)}, u32[]{:S(2)}, u32[]{:S(2)}) %collective-permute-start.47) | collective-permute-done | bytes 393248 | tf_op jit(solution)/shard_map/ppermute | solution.py:28
  416.8 12.8 %collective-permute-done.68 = bf16[192,768]{1,0:T(8,128)(2,1)S(1)} collective-permute-done((bf16[192,768]{1,0:T(8,128)(2,1)S(1)}, bf16[192,768]{1,0:T(8,128)(2,1)S(1)}, u32[]{:S(2)}, u32[]{:S(2)}) %collective-permute-start.68) | collective-permute-done | bytes 294944 | tf_op jit(solution)/shard_map/ppermute | solution.py:223
  429.8 2.1 collective-permute-start.69
  435.4 2.5 collective-permute-start.56
  437.9 9.2 %collective-permute-done.52 = f32[17064]{0:T(1024)S(1)} collective-permute-done((f32[17064]{0:T(1024)S(1)}, f32[17064]{0:T(1024)S(1)}, u32[]{:S(2)}, u32[]{:S(2)}) %collective-permute-start.52) | collective-permute-done | bytes 68288 | tf_op jit(solution)/shard_map/ppermute | solution.py:236
  451.0 3.5 collective-permute-start.57
  456.3 2.9 collective-permute-done.57
  464.1 11.6 %collective-permute-done.58 = bf16[384,768]{1,0:T(8,128)(2,1)S(1)} collective-permute-done((bf16[384,768]{1,0:T(8,128)(2,1)S(1)}, bf16[384,768]{1,0:T(8,128)(2,1)S(1)}, u32[]{:S(2)}, u32[]{:S(2)}) %collective-permute-start.58) | collective-permute-done | bytes 589856 | tf_op jit(solution)/shard_map/ppermute | solution.py:223
  477.2 2.0 maximum_convert_fusion.2
  479.2 17.0 %collective-permute-done.70 = bf16[768,768]{1,0:T(8,128)(2,1)S(1)} collective-permute-done((bf16[768,768]{1,0:T(8,128)(2,1)S(1)}, bf16[768,768]{1,0:T(8,128)(2,1)S(1)}, u32[]{:S(2)}, u32[]{:S(2)}) %collective-permute-start.70) | collective-permute-done | bytes 1179680 | tf_op jit(solution)/shard_map/ppermute | solution.py:223
  496.7 2.5 maximum_convert_fusion.1
  499.2 2.5 maximum_convert_fusion
  (691 shorter events, 155.9 us)
Async XLA Ops:
  8.0 18.9 %collective-permute-start.1 = (bf16[4,64,768]{2,1,0:T(8,128)(2,1)}, bf16[4,64,768]{2,1,0:T(8,128)(2,1)}, u32[]{:S(2)}, u32[]{:S(2)}) collective-permute-start(bf16[4,64,768]{2,1,0:T(8,128)(2,1)} %fusion.66), channel_id=1, source_target_pairs={{0,2},{1,3},{2,0},{3,1},{4,6},{5,7},{6,4},{7,5},{8,10},{9,11},{10,... | collective-permute-start | bytes 1179656 | tf_op jit(solution)/shard_map/ppermute | solution.py:28
  11.0 19.7 %collective-permute-start = (bf16[4,64,768]{2,1,0:T(8,128)(2,1)}, bf16[4,64,768]{2,1,0:T(8,128)(2,1)}, u32[]{:S(2)}, u32[]{:S(2)}) collective-permute-start(bf16[4,64,768]{2,1,0:T(8,128)(2,1)} %fusion.66), channel_id=1, source_target_pairs={{0,1},{1,0},{2,3},{3,2},{4,5},{5,4},{6,7},{7,6},{8,9},{9,8},{10,11... | collective-permute-start | bytes 1179656 | tf_op jit(solution)/shard_map/ppermute | solution.py:24
  40.0 11.2 %collective-permute-start.5 = (bf16[4,64,768]{2,1,0:T(8,128)(2,1)S(1)}, bf16[4,64,768]{2,1,0:T(8,128)(2,1)S(1)}, u32[]{:S(2)}, u32[]{:S(2)}) collective-permute-start(bf16[4,64,768]{2,1,0:T(8,128)(2,1)S(1)} %slice_add_fusion.7), channel_id=1, source_target_pairs={{0,2},{1,3},{2,0},{3,1},{4,6},{5,7},{6,4},{7,5},{8,10},{9,11},{10,... | collective-permute-start | bytes 1179656 | tf_op jit(solution)/shard_map/ppermute | solution.py:28
  52.1 10.4 %collective-permute-start.7 = (bf16[4,64,768]{2,1,0:T(8,128)(2,1)S(1)}, bf16[4,64,768]{2,1,0:T(8,128)(2,1)S(1)}, u32[]{:S(2)}, u32[]{:S(2)}) collective-permute-start(bf16[4,64,768]{2,1,0:T(8,128)(2,1)S(1)} %add_convert_fusion.4), channel_id=1, source_target_pairs={{0,2},{1,3},{2,0},{3,1},{4,6},{5,7},{6,4},{7,5},{8,10},{9,11},{10,... | collective-permute-start | bytes 1179656 | tf_op jit(solution)/shard_map/ppermute | solution.py:28
  52.5 10.7 %collective-permute-start.6 = (bf16[4,64,768]{2,1,0:T(8,128)(2,1)S(1)}, bf16[4,64,768]{2,1,0:T(8,128)(2,1)S(1)}, u32[]{:S(2)}, u32[]{:S(2)}) collective-permute-start(bf16[4,64,768]{2,1,0:T(8,128)(2,1)S(1)} %add_convert_fusion.4), channel_id=1, source_target_pairs={{0,1},{1,0},{2,3},{3,2},{4,5},{5,4},{6,7},{7,6},{8,9},{9,8},{10,11... | collective-permute-start | bytes 1179656 | tf_op jit(solution)/shard_map/ppermute | solution.py:24
  69.8 11.2 %collective-permute-start.11 = (bf16[4,64,768]{2,1,0:T(8,128)(2,1)S(1)}, bf16[4,64,768]{2,1,0:T(8,128)(2,1)S(1)}, u32[]{:S(2)}, u32[]{:S(2)}) collective-permute-start(bf16[4,64,768]{2,1,0:T(8,128)(2,1)S(1)} %slice_add_fusion.6), channel_id=1, source_target_pairs={{0,2},{1,3},{2,0},{3,1},{4,6},{5,7},{6,4},{7,5},{8,10},{9,11},{10,... | collective-permute-start | bytes 1179656 | tf_op jit(solution)/shard_map/ppermute | solution.py:28
  83.1 10.6 %collective-permute-start.13 = (bf16[4,64,768]{2,1,0:T(8,128)(2,1)}, bf16[4,64,768]{2,1,0:T(8,128)(2,1)}, u32[]{:S(2)}, u32[]{:S(2)}) collective-permute-start(bf16[4,64,768]{2,1,0:T(8,128)(2,1)} %add_convert_fusion.3), channel_id=1, source_target_pairs={{0,2},{1,3},{2,0},{3,1},{4,6},{5,7},{6,4},{7,5},{8,10},{9,11},{10,... | collective-permute-start | bytes 1179656 | tf_op jit(solution)/shard_map/ppermute | solution.py:28
  83.7 15.0 %collective-permute-start.12 = (bf16[4,64,768]{2,1,0:T(8,128)(2,1)}, bf16[4,64,768]{2,1,0:T(8,128)(2,1)}, u32[]{:S(2)}, u32[]{:S(2)}) collective-permute-start(bf16[4,64,768]{2,1,0:T(8,128)(2,1)} %add_convert_fusion.3), channel_id=1, source_target_pairs={{0,1},{1,0},{2,3},{3,2},{4,5},{5,4},{6,7},{7,6},{8,9},{9,8},{10,11... | collective-permute-start | bytes 1179656 | tf_op jit(solution)/shard_map/ppermute | solution.py:24
  93.8 5.0 collective-permute-start.14
  108.7 11.5 %collective-permute-start.17 = (bf16[4,64,768]{2,1,0:T(8,128)(2,1)S(1)}, bf16[4,64,768]{2,1,0:T(8,128)(2,1)S(1)}, u32[]{:S(2)}, u32[]{:S(2)}) collective-permute-start(bf16[4,64,768]{2,1,0:T(8,128)(2,1)S(1)} %slice_add_fusion.5), channel_id=1, source_target_pairs={{0,2},{1,3},{2,0},{3,1},{4,6},{5,7},{6,4},{7,5},{8,10},{9,11},{10,... | collective-permute-start | bytes 1179656 | tf_op jit(solution)/shard_map/ppermute | solution.py:28
  122.3 12.4 %collective-permute-start.19 = (bf16[4,64,768]{2,1,0:T(8,128)(2,1)}, bf16[4,64,768]{2,1,0:T(8,128)(2,1)}, u32[]{:S(2)}, u32[]{:S(2)}) collective-permute-start(bf16[4,64,768]{2,1,0:T(8,128)(2,1)} %add_convert_fusion.1), channel_id=1, source_target_pairs={{0,2},{1,3},{2,0},{3,1},{4,6},{5,7},{6,4},{7,5},{8,10},{9,11},{10,... | collective-permute-start | bytes 1179656 | tf_op jit(solution)/shard_map/ppermute | solution.py:28
  123.7 17.9 %collective-permute-start.25 = (bf16[4,64,768]{2,1,0:T(8,128)(2,1)}, bf16[4,64,768]{2,1,0:T(8,128)(2,1)}, u32[]{:S(2)}, u32[]{:S(2)}) collective-permute-start(bf16[4,64,768]{2,1,0:T(8,128)(2,1)} %bitcast.240), channel_id=1, source_target_pairs={{0,2},{1,3},{2,0},{3,1},{4,6},{5,7},{6,4},{7,5},{8,10},{9,11},{10,... | collective-permute-start | bytes 1179656 | tf_op jit(solution)/shard_map/ppermute | solution.py:28
  125.1 16.5 %collective-permute-start.18 = (bf16[4,64,768]{2,1,0:T(8,128)(2,1)}, bf16[4,64,768]{2,1,0:T(8,128)(2,1)}, u32[]{:S(2)}, u32[]{:S(2)}) collective-permute-start(bf16[4,64,768]{2,1,0:T(8,128)(2,1)} %add_convert_fusion.1), channel_id=1, source_target_pairs={{0,1},{1,0},{2,3},{3,2},{4,5},{5,4},{6,7},{7,6},{8,9},{9,8},{10,11... | collective-permute-start | bytes 1179656 | tf_op jit(solution)/shard_map/ppermute | solution.py:24
  134.6 7.0 %collective-permute-start.20 = (bf16[4,64,768]{2,1,0:T(8,128)(2,1)}, bf16[4,64,768]{2,1,0:T(8,128)(2,1)}, u32[]{:S(2)}, u32[]{:S(2)}) collective-permute-start(bf16[4,64,768]{2,1,0:T(8,128)(2,1)} %collective-permute-done.19), channel_id=1, source_target_pairs={{0,1},{1,0},{2,3},{3,2},{4,5},{5,4},{6,7},{7,6},{8,9},{9,8},{10,11... | collective-permute-start | bytes 1179656 | tf_op jit(solution)/shard_map/ppermute | solution.py:24
  134.6 13.0 %collective-permute-start.24 = (bf16[4,64,768]{2,1,0:T(8,128)(2,1)}, bf16[4,64,768]{2,1,0:T(8,128)(2,1)}, u32[]{:S(2)}, u32[]{:S(2)}) collective-permute-start(bf16[4,64,768]{2,1,0:T(8,128)(2,1)} %bitcast.240), channel_id=1, source_target_pairs={{0,1},{1,0},{2,3},{3,2},{4,5},{5,4},{6,7},{7,6},{8,9},{9,8},{10,11... | collective-permute-start | bytes 1179656 | tf_op jit(solution)/shard_map/ppermute | solution.py:24
  141.6 6.0 %collective-permute-start.26 = (bf16[4,64,768]{2,1,0:T(8,128)(2,1)}, bf16[4,64,768]{2,1,0:T(8,128)(2,1)S(1)}, u32[]{:S(2)}, u32[]{:S(2)}) collective-permute-start(bf16[4,64,768]{2,1,0:T(8,128)(2,1)} %collective-permute-done.25), channel_id=1, source_target_pairs={{0,1},{1,0},{2,3},{3,2},{4,5},{5,4},{6,7},{7,6},{8,9},{9,8},{10,11... | collective-permute-start | bytes 1179656 | tf_op jit(solution)/shard_map/ppermute | solution.py:24
  146.9 23.9 %collective-permute-start.21 = (bf16[4,64,768]{2,1,0:T(8,128)(2,1)S(1)}, bf16[4,64,768]{2,1,0:T(8,128)(2,1)S(1)}, u32[]{:S(2)}, u32[]{:S(2)}) collective-permute-start(bf16[4,64,768]{2,1,0:T(8,128)(2,1)S(1)} %get-tuple-element.140), channel_id=1, source_target_pairs={{0,1},{1,0},{2,3},{3,2},{4,5},{5,4},{6,7},{7,6},{8,9},{9,8},{10,11... | collective-permute-start | bytes 1179656 | tf_op jit(solution)/shard_map/ppermute | solution.py:24
  147.5 17.0 %collective-permute-start.22 = (bf16[4,64,768]{2,1,0:T(8,128)(2,1)S(1)}, bf16[4,64,768]{2,1,0:T(8,128)(2,1)S(1)}, u32[]{:S(2)}, u32[]{:S(2)}) collective-permute-start(bf16[4,64,768]{2,1,0:T(8,128)(2,1)S(1)} %get-tuple-element.141), channel_id=1, source_target_pairs={{0,1},{1,0},{2,3},{3,2},{4,5},{5,4},{6,7},{7,6},{8,9},{9,8},{10,11... | collective-permute-start | bytes 1179656 | tf_op jit(solution)/shard_map/ppermute | solution.py:24
  154.1 12.1 %collective-permute-start.27 = (bf16[4,64,768]{2,1,0:T(8,128)(2,1)S(1)}, bf16[4,64,768]{2,1,0:T(8,128)(2,1)S(1)}, u32[]{:S(2)}, u32[]{:S(2)}) collective-permute-start(bf16[4,64,768]{2,1,0:T(8,128)(2,1)S(1)} %get-tuple-element.138), channel_id=1, source_target_pairs={{0,1},{1,0},{2,3},{3,2},{4,5},{5,4},{6,7},{7,6},{8,9},{9,8},{10,11... | collective-permute-start | bytes 1179656 | tf_op jit(solution)/shard_map/ppermute | solution.py:24
  157.6 12.2 %collective-permute-start.29 = (bf16[4,64,768]{2,1,0:T(8,128)(2,1)S(1)}, bf16[4,64,768]{2,1,0:T(8,128)(2,1)S(1)}, u32[]{:S(2)}, u32[]{:S(2)}) collective-permute-start(bf16[4,64,768]{2,1,0:T(8,128)(2,1)S(1)} %slice_add_fusion.3), channel_id=1, source_target_pairs={{0,2},{1,3},{2,0},{3,1},{4,6},{5,7},{6,4},{7,5},{8,10},{9,11},{10,... | collective-permute-start | bytes 1179656 | tf_op jit(solution)/shard_map/ppermute | solution.py:28
  163.1 29.5 %collective-permute-start.71 = (bf16[768,768]{1,0:T(8,128)(2,1)}, bf16[768,768]{1,0:T(8,128)(2,1)}, u32[]{:S(2)}, u32[]{:S(2)}) collective-permute-start(bf16[768,768]{1,0:T(8,128)(2,1)} %get-tuple-element.229), channel_id=1, source_target_pairs={{0,4},{4,0},{8,12},{12,8},{16,20},{20,16},{24,28},{28,24},{1,5},{5... | collective-permute-start | bytes 3538952 | tf_op jit(solution)/shard_map/ppermute | solution.py:215
  164.6 13.2 %collective-permute-start.23 = (bf16[4,64,768]{2,1,0:T(8,128)(2,1)S(1)}, bf16[4,64,768]{2,1,0:T(8,128)(2,1)S(1)}, u32[]{:S(2)}, u32[]{:S(2)}) collective-permute-start(bf16[4,64,768]{2,1,0:T(8,128)(2,1)S(1)} %slice_add_fusion.4), channel_id=1, source_target_pairs={{0,2},{1,3},{2,0},{3,1},{4,6},{5,7},{6,4},{7,5},{8,10},{9,11},{10,... | collective-permute-start | bytes 1179656 | tf_op jit(solution)/shard_map/ppermute | solution.py:28
  181.5 11.1 %collective-permute-start.31 = (bf16[4,64,768]{2,1,0:T(8,128)(2,1)}, bf16[4,64,768]{2,1,0:T(8,128)(2,1)}, u32[]{:S(2)}, u32[]{:S(2)}) collective-permute-start(bf16[4,64,768]{2,1,0:T(8,128)(2,1)} %convert_element_type.517), channel_id=1, source_target_pairs={{0,2},{1,3},{2,0},{3,1},{4,6},{5,7},{6,4},{7,5},{8,10},{9,11},{10,... | collective-permute-start | bytes 1179656 | tf_op jit(solution)/shard_map/ppermute | solution.py:28
  184.9 11.8 %collective-permute-start.30 = (bf16[4,64,768]{2,1,0:T(8,128)(2,1)}, bf16[4,64,768]{2,1,0:T(8,128)(2,1)S(1)}, u32[]{:S(2)}, u32[]{:S(2)}) collective-permute-start(bf16[4,64,768]{2,1,0:T(8,128)(2,1)} %convert_element_type.517), channel_id=1, source_target_pairs={{0,1},{1,0},{2,3},{3,2},{4,5},{5,4},{6,7},{7,6},{8,9},{9,8},{10,11... | collective-permute-start | bytes 1179656 | tf_op jit(solution)/shard_map/ppermute | solution.py:24
  195.2 23.1 %collective-permute-start.72 = (bf16[384,768]{1,0:T(8,128)(2,1)}, bf16[384,768]{1,0:T(8,128)(2,1)}, u32[]{:S(2)}, u32[]{:S(2)}) collective-permute-start(bf16[384,768]{1,0:T(8,128)(2,1)} %broadcast_select_fusion.4), channel_id=1, source_target_pairs={{0,8},{4,12},{8,0},{12,4},{16,24},{20,28},{24,16},{28,20},{1,9},{5... | collective-permute-start | bytes 1769480 | tf_op jit(solution)/shard_map/ppermute | solution.py:215
  212.9 26.9 %collective-permute-start.59 = (bf16[384,768]{1,0:T(8,128)(2,1)}, bf16[384,768]{1,0:T(8,128)(2,1)}, u32[]{:S(2)}, u32[]{:S(2)}) collective-permute-start(bf16[384,768]{1,0:T(8,128)(2,1)} %broadcast_select_fusion.10), channel_id=1, source_target_pairs={{0,4},{4,0},{8,12},{12,8},{16,20},{20,16},{24,28},{28,24},{1,5},{5... | collective-permute-start | bytes 1769480 | tf_op jit(solution)/shard_map/ppermute | solution.py:215
  218.3 16.2 %collective-permute-start.34 = (bf16[4,64,768]{2,1,0:T(8,128)(2,1)}, bf16[4,64,768]{2,1,0:T(8,128)(2,1)}, u32[]{:S(2)}, u32[]{:S(2)}) collective-permute-start(bf16[4,64,768]{2,1,0:T(8,128)(2,1)} %get-tuple-element.137), channel_id=1, source_target_pairs={{0,1},{1,0},{2,3},{3,2},{4,5},{5,4},{6,7},{7,6},{8,9},{9,8},{10,11... | collective-permute-start | bytes 1179656 | tf_op jit(solution)/shard_map/ppermute | solution.py:24
  222.2 16.4 %collective-permute-start.73 = (bf16[192,768]{1,0:T(8,128)(2,1)}, bf16[192,768]{1,0:T(8,128)(2,1)}, u32[]{:S(2)}, u32[]{:S(2)}) collective-permute-start(bf16[192,768]{1,0:T(8,128)(2,1)} %broadcast_select_fusion.16), channel_id=1, source_target_pairs={{0,16},{4,20},{8,24},{12,28},{16,0},{20,4},{24,8},{28,12},{1,17},{... | collective-permute-start | bytes 884744 | tf_op jit(solution)/shard_map/ppermute | solution.py:215
  234.5 24.3 %collective-permute-start.33 = (bf16[4,64,768]{2,1,0:T(8,128)(2,1)}, bf16[4,64,768]{2,1,0:T(8,128)(2,1)S(1)}, u32[]{:S(2)}, u32[]{:S(2)}) collective-permute-start(bf16[4,64,768]{2,1,0:T(8,128)(2,1)} %get-tuple-element.136), channel_id=1, source_target_pairs={{0,1},{1,0},{2,3},{3,2},{4,5},{5,4},{6,7},{7,6},{8,9},{9,8},{10,11... | collective-permute-start | bytes 1179656 | tf_op jit(solution)/shard_map/ppermute | solution.py:24
  235.8 23.0 %collective-permute-start.35 = (bf16[4,64,768]{2,1,0:T(8,128)(2,1)S(1)}, bf16[4,64,768]{2,1,0:T(8,128)(2,1)S(1)}, u32[]{:S(2)}, u32[]{:S(2)}) collective-permute-start(bf16[4,64,768]{2,1,0:T(8,128)(2,1)S(1)} %slice_add_fusion.2), channel_id=1, source_target_pairs={{0,2},{1,3},{2,0},{3,1},{4,6},{5,7},{6,4},{7,5},{8,10},{9,11},{10,... | collective-permute-start | bytes 1179656 | tf_op jit(solution)/shard_map/ppermute | solution.py:28
  239.8 15.7 %collective-permute-start.74 = (bf16[192,768]{1,0:T(8,128)(2,1)S(1)}, bf16[192,768]{1,0:T(8,128)(2,1)S(1)}, u32[]{:S(2)}, u32[]{:S(2)}) collective-permute-start(bf16[192,768]{1,0:T(8,128)(2,1)S(1)} %select_add_fusion.6), channel_id=1, source_target_pairs={{0,16},{4,20},{8,24},{12,28},{16,0},{20,4},{24,8},{28,12},{1,17},{... | collective-permute-start | bytes 884744 | tf_op jit(solution)/shard_map/ppermute | solution.py:223
  241.3 18.6 %collective-permute-start.60 = (bf16[192,768]{1,0:T(8,128)(2,1)S(1)}, bf16[192,768]{1,0:T(8,128)(2,1)S(1)}, u32[]{:S(2)}, u32[]{:S(2)}) collective-permute-start(bf16[192,768]{1,0:T(8,128)(2,1)S(1)} %broadcast_select_fusion.22), channel_id=1, source_target_pairs={{0,8},{4,12},{8,0},{12,4},{16,24},{20,28},{24,16},{28,20},{1,9},{5... | collective-permute-start | bytes 884744 | tf_op jit(solution)/shard_map/ppermute | solution.py:215
  258.8 33.6 %collective-permute-start.75 = (bf16[384,768]{1,0:T(8,128)(2,1)}, bf16[384,768]{1,0:T(8,128)(2,1)}, u32[]{:S(2)}, u32[]{:S(2)}) collective-permute-start(bf16[384,768]{1,0:T(8,128)(2,1)} %pad_maximum_fusion.19), channel_id=1, source_target_pairs={{0,8},{4,12},{8,0},{12,4},{16,24},{20,28},{24,16},{28,20},{1,9},{5... | collective-permute-start | bytes 1769480 | tf_op jit(solution)/shard_map/ppermute | solution.py:223
  260.0 15.2 %collective-permute-start.61 = (bf16[96,768]{1,0:T(8,128)(2,1)S(1)}, bf16[96,768]{1,0:T(8,128)(2,1)S(1)}, u32[]{:S(2)}, u32[]{:S(2)}) collective-permute-start(bf16[96,768]{1,0:T(8,128)(2,1)S(1)} %broadcast_select_fusion.31), channel_id=1, source_target_pairs={{0,16},{4,20},{8,24},{12,28},{16,0},{20,4},{24,8},{28,12},{1,17},{... | collective-permute-start | bytes 442376 | tf_op jit(solution)/shard_map/ppermute | solution.py:215
  275.9 10.3 %collective-permute-start.62 = (bf16[96,768]{1,0:T(8,128)(2,1)}, bf16[96,768]{1,0:T(8,128)(2,1)}, u32[]{:S(2)}, u32[]{:S(2)}) collective-permute-start(bf16[96,768]{1,0:T(8,128)(2,1)} %select_add_fusion.10), channel_id=1, source_target_pairs={{0,16},{4,20},{8,24},{12,28},{16,0},{20,4},{24,8},{28,12},{1,17},{... | collective-permute-start | bytes 442376 | tf_op jit(solution)/shard_map/ppermute | solution.py:223
  281.9 10.5 %collective-permute-start.37 = (bf16[4,64,768]{2,1,0:T(8,128)(2,1)}, bf16[4,64,768]{2,1,0:T(8,128)(2,1)}, u32[]{:S(2)}, u32[]{:S(2)}) collective-permute-start(bf16[4,64,768]{2,1,0:T(8,128)(2,1)} %convert_element_type.529), channel_id=1, source_target_pairs={{0,2},{1,3},{2,0},{3,1},{4,6},{5,7},{6,4},{7,5},{8,10},{9,11},{10,... | collective-permute-start | bytes 1179656 | tf_op jit(solution)/shard_map/ppermute | solution.py:28
  285.5 11.3 %collective-permute-start.36 = (bf16[4,64,768]{2,1,0:T(8,128)(2,1)}, bf16[4,64,768]{2,1,0:T(8,128)(2,1)S(1)}, u32[]{:S(2)}, u32[]{:S(2)}) collective-permute-start(bf16[4,64,768]{2,1,0:T(8,128)(2,1)} %convert_element_type.529), channel_id=1, source_target_pairs={{0,1},{1,0},{2,3},{3,2},{4,5},{5,4},{6,7},{7,6},{8,9},{9,8},{10,11... | collective-permute-start | bytes 1179656 | tf_op jit(solution)/shard_map/ppermute | solution.py:24
  287.2 8.8 %collective-permute-start.63 = (bf16[192,768]{1,0:T(8,128)(2,1)S(1)}, bf16[192,768]{1,0:T(8,128)(2,1)S(1)}, u32[]{:S(2)}, u32[]{:S(2)}) collective-permute-start(bf16[192,768]{1,0:T(8,128)(2,1)S(1)} %pad_maximum_fusion.21), channel_id=1, source_target_pairs={{0,8},{4,12},{8,0},{12,4},{16,24},{20,28},{24,16},{28,20},{1,9},{5... | collective-permute-start | bytes 884744 | tf_op jit(solution)/shard_map/ppermute | solution.py:223
  294.1 46.3 %collective-permute-start.76 = (bf16[768,768]{1,0:T(8,128)(2,1)S(1)}, bf16[768,768]{1,0:T(8,128)(2,1)S(1)}, u32[]{:S(2)}, u32[]{:S(2)}) collective-permute-start(bf16[768,768]{1,0:T(8,128)(2,1)S(1)} %pad_maximum_fusion.11), channel_id=1, source_target_pairs={{0,4},{4,0},{8,12},{12,8},{16,20},{20,16},{24,28},{28,24},{1,5},{5... | collective-permute-start | bytes 3538952 | tf_op jit(solution)/shard_map/ppermute | solution.py:223
  296.2 39.4 %collective-permute-start.64 = (bf16[384,768]{1,0:T(8,128)(2,1)S(1)}, bf16[384,768]{1,0:T(8,128)(2,1)S(1)}, u32[]{:S(2)}, u32[]{:S(2)}) collective-permute-start(bf16[384,768]{1,0:T(8,128)(2,1)S(1)} %pad_maximum_fusion.17), channel_id=1, source_target_pairs={{0,4},{4,0},{8,12},{12,8},{16,20},{20,16},{24,28},{28,24},{1,5},{5... | collective-permute-start | bytes 1769480 | tf_op jit(solution)/shard_map/ppermute | solution.py:223
  303.2 6.4 %collective-permute-start.40 = (bf16[4,64,768]{2,1,0:T(8,128)(2,1)S(1)}, bf16[4,64,768]{2,1,0:T(8,128)(2,1)S(1)}, u32[]{:S(2)}, u32[]{:S(2)}) collective-permute-start(bf16[4,64,768]{2,1,0:T(8,128)(2,1)S(1)} %get-tuple-element.135), channel_id=1, source_target_pairs={{0,1},{1,0},{2,3},{3,2},{4,5},{5,4},{6,7},{7,6},{8,9},{9,8},{10,11... | collective-permute-start | bytes 1179656 | tf_op jit(solution)/shard_map/ppermute | solution.py:24
  307.9 52.6 %collective-permute-start.65 = (bf16[768,768]{1,0:T(8,128)(2,1)S(1)}, bf16[768,768]{1,0:T(8,128)(2,1)S(1)}, u32[]{:S(2)}, u32[]{:S(2)}) collective-permute-start(bf16[768,768]{1,0:T(8,128)(2,1)S(1)} %get-tuple-element.231), channel_id=1, source_target_pairs={{0,4},{4,0},{8,12},{12,8},{16,20},{20,16},{24,28},{28,24},{1,5},{5... | collective-permute-start | bytes 3538952 | tf_op jit(solution)/shard_map/ppermute | solution.py:215
  309.4 27.1 %collective-permute-start.39 = (bf16[4,64,768]{2,1,0:T(8,128)(2,1)S(1)}, bf16[4,64,768]{2,1,0:T(8,128)(2,1)S(1)}, u32[]{:S(2)}, u32[]{:S(2)}) collective-permute-start(bf16[4,64,768]{2,1,0:T(8,128)(2,1)S(1)} %get-tuple-element.134), channel_id=1, source_target_pairs={{0,1},{1,0},{2,3},{3,2},{4,5},{5,4},{6,7},{7,6},{8,9},{9,8},{10,11... | collective-permute-start | bytes 1179656 | tf_op jit(solution)/shard_map/ppermute | solution.py:24
  309.7 26.9 %collective-permute-start.41 = (bf16[4,64,768]{2,1,0:T(8,128)(2,1)S(1)}, bf16[4,64,768]{2,1,0:T(8,128)(2,1)S(1)}, u32[]{:S(2)}, u32[]{:S(2)}) collective-permute-start(bf16[4,64,768]{2,1,0:T(8,128)(2,1)S(1)} %slice_add_fusion.1), channel_id=1, source_target_pairs={{0,2},{1,3},{2,0},{3,1},{4,6},{5,7},{6,4},{7,5},{8,10},{9,11},{10,... | collective-permute-start | bytes 1179656 | tf_op jit(solution)/shard_map/ppermute | solution.py:28
  338.9 10.4 %collective-permute-start.43 = (bf16[4,64,768]{2,1,0:T(8,128)(2,1)S(1)}, bf16[4,64,768]{2,1,0:T(8,128)(2,1)S(1)}, u32[]{:S(2)}, u32[]{:S(2)}) collective-permute-start(bf16[4,64,768]{2,1,0:T(8,128)(2,1)S(1)} %get-tuple-element.109), channel_id=1, source_target_pairs={{0,2},{1,3},{2,0},{3,1},{4,6},{5,7},{6,4},{7,5},{8,10},{9,11},{10,... | collective-permute-start | bytes 1179656 | tf_op jit(solution)/shard_map/ppermute | solution.py:28
  340.4 21.4 %collective-permute-start.42 = (bf16[4,64,768]{2,1,0:T(8,128)(2,1)S(1)}, bf16[4,64,768]{2,1,0:T(8,128)(2,1)S(1)}, u32[]{:S(2)}, u32[]{:S(2)}) collective-permute-start(bf16[4,64,768]{2,1,0:T(8,128)(2,1)S(1)} %get-tuple-element.109), channel_id=1, source_target_pairs={{0,1},{1,0},{2,3},{3,2},{4,5},{5,4},{6,7},{7,6},{8,9},{9,8},{10,11... | collective-permute-start | bytes 1179656 | tf_op jit(solution)/shard_map/ppermute | solution.py:24
  349.2 12.5 %collective-permute-start.44 = (bf16[4,64,768]{2,1,0:T(8,128)(2,1)S(1)}, bf16[4,64,768]{2,1,0:T(8,128)(2,1)S(1)}, u32[]{:S(2)}, u32[]{:S(2)}) collective-permute-start(bf16[4,64,768]{2,1,0:T(8,128)(2,1)S(1)} %collective-permute-done.43), channel_id=1, source_target_pairs={{0,1},{1,0},{2,3},{3,2},{4,5},{5,4},{6,7},{7,6},{8,9},{9,8},{10,11... | collective-permute-start | bytes 1179656 | tf_op jit(solution)/shard_map/ppermute | solution.py:24
  361.8 27.4 %collective-permute-start.66 = (bf16[384,768]{1,0:T(8,128)(2,1)}, bf16[384,768]{1,0:T(8,128)(2,1)}, u32[]{:S(2)}, u32[]{:S(2)}) collective-permute-start(bf16[384,768]{1,0:T(8,128)(2,1)} %broadcast_select_fusion.7), channel_id=1, source_target_pairs={{0,8},{4,12},{8,0},{12,4},{16,24},{20,28},{24,16},{28,20},{1,9},{5... | collective-permute-start | bytes 1769480 | tf_op jit(solution)/shard_map/ppermute | solution.py:215
  376.0 18.5 %collective-permute-start.53 = (bf16[384,768]{1,0:T(8,128)(2,1)}, bf16[384,768]{1,0:T(8,128)(2,1)}, u32[]{:S(2)}, u32[]{:S(2)}) collective-permute-start(bf16[384,768]{1,0:T(8,128)(2,1)} %broadcast_select_fusion.13), channel_id=1, source_target_pairs={{0,4},{4,0},{8,12},{12,8},{16,20},{20,16},{24,28},{28,24},{1,5},{5... | collective-permute-start | bytes 1769480 | tf_op jit(solution)/shard_map/ppermute | solution.py:215
  379.0 17.3 %collective-permute-start.45 = (bf16[4,64,768]{2,1,0:T(8,128)(2,1)}, bf16[4,64,768]{2,1,0:T(8,128)(2,1)}, u32[]{:S(2)}, u32[]{:S(2)}) collective-permute-start(bf16[4,64,768]{2,1,0:T(8,128)(2,1)} %get-tuple-element.132), channel_id=1, source_target_pairs={{0,1},{1,0},{2,3},{3,2},{4,5},{5,4},{6,7},{7,6},{8,9},{9,8},{10,11... | collective-permute-start | bytes 1179656 | tf_op jit(solution)/shard_map/ppermute | solution.py:24
  379.4 13.4 %collective-permute-start.46 = (bf16[4,64,768]{2,1,0:T(8,128)(2,1)}, bf16[4,64,768]{2,1,0:T(8,128)(2,1)}, u32[]{:S(2)}, u32[]{:S(2)}) collective-permute-start(bf16[4,64,768]{2,1,0:T(8,128)(2,1)} %get-tuple-element.133), channel_id=1, source_target_pairs={{0,1},{1,0},{2,3},{3,2},{4,5},{5,4},{6,7},{7,6},{8,9},{9,8},{10,11... | collective-permute-start | bytes 1179656 | tf_op jit(solution)/shard_map/ppermute | solution.py:24
  391.2 18.1 %collective-permute-start.67 = (bf16[192,768]{1,0:T(8,128)(2,1)}, bf16[192,768]{1,0:T(8,128)(2,1)}, u32[]{:S(2)}, u32[]{:S(2)}) collective-permute-start(bf16[192,768]{1,0:T(8,128)(2,1)} %broadcast_select_fusion.19), channel_id=1, source_target_pairs={{0,16},{4,20},{8,24},{12,28},{16,0},{20,4},{24,8},{28,12},{1,17},{... | collective-permute-start | bytes 884744 | tf_op jit(solution)/shard_map/ppermute | solution.py:215
  393.9 11.1 %collective-permute-start.47 = (bf16[4,64,768]{2,1,0:T(8,128)(2,1)S(1)}, bf16[4,64,768]{2,1,0:T(8,128)(2,1)S(1)}, u32[]{:S(2)}, u32[]{:S(2)}) collective-permute-start(bf16[4,64,768]{2,1,0:T(8,128)(2,1)S(1)} %slice_add_fusion), channel_id=1, source_target_pairs={{0,2},{1,3},{2,0},{3,1},{4,6},{5,7},{6,4},{7,5},{8,10},{9,11},{10,... | collective-permute-start | bytes 1179656 | tf_op jit(solution)/shard_map/ppermute | solution.py:28
  395.9 18.5 %collective-permute-start.54 = (bf16[192,768]{1,0:T(8,128)(2,1)S(1)}, bf16[192,768]{1,0:T(8,128)(2,1)}, u32[]{:S(2)}, u32[]{:S(2)}) collective-permute-start(bf16[192,768]{1,0:T(8,128)(2,1)S(1)} %broadcast_select_fusion.25), channel_id=1, source_target_pairs={{0,8},{4,12},{8,0},{12,4},{16,24},{20,28},{24,16},{28,20},{1,9},{5... | collective-permute-start | bytes 884744 | tf_op jit(solution)/shard_map/ppermute | solution.py:215
  410.2 19.4 %collective-permute-start.68 = (bf16[192,768]{1,0:T(8,128)(2,1)S(1)}, bf16[192,768]{1,0:T(8,128)(2,1)S(1)}, u32[]{:S(2)}, u32[]{:S(2)}) collective-permute-start(bf16[192,768]{1,0:T(8,128)(2,1)S(1)} %select_add_fusion.7), channel_id=1, source_target_pairs={{0,16},{4,20},{8,24},{12,28},{16,0},{20,4},{24,8},{28,12},{1,17},{... | collective-permute-start | bytes 884744 | tf_op jit(solution)/shard_map/ppermute | solution.py:223
  412.9 16.8 %collective-permute-start.50 = (f32[17064]{0:T(1024)S(1)}, f32[17064]{0:T(1024)S(1)}, u32[]{:S(2)}, u32[]{:S(2)}) collective-permute-start(f32[17064]{0:T(1024)S(1)} %concatenate.142), channel_id=1, source_target_pairs={{0,4},{4,0},{8,12},{12,8},{16,20},{20,16},{24,28},{28,24},{1,5},{5... | collective-permute-start | bytes 204776 | tf_op jit(solution)/shard_map/ppermute | solution.py:236
  415.5 20.0 %collective-permute-start.55 = (bf16[96,768]{1,0:T(8,128)(2,1)S(1)}, bf16[96,768]{1,0:T(8,128)(2,1)S(1)}, u32[]{:S(2)}, u32[]{:S(2)}) collective-permute-start(bf16[96,768]{1,0:T(8,128)(2,1)S(1)} %broadcast_select_fusion.34), channel_id=1, source_target_pairs={{0,16},{4,20},{8,24},{12,28},{16,0},{20,4},{24,8},{28,12},{1,17},{... | collective-permute-start | bytes 442376 | tf_op jit(solution)/shard_map/ppermute | solution.py:215
  429.7 5.1 %collective-permute-start.51 = (f32[17064]{0:T(1024)S(1)}, f32[17064]{0:T(1024)S(1)}, u32[]{:S(2)}, u32[]{:S(2)}) collective-permute-start(f32[17064]{0:T(1024)S(1)} %add.472), channel_id=1, source_target_pairs={{0,8},{4,12},{8,0},{12,4},{16,24},{20,28},{24,16},{28,20},{1,9},{5... | collective-permute-start | bytes 204776 | tf_op jit(solution)/shard_map/ppermute | solution.py:236
  429.8 31.1 %collective-permute-start.69 = (bf16[384,768]{1,0:T(8,128)(2,1)S(1)}, bf16[384,768]{1,0:T(8,128)(2,1)}, u32[]{:S(2)}, u32[]{:S(2)}) collective-permute-start(bf16[384,768]{1,0:T(8,128)(2,1)S(1)} %pad_maximum_fusion.18), channel_id=1, source_target_pairs={{0,8},{4,12},{8,0},{12,4},{16,24},{20,28},{24,16},{28,20},{1,9},{5... | collective-permute-start | bytes 1769480 | tf_op jit(solution)/shard_map/ppermute | solution.py:223
  434.8 12.3 %collective-permute-start.52 = (f32[17064]{0:T(1024)S(1)}, f32[17064]{0:T(1024)S(1)}, u32[]{:S(2)}, u32[]{:S(2)}) collective-permute-start(f32[17064]{0:T(1024)S(1)} %add.473), channel_id=1, source_target_pairs={{0,16},{4,20},{8,24},{12,28},{16,0},{20,4},{24,8},{28,12},{1,17},{... | collective-permute-start | bytes 204776 | tf_op jit(solution)/shard_map/ppermute | solution.py:236
  435.4 15.5 %collective-permute-start.56 = (bf16[96,768]{1,0:T(8,128)(2,1)S(1)}, bf16[96,768]{1,0:T(8,128)(2,1)S(1)}, u32[]{:S(2)}, u32[]{:S(2)}) collective-permute-start(bf16[96,768]{1,0:T(8,128)(2,1)S(1)} %select_add_fusion.11), channel_id=1, source_target_pairs={{0,16},{4,20},{8,24},{12,28},{16,0},{20,4},{24,8},{28,12},{1,17},{... | collective-permute-start | bytes 442376 | tf_op jit(solution)/shard_map/ppermute | solution.py:223
  451.0 8.2 %collective-permute-start.57 = (bf16[192,768]{1,0:T(8,128)(2,1)S(1)}, bf16[192,768]{1,0:T(8,128)(2,1)S(1)}, u32[]{:S(2)}, u32[]{:S(2)}) collective-permute-start(bf16[192,768]{1,0:T(8,128)(2,1)S(1)} %pad_maximum_fusion.20), channel_id=1, source_target_pairs={{0,8},{4,12},{8,0},{12,4},{16,24},{20,28},{24,16},{28,20},{1,9},{5... | collective-permute-start | bytes 884744 | tf_op jit(solution)/shard_map/ppermute | solution.py:223
  459.3 16.3 %collective-permute-start.58 = (bf16[384,768]{1,0:T(8,128)(2,1)S(1)}, bf16[384,768]{1,0:T(8,128)(2,1)S(1)}, u32[]{:S(2)}, u32[]{:S(2)}) collective-permute-start(bf16[384,768]{1,0:T(8,128)(2,1)S(1)} %pad_maximum_fusion.16), channel_id=1, source_target_pairs={{0,4},{4,0},{8,12},{12,8},{16,20},{20,16},{24,28},{28,24},{1,5},{5... | collective-permute-start | bytes 1769480 | tf_op jit(solution)/shard_map/ppermute | solution.py:223
  462.3 34.0 %collective-permute-start.70 = (bf16[768,768]{1,0:T(8,128)(2,1)S(1)}, bf16[768,768]{1,0:T(8,128)(2,1)S(1)}, u32[]{:S(2)}, u32[]{:S(2)}) collective-permute-start(bf16[768,768]{1,0:T(8,128)(2,1)S(1)} %pad_maximum_fusion.10), channel_id=1, source_target_pairs={{0,4},{4,0},{8,12},{12,8},{16,20},{20,16},{24,28},{28,24},{1,5},{5... | collective-permute-start | bytes 3538952 | tf_op jit(solution)/shard_map/ppermute | solution.py:223
  (179 other events, 1254.9 us)

commit v2 on v1

v2 whole, which is shorter than its diff:
```python
import functools

import jax
import jax.numpy as jnp
from jax import lax
from jax.experimental import pallas as pl
from jax.experimental.pallas import tpu as pltpu
from jax.sharding import PartitionSpec as P

HEAD_DIM = 64
BUCKETS = 732
LAYERS = 2
EPSILON = 1e-06
VMEM_GRANT = 10 * 1024 * 1024
GELU_SCALE = 0.7978845608028654
GELU_CUBE = 0.044715

BF = jnp.bfloat16
F32 = jnp.float32
CORE = [(i, i ^ 1) for i in range(4)]
CHIP = [(i, i ^ 2) for i in range(4)]
VMEM = pl.BlockSpec(memory_space=pltpu.VMEM)
NN = (((1,), (0,)), ((), ()))
NT = (((1,), (1,)), ((), ()))
TN = (((0,), (0,)), ((), ()))


def shape(dims, kind):
    return jax.ShapeDtypeStruct(dims, kind)


def scalar(values):
    return (values, pl.BlockSpec(memory_space=pltpu.SMEM))


def kernel_call(body, name, outs, flops, *operands, scratch=()):
    specs = [x[1] if isinstance(x, tuple) else VMEM for x in operands]
    operands = [x[0] if isinstance(x, tuple) else x for x in operands]
    moved = sum(x.size * x.dtype.itemsize for x in operands) + sum(
        o.size * o.dtype.itemsize for o in outs
    )
    return pl.pallas_call(
        body,
        out_shape=tuple(outs),
        in_specs=specs,
        out_specs=tuple([VMEM] * len(outs)),
        scratch_shapes=list(scratch),
        name=name,
        compiler_params=pltpu.CompilerParams(vmem_limit_bytes=VMEM_GRANT),
        cost_estimate=pl.CostEstimate(flops=flops // 100, bytes_accessed=moved // 100, transcendentals=0),
    )(*operands)


def mxu(left, right, dims):
    return lax.dot_general(left, right, dims, preferred_element_type=F32)


def swap_core(values):
    return lax.ppermute(values, "tensor", CORE)


def swap_chip(values):
    return lax.ppermute(values, "tensor", CHIP)


def tied(values, token):
    return lax.optimization_barrier((values, token))[0]


def spread(own, meanwhile=()):
    far = swap_chip(own)
    near = swap_core(own)
    if meanwhile:
        far = tied(far, meanwhile)
    return [own, near, far, swap_core(far)]


def collect(partial):
    pair_far = partial[2] + swap_core(partial[3])
    return [partial[0], swap_core(partial[1])], swap_chip(pair_far), pair_far


def bias_kernel(table_ref, index_ref, pad_ref, member_ref, out_ref, ordered_ref, bias_ref):
    heads, layers, entries = table_ref.shape
    lanes = 128
    chunks = (entries + lanes - 1) // lanes
    member = member_ref[0]
    low, high = member & 1, member >> 1
    block = index_ref.shape[0] // 4

    def picked(ref, rows, half):
        tile = ref[rows, pl.ds(pl.multiple_of((half ^ high) * lanes, lanes), lanes)]
        return jnp.where(low == 1, jnp.concatenate([tile[:, block:], tile[:, :block]], axis=1), tile)

    for half in range(2):
        columns = slice(half * lanes, half * lanes + lanes)
        pads = picked(pad_ref, slice(None), half)
        bias_ref[:, 0, columns] = jnp.where(pads == 1, -1000000000.0, 0.0)

    def line_of(layer, head, chunk):
        size = min(lanes, entries - chunk * lanes)
        line = table_ref[head, layer : layer + 1, chunk * lanes : chunk * lanes + size].astype(F32)
        return jnp.concatenate([line, jnp.zeros((1, lanes - size), F32)], axis=1) if size < lanes else line

    lines = [[line_of(l, h, c) for c in range(chunks)] for l in range(layers) for h in range(heads)]

    def rows_step(step, carry):
        start = (member ^ (step // 4)) * block + (step % 4) * 16
        rows = pl.ds(pl.multiple_of(start, 16), 16)
        place = pl.ds(pl.multiple_of(step * 16, 16), 16)
        for half in range(2):
            columns = slice(half * lanes, half * lanes + lanes)
            index = picked(index_ref, rows, half)
            ordered_ref[place, columns] = index
            lane, chunk = index & (lanes - 1), index // lanes
            here = [chunk == c for c in range(chunks)]
            for table in range(layers * heads):
                total = jnp.zeros((16, lanes), F32)
                for c in range(chunks):
                    line = jnp.broadcast_to(lines[table][c], (16, lanes))
                    total = jnp.where(here[c], jnp.take_along_axis(line, lane, axis=1), total)
                out_ref[table // heads, table % heads, place, columns] = total.astype(out_ref.dtype)
        return carry

    lax.fori_loop(0, index_ref.shape[0] // 16, rows_step, 0)


def bias_of_buckets(tables, buckets, pads, member):
    heads, layers, entries = tables.shape
    pages, length = pads.shape
    outs = [shape((layers, heads) + buckets.shape, BF), shape(buckets.shape, jnp.int32)]
    outs += [shape((pages, 1, length), F32)]
    return kernel_call(
        bias_kernel, "bias_of_buckets", outs, 4_000_000_000, tables, buckets, pads, scalar(member)
    )


def bucket_kernel(values_ref, index_ref, out_ref):
    heads, size, width = values_ref.shape
    chunk = 32

    def step(i, total):
        start = pl.multiple_of(i * chunk, chunk)
        index = index_ref[pl.ds(start, chunk), :]
        left, right = [], []
        for r in range(chunk):
            row = index[r : r + 1, :]
            at_high = lax.broadcasted_iota(jnp.int32, (24, width), 0) == (row >> 5)
            at_low = lax.broadcasted_iota(jnp.int32, (32, width), 0) == (row & 31)
            right.append(jnp.where(at_low, 1.0, 0.0).astype(BF))
            left.append(
                jnp.concatenate(
                    [
                        jnp.where(at_high, values_ref[h, pl.ds(start + r, 1), :], 0.0).astype(BF)
                        for h in range(heads)
                    ],
                    0,
                )
            )
        return total + mxu(jnp.concatenate(left, 1), jnp.concatenate(right, 1), NT)

    out_ref[...] = lax.fori_loop(0, size // chunk, step, jnp.zeros((heads * 24, 32), F32))


def sum_by_bucket(values, buckets):
    heads = values.shape[0]
    return kernel_call(
        bucket_kernel, "sum_by_bucket", [shape((heads * 24, 32), F32)], 6_000_000_000, values, buckets
    )[0]


def normal_of(values):
    center = values - jnp.mean(values, axis=-1, keepdims=True)
    inverse = lax.rsqrt(jnp.mean(center * center, axis=-1, keepdims=True) + EPSILON)
    return center * inverse, inverse


def of_layer(ref, layer):
    return ref[layer : layer + 1, :].astype(F32)


def mask_columns(masked_ref):
    pages, size = masked_ref.shape
    row = lax.broadcasted_iota(jnp.int32, (size, size), 0)
    diagonal = row == lax.broadcasted_iota(jnp.int32, (size, size), 1)
    flags = masked_ref[...].astype(F32)
    spreads = [jnp.where(diagonal, flags[page : page + 1, :], 0.0) for page in range(pages)]
    return [jnp.sum(values, axis=1, keepdims=True) == 1.0 for values in spreads]


def first_norm_kernel(
    rows_ref, grads_ref, masked_ref, embed_ref, gain_ref, shift_ref, hidden_ref, normed_ref, grad_ref, sums_ref
):
    size, pages, width = rows_ref.shape
    gain, shift = of_layer(gain_ref, 0), of_layer(shift_ref, 0)
    total = jnp.zeros((8, width), F32)
    masks = mask_columns(masked_ref)
    for page in range(pages):
        at = slice(page * size, page * size + size)
        masked = masks[page]
        rows = jnp.where(masked, embed_ref[...].astype(F32), rows_ref[:, page, :].astype(F32))
        hidden_ref[at, :] = rows
        normed_ref[at, :] = (normal_of(rows)[0] * gain + shift).astype(BF)
        grad = grads_ref[:, page, :]
        grad_ref[at, :] = grad
        total = total + fold_rows(grad.astype(F32))
    sums_ref[...] = total


def first_norm(rows, grads, masked, embed, gains, shifts):
    size, pages, width = rows.shape
    flat = (size * pages, width)
    return kernel_call(
        first_norm_kernel,
        "first_norm",
        [shape(flat, F32), shape(flat, BF), shape(flat, BF), shape((8, width), F32)],
        1_000_000_000,
        rows,
        grads,
        masked,
        embed,
        gains,
        shifts,
    )


def norm_kernel(layers, hidden_ref, one_ref, two_ref, three_ref, bias_ref, gain_ref, shift_ref, out_ref, normed_ref):
    size = 64
    bias = of_layer(bias_ref, layers[0])
    gain, shift = of_layer(gain_ref, layers[1]), of_layer(shift_ref, layers[1])

    def step(i, carry):
        at = pl.ds(pl.multiple_of(i * size, size), size)
        total = one_ref[at, :].astype(F32) + two_ref[at, :].astype(F32) + three_ref[at, :].astype(F32)
        rows = hidden_ref[at, :] + total + bias
        out_ref[at, :] = rows
        normed_ref[at, :] = (normal_of(rows)[0] * gain + shift).astype(BF)
        return carry

    lax.fori_loop(0, hidden_ref.shape[0] // size, step, 0, unroll=True)


def add_norm(hidden, terms, layers, biases, gains, shifts):
    return kernel_call(
        functools.partial(norm_kernel, layers),
        "add_norm",
        [shape(hidden.shape, F32), shape(hidden.shape, BF)],
        1_000_000_000,
        hidden,
        *terms,
        biases,
        gains,
        shifts,
    )


def result_kernel(layer, hidden_ref, one_ref, two_ref, three_ref, bias_ref, out_ref):
    size, pages, unused = out_ref.shape
    bias = of_layer(bias_ref, layer)
    for page in range(pages):
        at = slice(page * size, page * size + size)
        total = one_ref[at, :].astype(F32) + two_ref[at, :].astype(F32) + three_ref[at, :].astype(F32)
        out_ref[:, page, :] = (hidden_ref[at, :] + total + bias).astype(BF)


def last_result(hidden, terms, layer, biases, pages):
    rows, width = hidden.shape
    return kernel_call(
        functools.partial(result_kernel, layer),
        "last_result",
        [shape((rows // pages, pages, width), BF)],
        1_000_000_000,
        hidden,
        *terms,
        biases,
    )[0]


def fold_rows(values):
    return jnp.sum(values.reshape(-1, 8, values.shape[-1]), axis=0)


def norm_back_step(at, grad_ref, terms, values_ref, gain, sums_ref):
    total = sum(term[at, :].astype(F32) for term in terms)
    normal, inverse = normal_of(values_ref[at, :])
    scaled = total * gain
    inner = scaled - jnp.mean(scaled, -1, keepdims=True)
    inner = inner - normal * jnp.mean(scaled * normal, -1, keepdims=True)
    grad = grad_ref[at, :].astype(F32) + inner * inverse
    sums_ref[0] += fold_rows(total * normal)
    sums_ref[1] += fold_rows(total)
    return grad


def norm_back_kernel(layer, grad_ref, one_ref, two_ref, three_ref, values_ref, gain_ref, out_ref, low_ref, sums_ref):
    size = 64
    sums_ref[...] = jnp.zeros(sums_ref.shape, F32)

    def step(i, carry):
        at = pl.ds(pl.multiple_of(i * size, size), size)
        terms = (one_ref, two_ref, three_ref)
        grad = norm_back_step(at, grad_ref, terms, values_ref, of_layer(gain_ref, layer), sums_ref)
        sums_ref[2] += fold_rows(grad)
        out_ref[at, :] = grad
        low_ref[at, :] = grad.astype(BF)
        return carry

    lax.fori_loop(0, grad_ref.shape[0] // size, step, 0, unroll=True)


def norm_back(grad, terms, values, layer, gains):
    return kernel_call(
        functools.partial(norm_back_kernel, layer),
        "norm_back",
        [shape(grad.shape, F32), shape(grad.shape, BF), shape((3, 8, grad.shape[-1]), F32)],
        1_500_000_000,
        grad,
        *terms,
        values,
        gains,
    )


def last_norm_back_kernel(
    grad_ref, one_ref, two_ref, three_ref, values_ref, gain_ref, masked_ref, out_ref, sums_ref
):
    size, pages, unused = out_ref.shape
    sums_ref[...] = jnp.zeros(sums_ref.shape, F32)
    masks = mask_columns(masked_ref)
    for page in range(pages):
        at = slice(page * size, page * size + size)
        terms = (one_ref, two_ref, three_ref)
        grad = norm_back_step(at, grad_ref, terms, values_ref, of_layer(gain_ref, 0), sums_ref)
        masked = masks[page]
        sums_ref[2] += fold_rows(jnp.where(masked, grad, 0.0))
        out_ref[:, page, :] = jnp.where(masked, 0.0, grad)


def last_norm_back(grad, terms, values, gains, masked):
    pages, size = masked.shape
    width = grad.shape[-1]
    return kernel_call(
        last_norm_back_kernel,
        "last_norm_back",
        [shape((size, pages, width), F32), shape((3, 8, width), F32)],
        1_500_000_000,
        grad,
        *terms,
        values,
        gains,
        masked,
    )


def page_rows(refs, page, size):
    at = pl.ds(pl.multiple_of(page * size, size), size)
    return jnp.concatenate([ref[at, :] for ref in refs], axis=0)


def put_page(refs, page, size, values):
    at = pl.ds(pl.multiple_of(page * size, size), size)
    for i, ref in enumerate(refs):
        ref[at, :] = values[i * size : (i + 1) * size]


def head_masks(heads, kind):
    lane = lax.broadcasted_iota(jnp.int32, (1, heads * HEAD_DIM), 1)
    return [jnp.where((lane // HEAD_DIM) == h, 1.0, 0.0).astype(kind) for h in range(heads)]


def attention_kernel(
    layer, x0, x1, x2, x3, w_ref, bias_ref, rel_ref, pad_ref, wo_ref, p0, p1, p2, p3, q_ref, k_ref, v_ref, pb_ref, o_ref
):
    pages = pad_ref.shape[0]
    heads = rel_ref.shape[1]
    size = x0.shape[0] // pages

    def step(page, carry):
        masks = head_masks(heads, BF)
        rows = page_rows((x0, x1, x2, x3), page, size)
        q = ((mxu(rows, w_ref[layer, 0], NT) + bias_ref[layer, 0:1, :].astype(F32)) * HEAD_DIM**-0.5).astype(BF)
        k = mxu(rows, w_ref[layer, 1], NT).astype(BF)
        v = (mxu(rows, w_ref[layer, 2], NT) + bias_ref[layer, 1:2, :].astype(F32)).astype(BF)
        q_ref[page], k_ref[page], v_ref[page] = q, k, v
        o = jnp.zeros(q.shape, F32)
        for h in range(heads):
            s = mxu(q * masks[h], k, NT) + (rel_ref[layer, h].astype(F32) + pad_ref[page])
            e = jnp.exp(s - jnp.max(s, axis=-1, keepdims=True))
            pb = (e * (1.0 / jnp.sum(e, axis=-1, keepdims=True))).astype(BF)
            pb_ref[page, h] = pb
            o = o + mxu(pb, v * masks[h], NN)
        o = o.astype(BF)
        o_ref[page] = o
        put_page((p0, p1, p2, p3), page, size, mxu(o, wo_ref[layer], NN).astype(BF))
        return carry

    lax.fori_loop(0, pages, step, 0, unroll=2)


def attention(layer, blocks, w_qkv, qv_bias, rel_bias, pad_bias, w_out):
    pages, unused, length = pad_bias.shape
    heads = rel_bias.shape[1]
    local = heads * HEAD_DIM
    outs = [shape(blocks[0].shape, BF)] * 4 + [shape((pages, length, local), BF)] * 3
    outs += [shape((pages, heads, length, length), BF), shape((pages, length, local), BF)]
    made = kernel_call(
        functools.partial(attention_kernel, layer), "attention", outs, 6_000_000_000, *blocks, w_qkv, qv_bias, rel_bias, pad_bias, w_out
    )
    return made[:4], made[4:]


def attention_back_kernel(
    layer, g0, g1, g2, g3, q_ref, k_ref, v_ref, pb_ref, w_ref, wo_ref, p0, p1, p2, p3, stack_ref, total_ref, sums_ref
):
    pages, heads = pb_ref.shape[:2]
    size = g0.shape[0] // pages
    local = heads * HEAD_DIM
    total_ref[...] = jnp.zeros(total_ref.shape, F32)
    sums_ref[...] = jnp.zeros(sums_ref.shape, F32)

    def step(page, carry):
        masks = head_masks(heads, BF)
        rows = page_rows((g0, g1, g2, g3), page, size)
        go = mxu(rows, wo_ref[layer], NT).astype(BF)
        q, k, v = q_ref[page], k_ref[page], v_ref[page]
        gq = gk = gv = jnp.zeros(q.shape, F32)
        for h in range(heads):
            pb = pb_ref[page, h]
            go_h = go * masks[h]
            gv = gv + mxu(pb, go_h, TN)
            gp = mxu(go_h, v, NT)
            p = pb.astype(F32)
            gs = (p * (gp - jnp.sum(p * gp, axis=-1, keepdims=True))).astype(BF)
            total_ref[h] += gs.astype(F32)
            gq = gq + mxu(gs, k * masks[h], NN)
            gk = gk + mxu(gs, q * masks[h], TN)
        gq = (gq.astype(BF).astype(F32) * HEAD_DIM**-0.5).astype(BF)
        gk, gv = gk.astype(BF), gv.astype(BF)
        stack_ref[page, 0], stack_ref[page, 1], stack_ref[page, 2] = gq, gk, gv
        sums_ref[0] += fold_rows(gq.astype(F32))
        sums_ref[1] += fold_rows(gv.astype(F32))
        ga = mxu(gq, w_ref[layer, 0], NN) + mxu(gk, w_ref[layer, 1], NN) + mxu(gv, w_ref[layer, 2], NN)
        put_page((p0, p1, p2, p3), page, size, ga.astype(BF))
        return carry

    lax.fori_loop(0, pages, step, 0, unroll=2)


def attention_back(layer, blocks, kept, w_qkv, w_out):
    q, k, v, pb, unused = kept
    pages, length, local = q.shape
    heads = pb.shape[1]
    outs = [shape(blocks[0].shape, BF)] * 4
    outs += [shape((pages, 3, length, local), BF), shape((heads, length, length), F32), shape((2, 8, local), F32)]
    made = kernel_call(
        functools.partial(attention_back_kernel, layer), "attention_back", outs, 9_000_000_000, *blocks, q, k, v, pb, w_qkv, w_out
    )
    return made[:4], made[4:]


def fetched(sources, targets, sems):
    copies = [pltpu.make_async_copy(s, t, sems.at[i]) for i, (s, t) in enumerate(zip(sources, targets))]
    for copy in copies:
        copy.start()
    return copies


def fetching_call(body, name, outs, flops, operands, place, scratch):
    moved = sum(x.size * x.dtype.itemsize for x in operands)
    return pl.pallas_call(
        body,
        out_shape=tuple(outs),
        in_specs=[pl.BlockSpec(memory_space=pltpu.HBM)] * len(operands) + [pl.BlockSpec(memory_space=pltpu.SMEM)],
        out_specs=tuple([VMEM] * len(outs)),
        scratch_shapes=[pltpu.VMEM(x.shape, x.dtype) for x in operands]
        + [pltpu.SemaphoreType.DMA((len(operands),))]
        + list(scratch),
        name=name,
        compiler_params=pltpu.CompilerParams(vmem_limit_bytes=2 * VMEM_GRANT),
        cost_estimate=pl.CostEstimate(flops=flops // 100, bytes_accessed=moved // 100, transcendentals=0),
    )(*operands, place)


def attention_grads_kernel(*refs):
    sources, place_ref, keep_ref, send_ref = refs[:10], *refs[10:13]
    targets, sems, acc_ref = refs[13:23], *refs[23:]
    copies = fetched(sources, targets, sems)
    stack_ref, o_ref = targets[8:]
    pages, parts, length, local = stack_ref.shape
    size = targets[0].shape[0] // pages
    acc_ref[...] = jnp.zeros(acc_ref.shape, F32)
    for copy in copies:
        copy.wait()

    def step(page, carry):
        rows = page_rows(targets[:4], page, size)
        grad = page_rows(targets[4:8], page, size)
        acc_ref[:local] += mxu(o_ref[page], grad, TN)
        for t in range(parts):
            acc_ref[(t + 1) * local : (t + 2) * local] += mxu(stack_ref[page, t], rows, TN)
        return carry

    lax.fori_loop(0, pages, step, 0, unroll=2)
    half = keep_ref.shape[0]
    mine = place_ref[0] & 1
    keep_ref[...] = acc_ref[pl.ds(pl.multiple_of(mine * half, half), half), :].astype(BF)
    send_ref[...] = acc_ref[pl.ds(pl.multiple_of((1 - mine) * half, half), half), :].astype(BF)


def attention_grads(rows, grads, stack, o, place):
    local, width = o.shape[-1], rows[0].shape[-1]
    return fetching_call(
        attention_grads_kernel,
        "attention_grads",
        [shape((2 * local, width), BF)] * 2,
        3_000_000_000,
        [*rows, *grads, stack, o],
        place,
        [pltpu.VMEM((4 * local, width), F32)],
    )


def gelu_parts(u):
    square = u * u
    t = jnp.tanh(GELU_SCALE * (u + GELU_CUBE * (square * u)))
    plus = 0.5 * (1.0 + t)
    slope = plus + 0.5 * u * (1.0 - t * t) * (GELU_SCALE * (1.0 + (3.0 * GELU_CUBE) * square))
    return u * plus, slope


def up_rows(layer, at, rows_ref, up_ref, bias_ref, z_ref, slope_ref, block):
    u = mxu(rows_ref[at, :], up_ref[layer], NN) + of_layer(bias_ref, layer)
    z, slope = gelu_parts(u)
    z = z.astype(BF)
    z_ref[block, at, :] = z
    return z, slope


def forward_kernel(layer, c0, c1, c2, c3, up_ref, bias_ref, down_ref, p0, p1, p2, p3, z_ref, slope_ref):
    size = 256
    for block, (rows_ref, out_ref) in enumerate(zip((c0, c1, c2, c3), (p0, p1, p2, p3))):

        def step(i, carry):
            at = pl.ds(pl.multiple_of(i * size, size), size)
            z, slope = up_rows(layer, at, rows_ref, up_ref, bias_ref, z_ref, slope_ref, block)
            slope_ref[block, at, :] = slope.astype(BF)
            out_ref[at, :] = mxu(z, down_ref[layer], NN).astype(BF)
            return carry

        lax.fori_loop(0, rows_ref.shape[0] // size, step, 0)


def feed_forward(layer, blocks, w_up, up_bias, w_down):
    units = w_up.shape[2]
    size = blocks[0].shape[0]
    outs = [shape(blocks[0].shape, BF)] * 4 + [shape((4, size, units), BF)] * 2
    made = kernel_call(functools.partial(forward_kernel, layer), "feed_forward", outs, 4_000_000_000, *blocks, w_up, up_bias, w_down)
    return made[:4], made[4:]


def down_kernel(layer, z_ref, down_ref, p0, p1, p2, p3):
    size = 256
    for block, out_ref in enumerate((p0, p1, p2, p3)):

        def step(i, carry):
            at = pl.ds(pl.multiple_of(i * size, size), size)
            out_ref[at, :] = mxu(z_ref[block, at, :], down_ref[layer], NN).astype(BF)
            return carry

        lax.fori_loop(0, out_ref.shape[0] // size, step, 0)


def down_product(layer, z, w_down):
    outs = [shape((z.shape[1], w_down.shape[2]), BF)] * 4
    return kernel_call(functools.partial(down_kernel, layer), "down_product", outs, 1_500_000_000, z, w_down)


def back_kernel(layer, g0, g1, g2, g3, slope_ref, up_ref, down_ref, p0, p1, p2, p3, gu_ref, sums_ref):
    size = 256
    sums_ref[...] = jnp.zeros(sums_ref.shape, F32)
    for block, (grad_ref, out_ref) in enumerate(zip((g0, g1, g2, g3), (p0, p1, p2, p3))):

        def step(i, carry):
            at = pl.ds(pl.multiple_of(i * size, size), size)
            gz = mxu(grad_ref[at, :], down_ref[layer], NT)
            gu = (gz * slope_ref[block, at, :].astype(F32)).astype(BF)
            gu_ref[block, at, :] = gu
            sums_ref[...] += fold_rows(gu.astype(F32))
            out_ref[at, :] = mxu(gu, up_ref[layer], NT).astype(BF)
            return carry

        lax.fori_loop(0, grad_ref.shape[0] // size, step, 0)


def feed_back(layer, blocks, slope, w_up, w_down):
    size, units = blocks[0].shape[0], w_up.shape[2]
    outs = [shape(blocks[0].shape, BF)] * 4 + [shape((4, size, units), BF), shape((8, units), F32)]
    made = kernel_call(functools.partial(back_kernel, layer), "feed_back", outs, 4_000_000_000, *blocks, slope, w_up, w_down)
    return made[:4], made[4:]


def both_kernel(
    layer, c0, c1, c2, c3, g0, g1, g2, g3, up_ref, bias_ref, down_ref, p0, p1, p2, p3, z_ref, gu_ref, sums_ref
):
    size = 256
    sums_ref[...] = jnp.zeros(sums_ref.shape, F32)
    for block, (rows_ref, grad_ref, out_ref) in enumerate(
        zip((c0, c1, c2, c3), (g0, g1, g2, g3), (p0, p1, p2, p3))
    ):

        def step(i, carry):
            at = pl.ds(pl.multiple_of(i * size, size), size)
            gz = mxu(grad_ref[at, :], down_ref[layer], NT)
            z, slope = up_rows(layer, at, rows_ref, up_ref, bias_ref, z_ref, None, block)
            gu = (gz * slope).astype(BF)
            gu_ref[block, at, :] = gu
            sums_ref[...] += fold_rows(gu.astype(F32))
            out_ref[at, :] = mxu(gu, up_ref[layer], NT).astype(BF)
            return carry

        lax.fori_loop(0, rows_ref.shape[0] // size, step, 0)


def feed_both(layer, blocks, grads, w_up, up_bias, w_down):
    size, units = blocks[0].shape[0], w_up.shape[2]
    outs = [shape(blocks[0].shape, BF)] * 4 + [shape((4, size, units), BF)] * 2 + [shape((8, units), F32)]
    made = kernel_call(
        functools.partial(both_kernel, layer),
        "feed_both",
        outs,
        6_000_000_000,
        *blocks,
        *grads,
        w_up,
        up_bias,
        w_down,
    )
    return made[:4], made[4:]


def feed_grads_kernel(parts, *refs):
    sources, place_ref = refs[:10], refs[10]
    out_refs, refs = refs[11 : 11 + 2 * parts], refs[11 + 2 * parts :]
    targets, sems, both_ref = refs[:10], *refs[10:]
    copies = fetched(sources, targets, sems)
    rows_refs, grad_refs, z_ref, gu_ref = targets[:4], targets[4:8], *targets[8:]
    for copy in copies:
        copy.wait()
    unused, units, width = both_ref.shape
    step = 256
    for start in range(0, units, step):
        rows = slice(start, start + step)
        down = sum(mxu(z_ref[i, :, rows], g[...], TN) for i, g in enumerate(grad_refs))
        both_ref[0, rows, :] = down.astype(BF)
        up = sum(mxu(c[:, rows], gu_ref[i], TN) for i, c in enumerate(rows_refs))
        both_ref[1, rows, :] = up.astype(BF)
    mine = place_ref[0] & 1
    size = units // parts
    for part in range(parts):
        rows = slice(part * size, (part + 1) * size)
        out_refs[2 * part][...] = both_ref[mine, rows, :]
        out_refs[2 * part + 1][...] = both_ref[1 - mine, rows, :]


def feed_grads(rows, grads, z, gu, place, parts):
    units, width = z.shape[-1], rows[0].shape[-1]
    made = fetching_call(
        functools.partial(feed_grads_kernel, parts),
        "feed_grads",
        [shape((units // parts, width), BF)] * (2 * parts),
        4_000_000_000,
        [*rows, *grads, z, gu],
        place,
        [pltpu.VMEM((2, units, width), BF)],
    )
    return [made[2 * i : 2 * i + 2] for i in range(parts)]


def partners(bits, bit):
    return [(i, i ^ (1 << bit)) for i in range(1 << len(bits))]


def halve_kernel(bit, keep_ref, got_ref, place_ref, out_keep_ref, out_send_ref):
    half = out_keep_ref.shape[0]
    mine = (place_ref[0] >> bit) & 1
    for out_ref, which in ((out_send_ref, 1 - mine), (out_keep_ref, mine)):
        at = pl.ds(pl.multiple_of(which * half, half), half)
        out_ref[...] = (keep_ref[at, :].astype(F32) + got_ref[at, :].astype(F32)).astype(BF)


def halve(keep, got, bit, place):
    rows, width = keep.shape
    outs = [shape((rows // 2, width), BF)] * 2
    return kernel_call(
        functools.partial(halve_kernel, bit), "halve", outs, 200_000_000, keep, got, scalar(place)
    )


def join_kernel(bit, own_ref, got_ref, place_ref, out_ref):
    half = own_ref.shape[0]
    mine = (place_ref[0] >> bit) & 1
    out_ref[pl.ds(pl.multiple_of(mine * half, half), half), :] = own_ref[...]
    out_ref[pl.ds(pl.multiple_of((1 - mine) * half, half), half), :] = got_ref[...]


def join(own, got, bit, place):
    rows, width = own.shape
    return kernel_call(
        functools.partial(join_kernel, bit),
        "join",
        [shape((2 * rows, width), BF)],
        200_000_000,
        own,
        got,
        scalar(place),
    )[0]


class PageSum:
    def __init__(self, halves, bits, place):
        self.own, send = halves
        self.bits, self.place = bits, place
        self.cuts = bits[1:3]
        self.plan = [(self.down, bit) for bit in self.cuts] + [(self.turn, None)]
        self.plan += [(self.up, bit) for bit in reversed(self.cuts)]
        self.got = self.swap(send, 0)

    def swap(self, values, bit):
        self.sent = values
        return lax.ppermute(values, "dp", partners(self.bits, bit))

    def down(self, got, bit):
        self.own, send = halve(self.own, got, bit, self.place)
        return self.swap(send, bit)

    def turn(self, got, unused):
        self.own = self.own + got
        for bit in self.bits[3:]:
            self.own = self.own + self.swap(self.own, bit)
        return self.swap(self.own, self.cuts[-1] if self.cuts else 0)

    def up(self, got, bit):
        self.own = join(self.own, got, bit, self.place)
        index = self.bits.index(bit) - 1
        return self.swap(self.own, self.bits[index])

    def step(self, token):
        action, bit = self.plan.pop(0)
        self.got = action(tied(self.got, token), bit)
        return self.sent

    def ended(self):
        return self.own, self.got


def sum_small(values, axis, bits, count):
    for bit in bits:
        values = values + lax.ppermute(values, axis, partners(range(count), bit))
    return values


def row_sum(values):
    return jnp.sum(values, axis=0, keepdims=True)


def pack_rows_kernel(ones0, twos0, ones1, twos1, last_ref, out_ref):
    out_ref[...] = jnp.zeros(out_ref.shape, F32)
    for layer, (one_ref, two_ref) in enumerate(((ones0, twos0), (ones1, twos1))):
        down = ones1[2] if layer == 0 else last_ref[...]
        members = [one_ref[0], one_ref[1], two_ref[2], two_ref[0], two_ref[1], down]
        for i, member in enumerate(members):
            out_ref[2 * i + layer : 2 * i + layer + 1, :] = row_sum(member)
    out_ref[12:13, :] = row_sum(ones0[2])


def pack_rows(ones, twos, last):
    return kernel_call(
        pack_rows_kernel,
        "pack_rows",
        [shape((16, last.shape[-1]), F32)],
        1_000_000,
        ones[0],
        twos[0],
        ones[1],
        twos[1],
        last,
    )[0]


def pack_all_kernel(rows_ref, qv0, qv1, up0, up1, rel0, rel1, out_ref):
    local = qv0.shape[-1]
    out_ref[:16, :] = rows_ref[...]
    out_ref[16:, :] = jnp.zeros((32, out_ref.shape[1]), F32)
    for layer, (qv_ref, up_ref, rel_ref) in enumerate(((qv0, up0, rel0), (qv1, up1, rel1))):
        out_ref[16 + layer : 17 + layer, :] = row_sum(up_ref[...])
        for i in range(2):
            out_ref[18 + 2 * layer + i : 19 + 2 * layer + i, :local] = row_sum(qv_ref[i])
        heads = rel_ref.shape[0] // 24
        for h in range(heads):
            start = (layer * heads + h) * 128
            out_ref[24:48, start : start + 32] = rel_ref[h * 24 : h * 24 + 24, :]


def pack_all(rows, qv_sums, up_sums, rel_sums):
    return kernel_call(
        pack_all_kernel,
        "pack_all",
        [shape((48, rows.shape[-1]), F32)],
        1_000_000,
        rows,
        *qv_sums,
        *up_sums,
        *rel_sums,
    )[0]


def unpack_kernel(all_ref, *out_refs):
    rows, mask_ref, up_ref, qv_ref, rel_ref = out_refs[:6], *out_refs[6:]
    for i, row_ref in enumerate(rows):
        row_ref[...] = all_ref[2 * i : 2 * i + 2, :]
    mask_ref[...] = all_ref[12:13, :]
    up_ref[...] = all_ref[16:18, :]
    heads, layers, entries = rel_ref.shape
    local = qv_ref.shape[-1]
    for layer in range(layers):
        qv_ref[layer] = all_ref[18 + 2 * layer : 20 + 2 * layer, :local]
        for h in range(heads):
            start = (layer * heads + h) * 128
            for j in range(6):
                lines = [all_ref[24 + 4 * j + r : 25 + 4 * j + r, start : start + 32] for r in range(4)]
                size = min(128, entries - 128 * j)
                line = jnp.concatenate(lines, axis=1)[:, :size]
                rel_ref[h, layer : layer + 1, 128 * j : 128 * j + size] = line


def unpack(values, heads, entries):
    width = values.shape[-1]
    outs = [shape((LAYERS, width), F32)] * 6 + [shape((1, width), F32), shape((LAYERS, width), F32)]
    outs += [shape((LAYERS, 2, heads * HEAD_DIM), F32), shape((heads, LAYERS, entries), F32)]
    return kernel_call(unpack_kernel, "unpack", outs, 1_000_000, values)


def assemble_kernel(layer, pieces, own_ref, got_ref, place_ref, *refs):
    out_refs, (stage_ref, sems) = refs[-2 - len(pieces) : -2], refs[-2:]
    half = own_ref.shape[0]
    mine = place_ref[0] & 1
    stage_ref[pl.ds(pl.multiple_of(mine * half, half), half), :] = own_ref[...].astype(F32)
    stage_ref[pl.ds(pl.multiple_of((1 - mine) * half, half), half), :] = got_ref[...].astype(F32)
    copies = []
    for out_ref, parts in zip(out_refs, pieces):
        for index, start, rows in parts:
            target = out_ref.at[(layer,) + index]
            source = stage_ref.at[pl.ds(start, rows), :]
            copies.append(pltpu.make_async_copy(source, target, sems.at[len(copies)]))
    for copy in copies:
        copy.start()
    for copy in copies:
        copy.wait()


def assemble(layer, name, pieces, outs, own, got, place, before):
    rows, width = own.shape
    anywhere = pl.BlockSpec(memory_space=pl.ANY)
    count = sum(len(parts) for parts in pieces)
    return pl.pallas_call(
        functools.partial(assemble_kernel, layer, pieces),
        out_shape=tuple(outs),
        in_specs=[VMEM, VMEM, pl.BlockSpec(memory_space=pltpu.SMEM)] + [anywhere] * len(before),
        out_specs=tuple([anywhere] * len(outs)),
        scratch_shapes=[pltpu.VMEM((2 * rows, width), F32), pltpu.SemaphoreType.DMA((count,))],
        input_output_aliases={3 + i: i for i in range(len(before))},
        name=name,
        compiler_params=pltpu.CompilerParams(vmem_limit_bytes=VMEM_GRANT),
        cost_estimate=pl.CostEstimate(flops=1_000_000, bytes_accessed=rows * width, transcendentals=0),
    )(own, got, place, *before)


def assemble_feed(layer, part, parts, sums, place, before=()):
    own, got = sums.ended()
    size, width = own.shape
    pieces = [[((pl.ds(part * size, size),), 0, size)], [((pl.ds(part * size, size),), size, size)]]
    outs = [shape((LAYERS, parts * size, width), F32)] * 2
    return assemble(layer, "assemble_feed", pieces, outs, own, got, place, before)


def assemble_attention(layer, sums, place, before=()):
    own, got = sums.ended()
    local, width = own.shape[0] // 2, own.shape[1]
    pieces = [[((), 0, local)], [((t,), (t + 1) * local, local) for t in range(3)]]
    outs = [shape((LAYERS, local, width), F32), shape((LAYERS, 3, local, width), F32)]
    return assemble(layer, "assemble_attention", pieces, outs, own, got, place, before)


def shards(
    n_dp,
    patch_rows,
    cotangent,
    mask_flags,
    pad_flags,
    buckets,
    mask_emb,
    ln1_gain,
    ln1_bias,
    w_qkv,
    qv_bias,
    rel_table,
    w_out,
    out_bias,
    ln2_gain,
    ln2_bias,
    w_up,
    up_bias,
    w_down,
    down_bias,
):
    member = lax.axis_index("tensor").reshape(1).astype(jnp.int32)
    place = lax.axis_index("dp").reshape(1).astype(jnp.int32)
    bits = list(range(n_dp.bit_length() - 1))
    pages = patch_rows.shape[1]
    heads, entries = rel_table.shape[1:]
    last = LAYERS - 1
    masked = mask_flags.T
    w_qkv = jnp.swapaxes(w_qkv, 2, 3)

    hidden, own, last_own, last_sum = first_norm(
        patch_rows, cotangent, masked, mask_emb.reshape(1, -1), ln1_gain, ln1_bias
    )
    rel_bias, ordered, pad_bias = bias_of_buckets(jnp.swapaxes(rel_table, 0, 1), buckets, pad_flags.T, member)
    blocks = spread(own, (rel_bias,))
    last_blocks = spread(tied(last_own, blocks[3]))

    kept = []
    for layer in range(LAYERS):
        rows_one, before = blocks, hidden
        partial, saved = attention(layer, rows_one, w_qkv, qv_bias, rel_bias, pad_bias, w_out)
        near, far, unused = collect(partial)
        middle, own = add_norm(hidden, near + [far], (layer, layer), out_bias, ln2_gain, ln2_bias)
        rows_two = spread(own)
        if layer == last:
            partial, (z, gu, up_sums) = feed_both(layer, rows_two, last_blocks, w_up, up_bias, w_down)
            kept.append((rows_one, before, saved, middle, rows_two, z, gu))
        else:
            partial, (z, slope) = feed_forward(layer, rows_two, w_up, up_bias, w_down)
            kept.append((rows_one, before, saved, middle, rows_two, z, slope))
            near, far, unused = collect(partial)
            hidden, own = add_norm(middle, near + [far], (layer, layer + 1), down_bias, ln1_gain, ln1_bias)
            blocks = spread(own)

    rows_one, before, saved, middle, rows_two, z, gu = kept[last]
    near, far, sent = collect(partial)
    mlp = feed_grads(rows_two, last_blocks, tied(z, sent), gu, place, 1)
    mlp1 = PageSum(mlp[0], bits, place)
    far = tied(far, mlp)
    g1, low, twos1 = norm_back(last_own, near + [far], middle, last, ln2_gain)
    result_parts = down_product(last, tied(z, low), w_down)
    out_blocks = spread(low, result_parts)
    partial, (stack, totals, qv1) = attention_back(last, out_blocks, saved, w_qkv, w_out)
    near, far, sent = collect(partial)
    mix = attention_grads(rows_one, out_blocks, tied(stack, sent), saved[-1], place)
    mix1 = PageSum(mix, bits, place)
    far = tied(far, mlp1.step(mix))
    grad, low, ones1 = norm_back(g1, near + [far], before, last, ln1_gain)
    rel1 = sum_by_bucket(tied(totals, low), ordered)
    token = mlp1.step(rel1)
    grad_blocks = spread(low, (token,))
    up1 = up_sums

    rows_one, before, saved, middle, rows_two, z, slope = kept[0]
    partial, (gu, up0) = feed_back(0, grad_blocks, slope, w_up, w_down)
    near, far, sent = collect(partial)
    mlp = feed_grads(rows_two, grad_blocks, tied(z, sent), gu, place, 2)
    mlp0a = PageSum(mlp[0], bits, place)
    token = mix1.step(mlp)
    token = mlp1.step(token)
    far = tied(far, token)
    g1, low, twos0 = norm_back(grad, near + [far], middle, 0, ln2_gain)
    token = mix1.step(low)
    token = mlp1.step(token)
    token = mlp0a.step(token)
    mlp0b = PageSum([mlp[1][0], tied(mlp[1][1], token)], bits, place)
    out_blocks = spread(low, (token,))
    result_near, result_far, unused = collect([tied(p, out_blocks[3]) for p in result_parts])
    partial, (stack, totals, qv0) = attention_back(0, out_blocks, saved, w_qkv, w_out)
    near, far, sent = collect(partial)
    mix = attention_grads(rows_one, out_blocks, tied(stack, sent), saved[-1], place)
    mix0 = PageSum(mix, bits, place)
    token = mlp0a.step(mix)
    token = mlp0b.step(token)
    token = mix1.step(token)
    token = mlp1.step(token)
    far = tied(far, token)
    grad, ones0 = last_norm_back(g1, near + [far], before, ln1_gain, masked)

    rows = pack_rows((ones0, ones1), (twos0, twos1), last_sum)
    rows = rows + swap_core(rows)
    rel0 = sum_by_bucket(tied(totals, rows), ordered)
    token = mlp0a.step(rel0)
    token = mix0.step(token)
    token = mlp0b.step(token)
    rows = rows + swap_chip(tied(rows, rel0))
    small = pack_all(tied(rows, token), (qv0, qv1), (up0, up1), (rel0, rel1))
    small_got = lax.ppermute(small, "dp", partners(bits, 0))
    token = mix1.step(small)
    result = last_result(kept[last][3], result_near + [tied(result_far, token)], last, down_bias, pages)
    token = mlp0a.step((token, result))
    token = mix0.step(token)
    token = mlp0b.step(token)
    token = mix1.step(token)
    small = small + tied(small_got, token)
    small_got = lax.ppermute(small, "dp", partners(bits, bits[1])) if len(bits) > 1 else 0.0
    token = mlp0a.step((token, small))
    d_mlp = assemble_feed(last, 0, 1, mlp1, tied(place, token))
    token = mix0.step((token, d_mlp))
    token = mlp0b.step(token)
    small = sum_small(small + tied(small_got, token), "dp", bits[2:], len(bits))
    d_mix = assemble_attention(last, mix1, tied(place, token))
    token = mix0.step((token, d_mix))
    token = mlp0b.step(token)
    d_mlp = assemble_feed(0, 0, 2, mlp0a, tied(place, token), d_mlp)
    token = mix0.step((token, d_mlp))
    d_mlp = assemble_feed(0, 1, 2, mlp0b, tied(place, token), d_mlp)
    d_mix = assemble_attention(0, mix0, tied(place, token), d_mix)
    small = unpack(small, heads, entries)
    d_ln1_gain, d_ln1_bias, d_out_bias, d_ln2_gain, d_ln2_bias, d_down_bias, d_mask, d_up_bias, d_qv, d_rel = small
    return (
        result,
        grad,
        d_mask.reshape(-1),
        d_ln1_gain,
        d_ln1_bias,
        jnp.swapaxes(d_mix[1], 2, 3),
        d_qv,
        jnp.swapaxes(d_rel, 0, 1),
        d_mix[0],
        d_out_bias,
        d_ln2_gain,
        d_ln2_bias,
        d_mlp[1],
        d_up_bias,
        d_mlp[0],
        d_down_bias,
    )


def solution(mesh):
    rows = P("tensor", "dp", None)
    units = P(None, "tensor", None)
    columns = P(None, None, "tensor")
    whole = P()
    return jax.shard_map(
        functools.partial(shards, mesh.shape["dp"]),
        mesh=mesh,
        in_specs=(
            rows,
            rows,
            P("tensor", "dp"),
            P(None, "dp"),
            whole,
            whole,
            whole,
            whole,
            P(None, None, None, "tensor"),
            columns,
            units,
            units,
            whole,
            whole,
            whole,
            columns,
            P(None, "tensor"),
            units,
            whole,
        ),
        out_specs=(
            rows,
            rows,
            whole,
            whole,
            whole,
            P(None, None, None, "tensor"),
            columns,
            units,
            units,
            whole,
            whole,
            whole,
            columns,
            P(None, "tensor"),
            units,
            whole,
        ),
        check_vma=False,
    )
```

time: 508 us -> 389 us (0.77)
  other arithmetic: 77.9 us -> 2.44 us
  matrix products: 65.7 us -> 0 us
  Pallas kernels: 25 us -> 90.1 us
  waiting for transfers between devices: 229 us -> 195 us
  local copies, waits for them, and re-layouts: 45.1 us -> 28.1 us
  starting transfers between devices: 56 us -> 67.5 us
    dot_general x36 -> x0, matrix products: 65.7 us -> none  [dot(): return jnp.einsum(form, left, right, preferred_element_type=F32)]
    pallas_call x3 -> x52, Pallas kernels: 25 us -> 90.1 us  [the longest x43 63.5 us: kernel_call(): pl.pallas_call(body, out_shape=tuple(outs), in_specs=specs, out_specs=tup...]
    ppermute x16 -> x17, waiting for transfers between devices: 104 us -> 74.1 us  [swap_chip(): return lax.ppermute(values, 'tensor', CHIP)]
    reduce_sum x21 -> x0, other arithmetic: 18 us -> none  [the longest x2 3.79 us: attention_back(): totals = jnp.sum(gs.astype(F32), axis=0)]
    ppermute x29 -> x33, waiting for transfers between devices: 120 us -> 102 us  [the longest x30 76.4 us: swap(): return lax.ppermute(values, 'dp', partners(self.bits, bit))]
    another operation x15 -> x0, other arithmetic: 15.2 us -> none  [the longest x3 4.76 us: shards(): jnp.stack([large[i][0][:width].astype(F32) for i in range(LAYERS)])]
    convert_element_type x16 -> x0, other arithmetic: 14.3 us -> none  [the longest x4 4.09 us: norm_rows(): return (normal * gain + shift).astype(BF)]
    ppermute x32 -> x33, waiting for transfers between devices: 4.78 us -> 18.6 us  [swap_core(): return lax.ppermute(values, 'tensor', CORE)]
  transfers between devices with their start and end apart: 77 -> 83, of which waited for: 31 -> 43; matrix products, arithmetic and copies ran while one was open for 29% -> 0% of each run, Pallas kernels for 5% -> 16%
where the time goes in v2:
time: 389 us; the launch traced here: 385 us
  waiting for transfers between devices  195 us (50%)
  Pallas kernels  90.1 us (23%)
  starting transfers between devices  67.5 us (17%)
  local copies, waits for them, and re-layouts  28.1 us (7%)
    ppermute x30, waiting for transfers between devices, swap(): return lax.ppermute(values, 'dp', partners(self.bits, bit))  76.4 us
    ppermute x17, waiting for transfers between devices, swap_chip(): return lax.ppermute(values, 'tensor', CHIP)  74.1 us
    pallas_call x43, Pallas kernels, kernel_call(): pl.pallas_call(body, out_shape=tuple(outs), in_specs=specs, out_specs=tup...  63.5 us
    ppermute x30, starting transfers between devices, swap(): return lax.ppermute(values, 'dp', partners(self.bits, bit))  41.1 us
    unnamed x210, local copies, waits for them, and re-layouts  27.4 us
    ppermute x17, starting transfers between devices, swap_chip(): return lax.ppermute(values, 'tensor', CHIP)  22.4 us
    ppermute x33, waiting for transfers between devices, swap_core(): return lax.ppermute(values, 'tensor', CORE)  18.6 us
    pallas_call x4, Pallas kernels, fetching_call(): pl.pallas_call(body, out_shape=tuple(outs), in_specs=[pl.BlockSpec(memory...  17.8 us
  transfers between devices with their start and end apart: 83, of which 43 were waited for; matrix products, arithmetic and copies ran while one was open for 0% of the time, Pallas kernels for 16%

profile of v2, /device:TPU:0, one launch (start us, length us, event | category | flops | bytes accessed | tf_op | source)
XLA Modules:
  0.0 385.5 jit_solution(6048083428669864624)
XLA Ops:
  5.4 2.0 first_norm.1
  8.2 3.0 collective-permute-start.1
  13.5 5.1 %bias_of_buckets.1 = (bf16[2,3,256,256]{3,2,1,0:T(8,128)(2,1)S(1)}, s32[256,256]{1,0:T(8,128)S(1)}, f32[4,1,256]{2,1,0:T(1,128)S(1)}) custom-call(bf16[3,2,732]{2,1,0:T(2,128)(2,1)S(1)} %bitcast.12, s32[256,256]{1,0:T(8,128)S(1)} %copy-done.89, s32[4,256]{1,0:T(4,128)S(1)} %bitcast.15, s32[1]{0:T(128)} %bitcast.3.member_ref), custom_call_target="tpu_custom_call" | custom-call | flops 40000000 | bytes 13277 | tf_op jit(solution)/shard_map/bias_of_buckets/pallas_call | solution.py:42
  20.3 1.7 collective-permute-done.2.x3.refs_3_
  25.4 5.1 %attention.2 = (bf16[256,768]{1,0:T(8,128)(2,1)S(1)}, bf16[256,768]{1,0:T(8,128)(2,1)S(1)}, bf16[256,768]{1,0:T(8,128)(2,1)S(1)}, bf16[256,768]{1,0:T(8,128)(2,1...) custom-call(bf16[256,768]{1,0:T(8,128)(2,1)S(1)} %get-tuple-element., ...), custom_call_target="tpu_custom_call" | custom-call | flops 60000000 | bytes 94428 | tf_op jit(solution)/shard_map/attention/pallas_call | solution.py:42
  33.2 1.8 collective-permute-start.5
  35.1 9.4 %collective-permute-done.5.three_ref = bf16[256,768]{1,0:T(8,128)(2,1)S(1)} collective-permute-done((bf16[256,768]{1,0:T(8,128)(2,1)S(1)}, bf16[256,768]{1,0:T(8,128)(2,1)S(1)}, u32[]{:S(2)}, u32[]{:S(2)}) %collective-permute-start.5) | collective-permute-done | bytes 393248 | tf_op jit(solution)/shard_map/ppermute | solution.py:63
  45.0 1.8 collective-permute-start.7
  46.8 8.6 %collective-permute-done.7.c2.refs_2_ = bf16[256,768]{1,0:T(8,128)(2,1)S(1)} collective-permute-done((bf16[256,768]{1,0:T(8,128)(2,1)S(1)}, bf16[256,768]{1,0:T(8,128)(2,1)S(1)}, u32[]{:S(2)}, u32[]{:S(2)}) %collective-permute-start.7) | collective-permute-done | bytes 393248 | tf_op jit(solution)/shard_map/ppermute | solution.py:63
  55.5 1.7 collective-permute-done.8.c3.refs_3_
  57.2 3.7 feed_forward.1
  63.9 1.8 collective-permute-start.11
  65.7 9.4 %collective-permute-done.11.three_ref = bf16[256,768]{1,0:T(8,128)(2,1)S(1)} collective-permute-done((bf16[256,768]{1,0:T(8,128)(2,1)S(1)}, bf16[256,768]{1,0:T(8,128)(2,1)S(1)}, u32[]{:S(2)}, u32[]{:S(2)}) %collective-permute-start.11) | collective-permute-done | bytes 393248 | tf_op jit(solution)/shard_map/ppermute | solution.py:63
  75.6 1.8 collective-permute-start.13
  77.4 8.6 %collective-permute-done.13.x2.refs_2_ = bf16[256,768]{1,0:T(8,128)(2,1)S(1)} collective-permute-done((bf16[256,768]{1,0:T(8,128)(2,1)S(1)}, bf16[256,768]{1,0:T(8,128)(2,1)S(1)}, u32[]{:S(2)}, u32[]{:S(2)}) %collective-permute-start.13) | collective-permute-done | bytes 393248 | tf_op jit(solution)/shard_map/ppermute | solution.py:63
  86.0 1.7 collective-permute-done.14.x3.refs_3_
  87.7 5.6 %attention.3 = (bf16[256,768]{1,0:T(8,128)(2,1)S(1)}, bf16[256,768]{1,0:T(8,128)(2,1)S(1)}, bf16[256,768]{1,0:T(8,128)(2,1)S(1)}, bf16[256,768]{1,0:T(8,128)(2,1...) custom-call(bf16[256,768]{1,0:T(8,128)(2,1)S(1)} %get-tuple-element., ...), custom_call_target="tpu_custom_call" | custom-call | flops 60000000 | bytes 94428 | tf_op jit(solution)/shard_map/attention/pallas_call | solution.py:42
  96.1 1.8 collective-permute-start.17
  98.2 9.9 %collective-permute-done.17.three_ref = bf16[256,768]{1,0:T(8,128)(2,1)S(1)} collective-permute-done((bf16[256,768]{1,0:T(8,128)(2,1)S(1)}, bf16[256,768]{1,0:T(8,128)(2,1)S(1)}, u32[]{:S(2)}, u32[]{:S(2)}) %collective-permute-start.17) | collective-permute-done | bytes 393248 | tf_op jit(solution)/shard_map/ppermute | solution.py:63
  109.5 1.7 collective-permute-start.19
  111.2 5.3 %collective-permute-done.22.g2.refs_6_ = bf16[256,768]{1,0:T(8,128)(2,1)S(1)} collective-permute-done((bf16[256,768]{1,0:T(8,128)(2,1)S(1)}, bf16[256,768]{1,0:T(8,128)(2,1)S(1)}, u32[]{:S(2)}, u32[]{:S(2)}) %collective-permute-start.22) | collective-permute-done | bytes 393248 | tf_op jit(solution)/shard_map/ppermute | solution.py:63
  117.1 7.1 %collective-permute-done.19.c2.refs_2_ = bf16[256,768]{1,0:T(8,128)(2,1)S(1)} collective-permute-done((bf16[256,768]{1,0:T(8,128)(2,1)S(1)}, bf16[256,768]{1,0:T(8,128)(2,1)S(1)}, u32[]{:S(2)}, u32[]{:S(2)}) %collective-permute-start.19) | collective-permute-done | bytes 393248 | tf_op jit(solution)/shard_map/ppermute | solution.py:63
  125.9 6.0 %feed_both.1 = (bf16[256,768]{1,0:T(8,128)(2,1)S(1)}, bf16[256,768]{1,0:T(8,128)(2,1)}, bf16[256,768]{1,0:T(8,128)(2,1)S(1)}, bf16[256,768]{1,0:T(8,128)(2,1)S(1...) custom-call(bf16[256,768]{1,0:T(8,128)(2,1)S(1)} %get-tuple-element.222.c0.refs_0_, ...), custom_call_target="tpu_custom_call" | custom-call | flops 60000000 | bytes 126105 | tf_op jit(solution)/shard_map/feed_both/pallas_call | solution.py:42
  137.6 1.7 collective-permute-start.26
  149.1 5.1 %feed_grads.2 = (bf16[768,768]{1,0:T(8,128)(2,1)S(1)}, bf16[768,768]{1,0:T(8,128)(2,1)S(1)}) custom-call(bf16[256,768]{1,0:T(8,128)(2,1)S(1)} %copy-done.22, bf16[256,768]{1,0:T(8,128)(2,1)S(1)} %copy-done.30, bf16[256,768]{1,0:T(8,128)(2,1)S(1)} %copy-done.24, bf16[256,768]{1,0:T(8,128)(2,1)S(1)} %copy-done.32, ...), custom_call_target="tpu_custom_call" | custom-call | flops 40000000 | bytes 62914 | tf_op jit(solution)/shard_map/feed_grads/pallas_call | solution.py:470
  154.3 1.9 norm_back.3
  159.7 8.2 %collective-permute-done.28.g2.refs_6_ = bf16[256,768]{1,0:T(8,128)(2,1)S(1)} collective-permute-done((bf16[256,768]{1,0:T(8,128)(2,1)S(1)}, bf16[256,768]{1,0:T(8,128)(2,1)S(1)}, u32[]{:S(2)}, u32[]{:S(2)}) %collective-permute-start.28) | collective-permute-done | bytes 393248 | tf_op jit(solution)/shard_map/ppermute | solution.py:63
  167.9 1.7 collective-permute-done.29.g3.refs_7_
  169.7 6.6 %attention_back.2 = (bf16[256,768]{1,0:T(8,128)(2,1)S(1)}, bf16[256,768]{1,0:T(8,128)(2,1)S(1)}, bf16[256,768]{1,0:T(8,128)(2,1)S(1)}, bf16[256,768]{1,0:T(8,128...) custom-call(bf16[256,768]{1,0:T(8,128)(2,1)S(1)} %get-tuple-element.235.g0.re, ...), custom_call_target="tpu_custom_call" | custom-call | flops 90000000 | bytes 102359 | tf_op jit(solution)/shard_map/attention_back/pallas_call | solution.py:42
  178.6 3.6 attention_grads.2
  182.2 2.6 collective-permute-done.33.got_ref
  185.1 1.8 collective-permute-start.36
  186.9 2.5 collective-permute-done.32.three_ref
  190.5 4.0 %sum_by_bucket.2.rel1 = f32[72,32]{1,0:T(8,128)S(1)} custom-call(f32[3,256,256]{2,1,0:T(8,128)S(1)} %get-tuple-element.263.values_ref, s32[256,256]{1,0:T(8,128)S(1)} %copy-done.68), custom_call_target="tpu_custom_call" | custom-call | flops 60000000 | bytes 10577 | tf_op jit(solution)/shard_map/sum_by_bucket/pallas_call | solution.py:42
  194.6 5.3 %collective-permute-done.36.got_ref = bf16[384,768]{1,0:T(8,128)(2,1)S(1)} collective-permute-done((bf16[384,768]{1,0:T(8,128)(2,1)S(1)}, bf16[384,768]{1,0:T(8,128)(2,1)S(1)}, u32[]{:S(2)}, u32[]{:S(2)}) %collective-permute-start.36) | collective-permute-done | bytes 589856 | tf_op jit(solution)/shard_map/ppermute | solution.py:730
  200.6 1.7 collective-permute-done.37.g3.refs_7_
  202.3 2.9 feed_back.1
  208.3 2.6 collective-permute-start.41
  210.9 5.4 %feed_grads.3 = (bf16[384,768]{1,0:T(8,128)(2,1)S(1)}, bf16[384,768]{1,0:T(8,128)(2,1)S(1)}, bf16[384,768]{1,0:T(8,128)(2,1)S(1)}, bf16[384,768]{1,0:T(8,128)(2,1)S(1)}) custom-call(bf16[256,768]{1,0:T(8,128)(2,1)S(1)} %copy-done.38, bf16[256,768]{1,0:T(8,128)(2,1)S(1)} %copy-done.42, bf16[256,768]{1,0:T(8,128)(2,1)S(1)} %copy-done.40, ...), custom_call_target="tpu_custom_call" | custom-call | flops 40000000 | bytes 62914 | tf_op jit(solution)/shard_map/feed_grads/pallas_call | solution.py:470
  217.8 3.8 collective-permute-done.42.got_ref
  221.7 3.2 collective-permute-done.41
  227.5 3.4 collective-permute-start.45
  230.8 10.4 %collective-permute-done.46.got_ref = bf16[192,768]{1,0:T(8,128)(2,1)S(1)} collective-permute-done((bf16[192,768]{1,0:T(8,128)(2,1)S(1)}, bf16[192,768]{1,0:T(8,128)(2,1)S(1)}, u32[]{:S(2)}, u32[]{:S(2)}) %collective-permute-start.46) | collective-permute-done | bytes 294944 | tf_op jit(solution)/shard_map/ppermute | solution.py:730
  241.3 2.6 collective-permute-done.45.got_ref
  246.0 6.4 %attention_back.3 = (bf16[256,768]{1,0:T(8,128)(2,1)S(1)}, bf16[256,768]{1,0:T(8,128)(2,1)S(1)}, bf16[256,768]{1,0:T(8,128)(2,1)S(1)}, bf16[256,768]{1,0:T(8,128...) custom-call(bf16[256,768]{1,0:T(8,128)(2,1)S(1)} %get-tuple-element.285.g0.re, ...), custom_call_target="tpu_custom_call" | custom-call | flops 90000000 | bytes 102359 | tf_op jit(solution)/shard_map/attention_back/pallas_call | solution.py:42
  253.0 1.7 collective-permute-start.59
  256.9 18.7 %collective-permute-done.51 = bf16[96,768]{1,0:T(8,128)(2,1)S(1)} collective-permute-done((bf16[96,768]{1,0:T(8,128)(2,1)S(1)}, bf16[96,768]{1,0:T(8,128)(2,1)S(1)}, u32[]{:S(2)}, u32[]{:S(2)}) %collective-permute-start.51) | collective-permute-done | bytes 147488 | tf_op jit(solution)/shard_map/ppermute | solution.py:730
  275.6 3.6 attention_grads.3
  282.0 3.4 collective-permute-start.64
  285.4 1.9 last_norm_back.1
  289.0 4.3 %sum_by_bucket.3.rel0 = f32[72,32]{1,0:T(8,128)S(1)} custom-call(f32[3,256,256]{2,1,0:T(8,128)S(1)} %get-tuple-element.327.values_ref, s32[256,256]{1,0:T(8,128)S(1)} %copy-done.68), custom_call_target="tpu_custom_call" | custom-call | flops 60000000 | bytes 10577 | tf_op jit(solution)/shard_map/sum_by_bucket/pallas_call | solution.py:42
  294.5 2.9 collective-permute-done.61
  298.5 2.6 collective-permute-start.56
  301.5 5.5 %collective-permute-done.56.got_ref = bf16[96,768]{1,0:T(8,128)(2,1)S(1)} collective-permute-done((bf16[96,768]{1,0:T(8,128)(2,1)S(1)}, bf16[96,768]{1,0:T(8,128)(2,1)S(1)}, u32[]{:S(2)}, u32[]{:S(2)}) %collective-permute-start.56) | collective-permute-done | bytes 147488 | tf_op jit(solution)/shard_map/ppermute | solution.py:730
  312.3 8.3 %collective-permute-done.69.got_ref = bf16[96,768]{1,0:T(8,128)(2,1)S(1)} collective-permute-done((bf16[96,768]{1,0:T(8,128)(2,1)S(1)}, bf16[96,768]{1,0:T(8,128)(2,1)S(1)}, u32[]{:S(2)}, u32[]{:S(2)}) %collective-permute-start.69) | collective-permute-done | bytes 147488 | tf_op jit(solution)/shard_map/ppermute | solution.py:730
  327.9 12.6 %collective-permute-done.65 = f32[48,768]{1,0:T(8,128)S(1)} collective-permute-done((f32[48,768]{1,0:T(8,128)S(1)}, f32[48,768]{1,0:T(8,128)S(1)}, u32[]{:S(2)}, u32[]{:S(2)}) %collective-permute-start.65) | collective-permute-done | bytes 147488 | tf_op jit(solution)/shard_map/ppermute | solution.py:1002
  342.0 1.9 collective-permute-start.71
  343.8 2.5 assemble_feed.3
  347.5 6.4 %collective-permute-done.71.got_ref = bf16[96,768]{1,0:T(8,128)(2,1)S(1)} collective-permute-done((bf16[96,768]{1,0:T(8,128)(2,1)S(1)}, bf16[96,768]{1,0:T(8,128)(2,1)S(1)}, u32[]{:S(2)}, u32[]{:S(2)}) %collective-permute-start.71) | collective-permute-done | bytes 147488 | tf_op jit(solution)/shard_map/ppermute | solution.py:730
  355.6 2.1 collective-permute-start.78
  357.7 4.8 %collective-permute-done.79.got_ref = bf16[192,768]{1,0:T(8,128)(2,1)S(1)} collective-permute-done((bf16[192,768]{1,0:T(8,128)(2,1)S(1)}, bf16[192,768]{1,0:T(8,128)(2,1)S(1)}, u32[]{:S(2)}, u32[]{:S(2)}) %collective-permute-start.79) | collective-permute-done | bytes 294944 | tf_op jit(solution)/shard_map/ppermute | solution.py:730
  364.8 2.3 collective-permute-done.78.got_ref
  367.3 5.7 %collective-permute-done.70 = f32[48,768]{1,0:T(8,128)S(1)} collective-permute-done((f32[48,768]{1,0:T(8,128)S(1)}, f32[48,768]{1,0:T(8,128)S(1)}, u32[]{:S(2)}, u32[]{:S(2)}) %collective-permute-start.70) | collective-permute-done | bytes 147488 | tf_op jit(solution)/shard_map/ppermute | solution.py:1010
  373.1 7.5 %collective-permute-done.75 = f32[48,768]{1,0:T(8,128)S(1)} collective-permute-done((f32[48,768]{1,0:T(8,128)S(1)}, f32[48,768]{1,0:T(8,128)S(1)}, u32[]{:S(2)}, u32[]{:S(2)}) %collective-permute-start.75) | collective-permute-done | bytes 147488 | tf_op jit(solution)/shard_map/ppermute | solution.py:758
  (384 shorter events, 92.7 us)
Async XLA Ops:
  8.2 12.1 %collective-permute-start.1 = (bf16[256,768]{1,0:T(8,128)(2,1)S(1)}, bf16[256,768]{1,0:T(8,128)(2,1)S(1)}, u32[]{:S(2)}, u32[]{:S(2)}) collective-permute-start(bf16[256,768]{1,0:T(8,128)(2,1)S(1)} %get-tuple-element.201.x0.refs_0_), channel_id=1, source_target_pairs={{0,2},{1,3},{2,0},{3,1},{4,6},{5,7},{6,4},{7,5},{8,10},{9,11},{10,... | collective-permute-start | bytes 1179656 | tf_op jit(solution)/shard_map/ppermute | solution.py:63
  11.2 9.1 %collective-permute-start = (bf16[256,768]{1,0:T(8,128)(2,1)S(1)}, bf16[256,768]{1,0:T(8,128)(2,1)S(1)}, u32[]{:S(2)}, u32[]{:S(2)}) collective-permute-start(bf16[256,768]{1,0:T(8,128)(2,1)S(1)} %get-tuple-element.201.x0.refs_0_), channel_id=1, source_target_pairs={{0,1},{1,0},{2,3},{3,2},{4,5},{5,4},{6,7},{7,6},{8,9},{9,8},{10,11... | collective-permute-start | bytes 1179656 | tf_op jit(solution)/shard_map/ppermute | solution.py:59
  33.2 11.2 %collective-permute-start.5 = (bf16[256,768]{1,0:T(8,128)(2,1)S(1)}, bf16[256,768]{1,0:T(8,128)(2,1)S(1)}, u32[]{:S(2)}, u32[]{:S(2)}) collective-permute-start(bf16[256,768]{1,0:T(8,128)(2,1)S(1)} %add.54), channel_id=1, source_target_pairs={{0,2},{1,3},{2,0},{3,1},{4,6},{5,7},{6,4},{7,5},{8,10},{9,11},{10,... | collective-permute-start | bytes 1179656 | tf_op jit(solution)/shard_map/ppermute | solution.py:63
  45.0 10.4 %collective-permute-start.7 = (bf16[256,768]{1,0:T(8,128)(2,1)S(1)}, bf16[256,768]{1,0:T(8,128)(2,1)S(1)}, u32[]{:S(2)}, u32[]{:S(2)}) collective-permute-start(bf16[256,768]{1,0:T(8,128)(2,1)S(1)} %get-tuple-element.210.c0.refs_0_), channel_id=1, source_target_pairs={{0,2},{1,3},{2,0},{3,1},{4,6},{5,7},{6,4},{7,5},{8,10},{9,11},{10,... | collective-permute-start | bytes 1179656 | tf_op jit(solution)/shard_map/ppermute | solution.py:63
  46.8 8.6 %collective-permute-start.6 = (bf16[256,768]{1,0:T(8,128)(2,1)S(1)}, bf16[256,768]{1,0:T(8,128)(2,1)S(1)}, u32[]{:S(2)}, u32[]{:S(2)}) collective-permute-start(bf16[256,768]{1,0:T(8,128)(2,1)S(1)} %get-tuple-element.210.c0.refs_0_), channel_id=1, source_target_pairs={{0,1},{1,0},{2,3},{3,2},{4,5},{5,4},{6,7},{7,6},{8,9},{9,8},{10,11... | collective-permute-start | bytes 1179656 | tf_op jit(solution)/shard_map/ppermute | solution.py:59
  63.9 11.2 %collective-permute-start.11 = (bf16[256,768]{1,0:T(8,128)(2,1)S(1)}, bf16[256,768]{1,0:T(8,128)(2,1)S(1)}, u32[]{:S(2)}, u32[]{:S(2)}) collective-permute-start(bf16[256,768]{1,0:T(8,128)(2,1)S(1)} %add.55), channel_id=1, source_target_pairs={{0,2},{1,3},{2,0},{3,1},{4,6},{5,7},{6,4},{7,5},{8,10},{9,11},{10,... | collective-permute-start | bytes 1179656 | tf_op jit(solution)/shard_map/ppermute | solution.py:63
  75.6 10.4 %collective-permute-start.13 = (bf16[256,768]{1,0:T(8,128)(2,1)S(1)}, bf16[256,768]{1,0:T(8,128)(2,1)S(1)}, u32[]{:S(2)}, u32[]{:S(2)}) collective-permute-start(bf16[256,768]{1,0:T(8,128)(2,1)S(1)} %get-tuple-element.216.x0.refs_0_), channel_id=1, source_target_pairs={{0,2},{1,3},{2,0},{3,1},{4,6},{5,7},{6,4},{7,5},{8,10},{9,11},{10,... | collective-permute-start | bytes 1179656 | tf_op jit(solution)/shard_map/ppermute | solution.py:63
  77.4 8.6 %collective-permute-start.12 = (bf16[256,768]{1,0:T(8,128)(2,1)S(1)}, bf16[256,768]{1,0:T(8,128)(2,1)S(1)}, u32[]{:S(2)}, u32[]{:S(2)}) collective-permute-start(bf16[256,768]{1,0:T(8,128)(2,1)S(1)} %get-tuple-element.216.x0.refs_0_), channel_id=1, source_target_pairs={{0,1},{1,0},{2,3},{3,2},{4,5},{5,4},{6,7},{7,6},{8,9},{9,8},{10,11... | collective-permute-start | bytes 1179656 | tf_op jit(solution)/shard_map/ppermute | solution.py:59
  96.1 12.0 %collective-permute-start.17 = (bf16[256,768]{1,0:T(8,128)(2,1)S(1)}, bf16[256,768]{1,0:T(8,128)(2,1)S(1)}, u32[]{:S(2)}, u32[]{:S(2)}) collective-permute-start(bf16[256,768]{1,0:T(8,128)(2,1)S(1)} %add.56), channel_id=1, source_target_pairs={{0,2},{1,3},{2,0},{3,1},{4,6},{5,7},{6,4},{7,5},{8,10},{9,11},{10,... | collective-permute-start | bytes 1179656 | tf_op jit(solution)/shard_map/ppermute | solution.py:63
  97.9 18.7 %collective-permute-start.22 = (bf16[256,768]{1,0:T(8,128)(2,1)S(1)}, bf16[256,768]{1,0:T(8,128)(2,1)S(1)}, u32[]{:S(2)}, u32[]{:S(2)}) collective-permute-start(bf16[256,768]{1,0:T(8,128)(2,1)S(1)} %get-tuple-element.224.g0.refs_4_.grad_ref), channel_id=1, source_target_pairs={{0,2},{1,3},{2,0},{3,1},{4,6},{5,7},{6,4},{7,5},{8,10},{9,11},{10,... | collective-permute-start | bytes 1179656 | tf_op jit(solution)/shard_map/ppermute | solution.py:63
  109.5 14.7 %collective-permute-start.19 = (bf16[256,768]{1,0:T(8,128)(2,1)S(1)}, bf16[256,768]{1,0:T(8,128)(2,1)S(1)}, u32[]{:S(2)}, u32[]{:S(2)}) collective-permute-start(bf16[256,768]{1,0:T(8,128)(2,1)S(1)} %get-tuple-element.222.c0.refs_0_), channel_id=1, source_target_pairs={{0,2},{1,3},{2,0},{3,1},{4,6},{5,7},{6,4},{7,5},{8,10},{9,11},{10,... | collective-permute-start | bytes 1179656 | tf_op jit(solution)/shard_map/ppermute | solution.py:63
  111.2 13.0 %collective-permute-start.21 = (bf16[256,768]{1,0:T(8,128)(2,1)S(1)}, bf16[256,768]{1,0:T(8,128)(2,1)S(1)}, u32[]{:S(2)}, u32[]{:S(2)}) collective-permute-start(bf16[256,768]{1,0:T(8,128)(2,1)S(1)} %get-tuple-element.224.g0.refs_4_.grad_ref), channel_id=1, source_target_pairs={{0,1},{1,0},{2,3},{3,2},{4,5},{5,4},{6,7},{7,6},{8,9},{9,8},{10,11... | collective-permute-start | bytes 1179656 | tf_op jit(solution)/shard_map/ppermute | solution.py:59
  116.6 7.6 %collective-permute-start.23 = (bf16[256,768]{1,0:T(8,128)(2,1)S(1)}, bf16[256,768]{1,0:T(8,128)(2,1)S(1)}, u32[]{:S(2)}, u32[]{:S(2)}) collective-permute-start(bf16[256,768]{1,0:T(8,128)(2,1)S(1)} %collective-permute-done.22.g2.refs_6_), channel_id=1, source_target_pairs={{0,1},{1,0},{2,3},{3,2},{4,5},{5,4},{6,7},{7,6},{8,9},{9,8},{10,11... | collective-permute-start | bytes 1179656 | tf_op jit(solution)/shard_map/ppermute | solution.py:59
  116.6 7.7 %collective-permute-start.18 = (bf16[256,768]{1,0:T(8,128)(2,1)S(1)}, bf16[256,768]{1,0:T(8,128)(2,1)S(1)}, u32[]{:S(2)}, u32[]{:S(2)}) collective-permute-start(bf16[256,768]{1,0:T(8,128)(2,1)S(1)} %get-tuple-element.222.c0.refs_0_), channel_id=1, source_target_pairs={{0,1},{1,0},{2,3},{3,2},{4,5},{5,4},{6,7},{7,6},{8,9},{9,8},{10,11... | collective-permute-start | bytes 1179656 | tf_op jit(solution)/shard_map/ppermute | solution.py:59
  137.6 16.7 %collective-permute-start.26 = (bf16[256,768]{1,0:T(8,128)(2,1)}, bf16[256,768]{1,0:T(8,128)(2,1)}, u32[]{:S(2)}, u32[]{:S(2)}) collective-permute-start(bf16[256,768]{1,0:T(8,128)(2,1)} %add.57), channel_id=1, source_target_pairs={{0,2},{1,3},{2,0},{3,1},{4,6},{5,7},{6,4},{7,5},{8,10},{9,11},{10,... | collective-permute-start | bytes 1179656 | tf_op jit(solution)/shard_map/ppermute | solution.py:63
  139.3 15.0 %collective-permute-start.24 = (bf16[256,768]{1,0:T(8,128)(2,1)}, bf16[256,768]{1,0:T(8,128)(2,1)}, u32[]{:S(2)}, u32[]{:S(2)}) collective-permute-start(bf16[256,768]{1,0:T(8,128)(2,1)} %get-tuple-element.227), channel_id=1, source_target_pairs={{0,1},{1,0},{2,3},{3,2},{4,5},{5,4},{6,7},{7,6},{8,9},{9,8},{10,11... | collective-permute-start | bytes 1179656 | tf_op jit(solution)/shard_map/ppermute | solution.py:59
  156.3 11.6 %collective-permute-start.28 = (bf16[256,768]{1,0:T(8,128)(2,1)S(1)}, bf16[256,768]{1,0:T(8,128)(2,1)S(1)}, u32[]{:S(2)}, u32[]{:S(2)}) collective-permute-start(bf16[256,768]{1,0:T(8,128)(2,1)S(1)} %get-tuple-element.235.g0.refs_4_), channel_id=1, source_target_pairs={{0,2},{1,3},{2,0},{3,1},{4,6},{5,7},{6,4},{7,5},{8,10},{9,11},{10,... | collective-permute-start | bytes 1179656 | tf_op jit(solution)/shard_map/ppermute | solution.py:63
  156.6 28.2 %collective-permute-start.33 = (bf16[768,768]{1,0:T(8,128)(2,1)S(1)}, bf16[768,768]{1,0:T(8,128)(2,1)S(1)}, u32[]{:S(2)}, u32[]{:S(2)}) collective-permute-start(bf16[768,768]{1,0:T(8,128)(2,1)S(1)} %get-tuple-element.233), channel_id=1, source_target_pairs={{0,4},{4,0},{8,12},{12,8},{16,20},{20,16},{24,28},{28,24},{1,5},{5... | collective-permute-start | bytes 3538952 | tf_op jit(solution)/shard_map/ppermute | solution.py:730
  158.3 9.6 %collective-permute-start.27 = (bf16[256,768]{1,0:T(8,128)(2,1)S(1)}, bf16[256,768]{1,0:T(8,128)(2,1)S(1)}, u32[]{:S(2)}, u32[]{:S(2)}) collective-permute-start(bf16[256,768]{1,0:T(8,128)(2,1)S(1)} %get-tuple-element.235.g0.refs_4_), channel_id=1, source_target_pairs={{0,1},{1,0},{2,3},{3,2},{4,5},{5,4},{6,7},{7,6},{8,9},{9,8},{10,11... | collective-permute-start | bytes 1179656 | tf_op jit(solution)/shard_map/ppermute | solution.py:59
  178.2 11.2 %collective-permute-start.32 = (bf16[256,768]{1,0:T(8,128)(2,1)S(1)}, bf16[256,768]{1,0:T(8,128)(2,1)S(1)}, u32[]{:S(2)}, u32[]{:S(2)}) collective-permute-start(bf16[256,768]{1,0:T(8,128)(2,1)S(1)} %add.58), channel_id=1, source_target_pairs={{0,2},{1,3},{2,0},{3,1},{4,6},{5,7},{6,4},{7,5},{8,10},{9,11},{10,... | collective-permute-start | bytes 1179656 | tf_op jit(solution)/shard_map/ppermute | solution.py:63
  178.5 10.9 %collective-permute-start.30 = (bf16[256,768]{1,0:T(8,128)(2,1)S(1)}, bf16[256,768]{1,0:T(8,128)(2,1)S(1)}, u32[]{:S(2)}, u32[]{:S(2)}) collective-permute-start(bf16[256,768]{1,0:T(8,128)(2,1)S(1)} %get-tuple-element.248), channel_id=1, source_target_pairs={{0,1},{1,0},{2,3},{3,2},{4,5},{5,4},{6,7},{7,6},{8,9},{9,8},{10,11... | collective-permute-start | bytes 1179656 | tf_op jit(solution)/shard_map/ppermute | solution.py:59
  185.1 14.8 %collective-permute-start.36 = (bf16[384,768]{1,0:T(8,128)(2,1)S(1)}, bf16[384,768]{1,0:T(8,128)(2,1)S(1)}, u32[]{:S(2)}, u32[]{:S(2)}) collective-permute-start(bf16[384,768]{1,0:T(8,128)(2,1)S(1)} %get-tuple-element.257), channel_id=1, source_target_pairs={{0,8},{4,12},{8,0},{12,4},{16,24},{20,28},{24,16},{28,20},{1,9},{5... | collective-permute-start | bytes 1769480 | tf_op jit(solution)/shard_map/ppermute | solution.py:730
  190.2 10.4 %collective-permute-start.35 = (bf16[256,768]{1,0:T(8,128)(2,1)S(1)}, bf16[256,768]{1,0:T(8,128)(2,1)S(1)}, u32[]{:S(2)}, u32[]{:S(2)}) collective-permute-start(bf16[256,768]{1,0:T(8,128)(2,1)S(1)} %get-tuple-element.260.g0.refs_4_), channel_id=1, source_target_pairs={{0,2},{1,3},{2,0},{3,1},{4,6},{5,7},{6,4},{7,5},{8,10},{9,11},{10,... | collective-permute-start | bytes 1179656 | tf_op jit(solution)/shard_map/ppermute | solution.py:63
  190.5 10.0 %collective-permute-start.34 = (bf16[256,768]{1,0:T(8,128)(2,1)S(1)}, bf16[256,768]{1,0:T(8,128)(2,1)S(1)}, u32[]{:S(2)}, u32[]{:S(2)}) collective-permute-start(bf16[256,768]{1,0:T(8,128)(2,1)S(1)} %get-tuple-element.260.g0.refs_4_), channel_id=1, source_target_pairs={{0,1},{1,0},{2,3},{3,2},{4,5},{5,4},{6,7},{7,6},{8,9},{9,8},{10,11... | collective-permute-start | bytes 1179656 | tf_op jit(solution)/shard_map/ppermute | solution.py:59
  205.4 16.2 %collective-permute-start.42 = (bf16[384,768]{1,0:T(8,128)(2,1)S(1)}, bf16[384,768]{1,0:T(8,128)(2,1)S(1)}, u32[]{:S(2)}, u32[]{:S(2)}) collective-permute-start(bf16[384,768]{1,0:T(8,128)(2,1)S(1)} %get-tuple-element.255), channel_id=1, source_target_pairs={{0,4},{4,0},{8,12},{12,8},{16,20},{20,16},{24,28},{28,24},{1,5},{5... | collective-permute-start | bytes 1769480 | tf_op jit(solution)/shard_map/ppermute | solution.py:730
  207.1 17.9 %collective-permute-start.40 = (bf16[256,768]{1,0:T(8,128)(2,1)S(1)}, bf16[256,768]{1,0:T(8,128)(2,1)S(1)}, u32[]{:S(2)}, u32[]{:S(2)}) collective-permute-start(bf16[256,768]{1,0:T(8,128)(2,1)S(1)} %add.59), channel_id=1, source_target_pairs={{0,2},{1,3},{2,0},{3,1},{4,6},{5,7},{6,4},{7,5},{8,10},{9,11},{10,... | collective-permute-start | bytes 1179656 | tf_op jit(solution)/shard_map/ppermute | solution.py:63
  208.3 16.7 %collective-permute-start.38 = (bf16[256,768]{1,0:T(8,128)(2,1)S(1)}, bf16[256,768]{1,0:T(8,128)(2,1)S(1)}, u32[]{:S(2)}, u32[]{:S(2)}) collective-permute-start(bf16[256,768]{1,0:T(8,128)(2,1)S(1)} %get-tuple-element.270), channel_id=1, source_target_pairs={{0,1},{1,0},{2,3},{3,2},{4,5},{5,4},{6,7},{7,6},{8,9},{9,8},{10,11... | collective-permute-start | bytes 1179656 | tf_op jit(solution)/shard_map/ppermute | solution.py:59
  208.3 16.6 %collective-permute-start.41 = (bf16[192,768]{1,0:T(8,128)(2,1)S(1)}, bf16[192,768]{1,0:T(8,128)(2,1)S(1)}, u32[]{:S(2)}, u32[]{:S(2)}) collective-permute-start(bf16[192,768]{1,0:T(8,128)(2,1)S(1)} %get-tuple-element.266), channel_id=1, source_target_pairs={{0,16},{4,20},{8,24},{12,28},{16,0},{20,4},{24,8},{28,12},{1,17},{... | collective-permute-start | bytes 884744 | tf_op jit(solution)/shard_map/ppermute | solution.py:730
  216.3 27.6 %collective-permute-start.44 = (bf16[384,768]{1,0:T(8,128)(2,1)S(1)}, bf16[384,768]{1,0:T(8,128)(2,1)S(1)}, u32[]{:S(2)}, u32[]{:S(2)}) collective-permute-start(bf16[384,768]{1,0:T(8,128)(2,1)S(1)} %get-tuple-element.278), channel_id=1, source_target_pairs={{0,4},{4,0},{8,12},{12,8},{16,20},{20,16},{24,28},{28,24},{1,5},{5... | collective-permute-start | bytes 1769480 | tf_op jit(solution)/shard_map/ppermute | solution.py:730
  225.8 18.3 %collective-permute-start.43 = (bf16[256,768]{1,0:T(8,128)(2,1)S(1)}, bf16[256,768]{1,0:T(8,128)(2,1)S(1)}, u32[]{:S(2)}, u32[]{:S(2)}) collective-permute-start(bf16[256,768]{1,0:T(8,128)(2,1)S(1)} %get-tuple-element.285.g0.refs_4_), channel_id=1, source_target_pairs={{0,2},{1,3},{2,0},{3,1},{4,6},{5,7},{6,4},{7,5},{8,10},{9,11},{10,... | collective-permute-start | bytes 1179656 | tf_op jit(solution)/shard_map/ppermute | solution.py:63
  226.8 14.4 %collective-permute-start.46 = (bf16[192,768]{1,0:T(8,128)(2,1)S(1)}, bf16[192,768]{1,0:T(8,128)(2,1)S(1)}, u32[]{:S(2)}, u32[]{:S(2)}) collective-permute-start(bf16[192,768]{1,0:T(8,128)(2,1)S(1)} %get-tuple-element.282), channel_id=1, source_target_pairs={{0,8},{4,12},{8,0},{12,4},{16,24},{20,28},{24,16},{28,20},{1,9},{5... | collective-permute-start | bytes 884744 | tf_op jit(solution)/shard_map/ppermute | solution.py:730
  227.5 16.4 %collective-permute-start.45 = (bf16[192,768]{1,0:T(8,128)(2,1)S(1)}, bf16[192,768]{1,0:T(8,128)(2,1)S(1)}, u32[]{:S(2)}, u32[]{:S(2)}) collective-permute-start(bf16[192,768]{1,0:T(8,128)(2,1)S(1)} %add.60.own_ref), channel_id=1, source_target_pairs={{0,16},{4,20},{8,24},{12,28},{16,0},{20,4},{24,8},{28,12},{1,17},{... | collective-permute-start | bytes 884744 | tf_op jit(solution)/shard_map/ppermute | solution.py:730
  230.8 14.9 %collective-permute-start.54 = (bf16[256,768]{1,0:T(8,128)(2,1)S(1)}, bf16[256,768]{1,0:T(8,128)(2,1)S(1)}, u32[]{:S(2)}, u32[]{:S(2)}) collective-permute-start(bf16[256,768]{1,0:T(8,128)(2,1)S(1)} %get-tuple-element.285.g0.refs_4_), channel_id=1, source_target_pairs={{0,1},{1,0},{2,3},{3,2},{4,5},{5,4},{6,7},{7,6},{8,9},{9,8},{10,11... | collective-permute-start | bytes 1179656 | tf_op jit(solution)/shard_map/ppermute | solution.py:59
  244.2 36.6 %collective-permute-start.52 = (bf16[384,768]{1,0:T(8,128)(2,1)S(1)}, bf16[384,768]{1,0:T(8,128)(2,1)S(1)}, u32[]{:S(2)}, u32[]{:S(2)}) collective-permute-start(bf16[384,768]{1,0:T(8,128)(2,1)S(1)} %get-tuple-element.298), channel_id=1, source_target_pairs={{0,4},{4,0},{8,12},{12,8},{16,20},{20,16},{24,28},{28,24},{1,5},{5... | collective-permute-start | bytes 1769480 | tf_op jit(solution)/shard_map/ppermute | solution.py:730
  252.6 26.6 %collective-permute-start.53 = (bf16[192,768]{1,0:T(8,128)(2,1)S(1)}, bf16[192,768]{1,0:T(8,128)(2,1)S(1)}, u32[]{:S(2)}, u32[]{:S(2)}) collective-permute-start(bf16[192,768]{1,0:T(8,128)(2,1)S(1)} %get-tuple-element.291), channel_id=1, source_target_pairs={{0,8},{4,12},{8,0},{12,4},{16,24},{20,28},{24,16},{28,20},{1,9},{5... | collective-permute-start | bytes 884744 | tf_op jit(solution)/shard_map/ppermute | solution.py:730
  253.0 28.3 %collective-permute-start.59 = (bf16[384,768]{1,0:T(8,128)(2,1)S(1)}, bf16[384,768]{1,0:T(8,128)(2,1)S(1)}, u32[]{:S(2)}, u32[]{:S(2)}) collective-permute-start(bf16[384,768]{1,0:T(8,128)(2,1)S(1)} %join.10.own_ref), channel_id=1, source_target_pairs={{0,8},{4,12},{8,0},{12,4},{16,24},{20,28},{24,16},{28,20},{1,9},{5... | collective-permute-start | bytes 1769480 | tf_op jit(solution)/shard_map/ppermute | solution.py:730
  254.7 20.9 %collective-permute-start.51 = (bf16[96,768]{1,0:T(8,128)(2,1)S(1)}, bf16[96,768]{1,0:T(8,128)(2,1)S(1)}, u32[]{:S(2)}, u32[]{:S(2)}) collective-permute-start(bf16[96,768]{1,0:T(8,128)(2,1)S(1)} %get-tuple-element.288), channel_id=1, source_target_pairs={{0,16},{4,20},{8,24},{12,28},{16,0},{20,4},{24,8},{28,12},{1,17},{... | collective-permute-start | bytes 442376 | tf_op jit(solution)/shard_map/ppermute | solution.py:730
  255.7 26.3 %collective-permute-start.58 = (bf16[256,768]{1,0:T(8,128)(2,1)S(1)}, bf16[256,768]{1,0:T(8,128)(2,1)S(1)}, u32[]{:S(2)}, u32[]{:S(2)}) collective-permute-start(bf16[256,768]{1,0:T(8,128)(2,1)S(1)} %add.62), channel_id=1, source_target_pairs={{0,2},{1,3},{2,0},{3,1},{4,6},{5,7},{6,4},{7,5},{8,10},{9,11},{10,... | collective-permute-start | bytes 1179656 | tf_op jit(solution)/shard_map/ppermute | solution.py:63
  275.6 9.9 %collective-permute-start.57 = (bf16[256,768]{1,0:T(8,128)(2,1)S(1)}, bf16[256,768]{1,0:T(8,128)(2,1)S(1)}, u32[]{:S(2)}, u32[]{:S(2)}) collective-permute-start(bf16[256,768]{1,0:T(8,128)(2,1)S(1)} %get-tuple-element.318), channel_id=1, source_target_pairs={{0,1},{1,0},{2,3},{3,2},{4,5},{5,4},{6,7},{7,6},{8,9},{9,8},{10,11... | collective-permute-start | bytes 1179656 | tf_op jit(solution)/shard_map/ppermute | solution.py:59
  279.2 19.3 %collective-permute-start.63 = (bf16[384,768]{1,0:T(8,128)(2,1)S(1)}, bf16[384,768]{1,0:T(8,128)(2,1)S(1)}, u32[]{:S(2)}, u32[]{:S(2)}) collective-permute-start(bf16[384,768]{1,0:T(8,128)(2,1)S(1)} %get-tuple-element.310), channel_id=1, source_target_pairs={{0,4},{4,0},{8,12},{12,8},{16,20},{20,16},{24,28},{28,24},{1,5},{5... | collective-permute-start | bytes 1769480 | tf_op jit(solution)/shard_map/ppermute | solution.py:730
  280.8 12.5 %collective-permute-start.49 = (bf16[256,768]{1,0:T(8,128)(2,1)S(1)}, bf16[256,768]{1,0:T(8,128)(2,1)S(1)}, u32[]{:S(2)}, u32[]{:S(2)}) collective-permute-start(bf16[256,768]{1,0:T(8,128)(2,1)S(1)} %get-tuple-element.296), channel_id=1, source_target_pairs={{0,1},{1,0},{2,3},{3,2},{4,5},{5,4},{6,7},{7,6},{8,9},{9,8},{10,11... | collective-permute-start | bytes 1179656 | tf_op jit(solution)/shard_map/ppermute | solution.py:59
  281.4 62.4 %collective-permute-start.74 = (bf16[768,768]{1,0:T(8,128)(2,1)S(1)}, bf16[768,768]{1,0:T(8,128)(2,1)S(1)}, u32[]{:S(2)}, u32[]{:S(2)}) collective-permute-start(bf16[768,768]{1,0:T(8,128)(2,1)S(1)} %join.11.own_ref), channel_id=1, source_target_pairs={{0,4},{4,0},{8,12},{12,8},{16,20},{20,16},{24,28},{28,24},{1,5},{5... | collective-permute-start | bytes 3538952 | tf_op jit(solution)/shard_map/ppermute | solution.py:730
  282.0 12.4 %collective-permute-start.64 = (bf16[96,768]{1,0:T(8,128)(2,1)S(1)}, bf16[96,768]{1,0:T(8,128)(2,1)S(1)}, u32[]{:S(2)}, u32[]{:S(2)}) collective-permute-start(bf16[96,768]{1,0:T(8,128)(2,1)S(1)} %get-tuple-element.312), channel_id=1, source_target_pairs={{0,16},{4,20},{8,24},{12,28},{16,0},{20,4},{24,8},{28,12},{1,17},{... | collective-permute-start | bytes 442376 | tf_op jit(solution)/shard_map/ppermute | solution.py:730
  288.7 12.6 %collective-permute-start.62 = (bf16[192,768]{1,0:T(8,128)(2,1)S(1)}, bf16[192,768]{1,0:T(8,128)(2,1)S(1)}, u32[]{:S(2)}, u32[]{:S(2)}) collective-permute-start(bf16[192,768]{1,0:T(8,128)(2,1)S(1)} %get-tuple-element.314), channel_id=1, source_target_pairs={{0,8},{4,12},{8,0},{12,4},{16,24},{20,28},{24,16},{28,20},{1,9},{5... | collective-permute-start | bytes 884744 | tf_op jit(solution)/shard_map/ppermute | solution.py:730
  294.4 13.6 %collective-permute-start.48 = (bf16[256,768]{1,0:T(8,128)(2,1)S(1)}, bf16[256,768]{1,0:T(8,128)(2,1)S(1)}, u32[]{:S(2)}, u32[]{:S(2)}) collective-permute-start(bf16[256,768]{1,0:T(8,128)(2,1)S(1)} %get-tuple-element.294), channel_id=1, source_target_pairs={{0,1},{1,0},{2,3},{3,2},{4,5},{5,4},{6,7},{7,6},{8,9},{9,8},{10,11... | collective-permute-start | bytes 1179656 | tf_op jit(solution)/shard_map/ppermute | solution.py:59
  297.4 12.3 %collective-permute-start.50 = (bf16[256,768]{1,0:T(8,128)(2,1)S(1)}, bf16[256,768]{1,0:T(8,128)(2,1)S(1)}, u32[]{:S(2)}, u32[]{:S(2)}) collective-permute-start(bf16[256,768]{1,0:T(8,128)(2,1)S(1)} %add.61), channel_id=1, source_target_pairs={{0,2},{1,3},{2,0},{3,1},{4,6},{5,7},{6,4},{7,5},{8,10},{9,11},{10,... | collective-permute-start | bytes 1179656 | tf_op jit(solution)/shard_map/ppermute | solution.py:63
  298.5 8.5 %collective-permute-start.56 = (bf16[96,768]{1,0:T(8,128)(2,1)S(1)}, bf16[96,768]{1,0:T(8,128)(2,1)S(1)}, u32[]{:S(2)}, u32[]{:S(2)}) collective-permute-start(bf16[96,768]{1,0:T(8,128)(2,1)S(1)} %add.63.own_ref), channel_id=1, source_target_pairs={{0,16},{4,20},{8,24},{12,28},{16,0},{20,4},{24,8},{28,12},{1,17},{... | collective-permute-start | bytes 442376 | tf_op jit(solution)/shard_map/ppermute | solution.py:730
  301.3 19.3 %collective-permute-start.68 = (bf16[192,768]{1,0:T(8,128)(2,1)S(1)}, bf16[192,768]{1,0:T(8,128)(2,1)S(1)}, u32[]{:S(2)}, u32[]{:S(2)}) collective-permute-start(bf16[192,768]{1,0:T(8,128)(2,1)S(1)} %get-tuple-element.333), channel_id=1, source_target_pairs={{0,8},{4,12},{8,0},{12,4},{16,24},{20,28},{24,16},{28,20},{1,9},{5... | collective-permute-start | bytes 884744 | tf_op jit(solution)/shard_map/ppermute | solution.py:730
  307.1 16.4 %collective-permute-start.66 = (bf16[192,768]{1,0:T(8,128)(2,1)S(1)}, bf16[192,768]{1,0:T(8,128)(2,1)S(1)}, u32[]{:S(2)}, u32[]{:S(2)}) collective-permute-start(bf16[192,768]{1,0:T(8,128)(2,1)S(1)} %join.12.own_ref), channel_id=1, source_target_pairs={{0,8},{4,12},{8,0},{12,4},{16,24},{20,28},{24,16},{28,20},{1,9},{5... | collective-permute-start | bytes 884744 | tf_op jit(solution)/shard_map/ppermute | solution.py:730
  308.1 12.5 %collective-permute-start.69 = (bf16[96,768]{1,0:T(8,128)(2,1)S(1)}, bf16[96,768]{1,0:T(8,128)(2,1)S(1)}, u32[]{:S(2)}, u32[]{:S(2)}) collective-permute-start(bf16[96,768]{1,0:T(8,128)(2,1)S(1)} %add.66.own_ref), channel_id=1, source_target_pairs={{0,16},{4,20},{8,24},{12,28},{16,0},{20,4},{24,8},{28,12},{1,17},{... | collective-permute-start | bytes 442376 | tf_op jit(solution)/shard_map/ppermute | solution.py:730
  309.7 12.4 %collective-permute-start.67 = (bf16[96,768]{1,0:T(8,128)(2,1)S(1)}, bf16[96,768]{1,0:T(8,128)(2,1)S(1)}, u32[]{:S(2)}, u32[]{:S(2)}) collective-permute-start(bf16[96,768]{1,0:T(8,128)(2,1)S(1)} %get-tuple-element.335), channel_id=1, source_target_pairs={{0,16},{4,20},{8,24},{12,28},{16,0},{20,4},{24,8},{28,12},{1,17},{... | collective-permute-start | bytes 442376 | tf_op jit(solution)/shard_map/ppermute | solution.py:730
  323.5 30.5 %collective-permute-start.77 = (bf16[384,768]{1,0:T(8,128)(2,1)S(1)}, bf16[384,768]{1,0:T(8,128)(2,1)S(1)}, u32[]{:S(2)}, u32[]{:S(2)}) collective-permute-start(bf16[384,768]{1,0:T(8,128)(2,1)S(1)} %join.14.own_ref), channel_id=1, source_target_pairs={{0,4},{4,0},{8,12},{12,8},{16,20},{20,16},{24,28},{28,24},{1,5},{5... | collective-permute-start | bytes 1769480 | tf_op jit(solution)/shard_map/ppermute | solution.py:730
  324.9 15.6 %collective-permute-start.73 = (bf16[192,768]{1,0:T(8,128)(2,1)S(1)}, bf16[192,768]{1,0:T(8,128)(2,1)S(1)}, u32[]{:S(2)}, u32[]{:S(2)}) collective-permute-start(bf16[192,768]{1,0:T(8,128)(2,1)S(1)} %join.13.own_ref), channel_id=1, source_target_pairs={{0,8},{4,12},{8,0},{12,4},{16,24},{20,28},{24,16},{28,20},{1,9},{5... | collective-permute-start | bytes 884744 | tf_op jit(solution)/shard_map/ppermute | solution.py:730
  326.3 14.2 %collective-permute-start.65 = (f32[48,768]{1,0:T(8,128)S(1)}, f32[48,768]{1,0:T(8,128)S(1)}, u32[]{:S(2)}, u32[]{:S(2)}) collective-permute-start(f32[48,768]{1,0:T(8,128)S(1)} %pack_all.1), channel_id=1, source_target_pairs={{0,4},{4,0},{8,12},{12,8},{16,20},{20,16},{24,28},{28,24},{1,5},{5... | collective-permute-start | bytes 442376 | tf_op jit(solution)/shard_map/ppermute | solution.py:1002
  326.9 19.5 %collective-permute-start.72 = (bf16[96,768]{1,0:T(8,128)(2,1)S(1)}, bf16[96,768]{1,0:T(8,128)(2,1)S(1)}, u32[]{:S(2)}, u32[]{:S(2)}) collective-permute-start(bf16[96,768]{1,0:T(8,128)(2,1)S(1)} %get-tuple-element.348), channel_id=1, source_target_pairs={{0,16},{4,20},{8,24},{12,28},{16,0},{20,4},{24,8},{28,12},{1,17},{... | collective-permute-start | bytes 442376 | tf_op jit(solution)/shard_map/ppermute | solution.py:730
  340.6 22.6 %collective-permute-start.80 = (bf16[384,768]{1,0:T(8,128)(2,1)S(1)}, bf16[384,768]{1,0:T(8,128)(2,1)S(1)}, u32[]{:S(2)}, u32[]{:S(2)}) collective-permute-start(bf16[384,768]{1,0:T(8,128)(2,1)S(1)} %join.15.own_ref), channel_id=1, source_target_pairs={{0,4},{4,0},{8,12},{12,8},{16,20},{20,16},{24,28},{28,24},{1,5},{5... | collective-permute-start | bytes 1769480 | tf_op jit(solution)/shard_map/ppermute | solution.py:730
  342.0 11.9 %collective-permute-start.71 = (bf16[96,768]{1,0:T(8,128)(2,1)S(1)}, bf16[96,768]{1,0:T(8,128)(2,1)S(1)}, u32[]{:S(2)}, u32[]{:S(2)}) collective-permute-start(bf16[96,768]{1,0:T(8,128)(2,1)S(1)} %add.67.own_ref), channel_id=1, source_target_pairs={{0,16},{4,20},{8,24},{12,28},{16,0},{20,4},{24,8},{28,12},{1,17},{... | collective-permute-start | bytes 442376 | tf_op jit(solution)/shard_map/ppermute | solution.py:730
  346.4 9.2 %collective-permute-start.76 = (bf16[96,768]{1,0:T(8,128)(2,1)S(1)}, bf16[96,768]{1,0:T(8,128)(2,1)S(1)}, u32[]{:S(2)}, u32[]{:S(2)}) collective-permute-start(bf16[96,768]{1,0:T(8,128)(2,1)S(1)} %add.69.own_ref), channel_id=1, source_target_pairs={{0,16},{4,20},{8,24},{12,28},{16,0},{20,4},{24,8},{28,12},{1,17},{... | collective-permute-start | bytes 442376 | tf_op jit(solution)/shard_map/ppermute | solution.py:730
  353.9 8.6 %collective-permute-start.79 = (bf16[192,768]{1,0:T(8,128)(2,1)S(1)}, bf16[192,768]{1,0:T(8,128)(2,1)S(1)}, u32[]{:S(2)}, u32[]{:S(2)}) collective-permute-start(bf16[192,768]{1,0:T(8,128)(2,1)S(1)} %join.16.own_ref), channel_id=1, source_target_pairs={{0,8},{4,12},{8,0},{12,4},{16,24},{20,28},{24,16},{28,20},{1,9},{5... | collective-permute-start | bytes 884744 | tf_op jit(solution)/shard_map/ppermute | solution.py:730
  355.6 11.5 %collective-permute-start.78 = (bf16[192,768]{1,0:T(8,128)(2,1)S(1)}, bf16[192,768]{1,0:T(8,128)(2,1)S(1)}, u32[]{:S(2)}, u32[]{:S(2)}) collective-permute-start(bf16[192,768]{1,0:T(8,128)(2,1)S(1)} %join.17.own_ref), channel_id=1, source_target_pairs={{0,8},{4,12},{8,0},{12,4},{16,24},{20,28},{24,16},{28,20},{1,9},{5... | collective-permute-start | bytes 884744 | tf_op jit(solution)/shard_map/ppermute | solution.py:730
  362.5 19.5 %collective-permute-start.82 = (bf16[384,768]{1,0:T(8,128)(2,1)S(1)}, bf16[384,768]{1,0:T(8,128)(2,1)S(1)}, u32[]{:S(2)}, u32[]{:S(2)}) collective-permute-start(bf16[384,768]{1,0:T(8,128)(2,1)S(1)} %join.18.own_ref), channel_id=1, source_target_pairs={{0,4},{4,0},{8,12},{12,8},{16,20},{20,16},{24,28},{28,24},{1,5},{5... | collective-permute-start | bytes 1769480 | tf_op jit(solution)/shard_map/ppermute | solution.py:730
  367.2 16.4 %collective-permute-start.81 = (bf16[384,768]{1,0:T(8,128)(2,1)S(1)}, bf16[384,768]{1,0:T(8,128)(2,1)S(1)}, u32[]{:S(2)}, u32[]{:S(2)}) collective-permute-start(bf16[384,768]{1,0:T(8,128)(2,1)S(1)} %join.19.own_ref), channel_id=1, source_target_pairs={{0,4},{4,0},{8,12},{12,8},{16,20},{20,16},{24,28},{28,24},{1,5},{5... | collective-permute-start | bytes 1769480 | tf_op jit(solution)/shard_map/ppermute | solution.py:730
  367.2 5.7 %collective-permute-start.70 = (f32[48,768]{1,0:T(8,128)S(1)}, f32[48,768]{1,0:T(8,128)S(1)}, u32[]{:S(2)}, u32[]{:S(2)}) collective-permute-start(f32[48,768]{1,0:T(8,128)S(1)} %add.68), channel_id=1, source_target_pairs={{0,8},{4,12},{8,0},{12,4},{16,24},{20,28},{24,16},{28,20},{1,9},{5... | collective-permute-start | bytes 442376 | tf_op jit(solution)/shard_map/ppermute | solution.py:1010
  373.0 7.6 %collective-permute-start.75 = (f32[48,768]{1,0:T(8,128)S(1)}, f32[48,768]{1,0:T(8,128)S(1)}, u32[]{:S(2)}, u32[]{:S(2)}) collective-permute-start(f32[48,768]{1,0:T(8,128)S(1)} %add.70), channel_id=1, source_target_pairs={{0,16},{4,20},{8,24},{12,28},{16,0},{20,4},{24,8},{28,12},{1,17},{... | collective-permute-start | bytes 442376 | tf_op jit(solution)/shard_map/ppermute | solution.py:758
  (124 other events, 1228.6 us)

commit v3 on v2

--- a/solution.py
+++ b/solution.py
@@ -458,43 +458,15 @@
     return made[:4], made[4:]
 
 
-def fetched(sources, targets, sems):
-    copies = [pltpu.make_async_copy(s, t, sems.at[i]) for i, (s, t) in enumerate(zip(sources, targets))]
-    for copy in copies:
-        copy.start()
-    return copies
-
-
-def fetching_call(body, name, outs, flops, operands, place, scratch):
-    moved = sum(x.size * x.dtype.itemsize for x in operands)
-    return pl.pallas_call(
-        body,
-        out_shape=tuple(outs),
-        in_specs=[pl.BlockSpec(memory_space=pltpu.HBM)] * len(operands) + [pl.BlockSpec(memory_space=pltpu.SMEM)],
-        out_specs=tuple([VMEM] * len(outs)),
-        scratch_shapes=[pltpu.VMEM(x.shape, x.dtype) for x in operands]
-        + [pltpu.SemaphoreType.DMA((len(operands),))]
-        + list(scratch),
-        name=name,
-        compiler_params=pltpu.CompilerParams(vmem_limit_bytes=2 * VMEM_GRANT),
-        cost_estimate=pl.CostEstimate(flops=flops // 100, bytes_accessed=moved // 100, transcendentals=0),
-    )(*operands, place)
-
-
 def attention_grads_kernel(*refs):
-    sources, place_ref, keep_ref, send_ref = refs[:10], *refs[10:13]
-    targets, sems, acc_ref = refs[13:23], *refs[23:]
-    copies = fetched(sources, targets, sems)
-    stack_ref, o_ref = targets[8:]
+    rows_refs, grad_refs, (stack_ref, o_ref, place_ref, keep_ref, send_ref, acc_ref) = refs[:4], refs[4:8], refs[8:]
     pages, parts, length, local = stack_ref.shape
-    size = targets[0].shape[0] // pages
+    size = rows_refs[0].shape[0] // pages
     acc_ref[...] = jnp.zeros(acc_ref.shape, F32)
-    for copy in copies:
-        copy.wait()
 
     def step(page, carry):
-        rows = page_rows(targets[:4], page, size)
-        grad = page_rows(targets[4:8], page, size)
+        rows = page_rows(rows_refs, page, size)
+        grad = page_rows(grad_refs, page, size)
         acc_ref[:local] += mxu(o_ref[page], grad, TN)
         for t in range(parts):
             acc_ref[(t + 1) * local : (t + 2) * local] += mxu(stack_ref[page, t], rows, TN)
@@ -509,14 +481,17 @@
 
 def attention_grads(rows, grads, stack, o, place):
     local, width = o.shape[-1], rows[0].shape[-1]
-    return fetching_call(
+    return kernel_call(
         attention_grads_kernel,
         "attention_grads",
         [shape((2 * local, width), BF)] * 2,
         3_000_000_000,
-        [*rows, *grads, stack, o],
-        place,
-        [pltpu.VMEM((4 * local, width), F32)],
+        *rows,
+        *grads,
+        stack,
+        o,
+        scalar(place),
+        scratch=[pltpu.VMEM((4 * local, width), F32)],
     )
 
 
@@ -528,12 +503,10 @@
     return u * plus, slope
 
 
-def up_rows(layer, at, rows_ref, up_ref, bias_ref, z_ref, slope_ref, block):
-    u = mxu(rows_ref[at, :], up_ref[layer], NN) + of_layer(bias_ref, layer)
+def up_rows(layer, rows, up_ref, bias_ref):
+    u = mxu(rows, up_ref[layer], NN) + of_layer(bias_ref, layer)
     z, slope = gelu_parts(u)
-    z = z.astype(BF)
-    z_ref[block, at, :] = z
-    return z, slope
+    return z.astype(BF), slope
 
 
 def forward_kernel(layer, c0, c1, c2, c3, up_ref, bias_ref, down_ref, p0, p1, p2, p3, z_ref, slope_ref):
@@ -542,7 +515,8 @@
 
         def step(i, carry):
             at = pl.ds(pl.multiple_of(i * size, size), size)
-            z, slope = up_rows(layer, at, rows_ref, up_ref, bias_ref, z_ref, slope_ref, block)
+            z, slope = up_rows(layer, rows_ref[at, :], up_ref, bias_ref)
+            z_ref[block, at, :] = z
             slope_ref[block, at, :] = slope.astype(BF)
             out_ref[at, :] = mxu(z, down_ref[layer], NN).astype(BF)
             return carry
@@ -599,53 +573,7 @@
     return made[:4], made[4:]
 
 
-def both_kernel(
-    layer, c0, c1, c2, c3, g0, g1, g2, g3, up_ref, bias_ref, down_ref, p0, p1, p2, p3, z_ref, gu_ref, sums_ref
-):
-    size = 256
-    sums_ref[...] = jnp.zeros(sums_ref.shape, F32)
-    for block, (rows_ref, grad_ref, out_ref) in enumerate(
-        zip((c0, c1, c2, c3), (g0, g1, g2, g3), (p0, p1, p2, p3))
-    ):
-
-        def step(i, carry):
-            at = pl.ds(pl.multiple_of(i * size, size), size)
-            gz = mxu(grad_ref[at, :], down_ref[layer], NT)
-            z, slope = up_rows(layer, at, rows_ref, up_ref, bias_ref, z_ref, None, block)
-            gu = (gz * slope).astype(BF)
-            gu_ref[block, at, :] = gu
-            sums_ref[...] += fold_rows(gu.astype(F32))
-            out_ref[at, :] = mxu(gu, up_ref[layer], NT).astype(BF)
-            return carry
-
-        lax.fori_loop(0, rows_ref.shape[0] // size, step, 0)
-
-
-def feed_both(layer, blocks, grads, w_up, up_bias, w_down):
-    size, units = blocks[0].shape[0], w_up.shape[2]
-    outs = [shape(blocks[0].shape, BF)] * 4 + [shape((4, size, units), BF)] * 2 + [shape((8, units), F32)]
-    made = kernel_call(
-        functools.partial(both_kernel, layer),
-        "feed_both",
-        outs,
-        6_000_000_000,
-        *blocks,
-        *grads,
-        w_up,
-        up_bias,
-        w_down,
-    )
-    return made[:4], made[4:]
-
-
-def feed_grads_kernel(parts, *refs):
-    sources, place_ref = refs[:10], refs[10]
-    out_refs, refs = refs[11 : 11 + 2 * parts], refs[11 + 2 * parts :]
-    targets, sems, both_ref = refs[:10], *refs[10:]
-    copies = fetched(sources, targets, sems)
-    rows_refs, grad_refs, z_ref, gu_ref = targets[:4], targets[4:8], *targets[8:]
-    for copy in copies:
-        copy.wait()
+def feed_grads_into(rows_refs, grad_refs, z_ref, gu_ref, place_ref, out_refs, both_ref):
     unused, units, width = both_ref.shape
     step = 256
     for start in range(0, units, step):
@@ -655,6 +583,7 @@
         up = sum(mxu(c[:, rows], gu_ref[i], TN) for i, c in enumerate(rows_refs))
         both_ref[1, rows, :] = up.astype(BF)
     mine = place_ref[0] & 1
+    parts = len(out_refs) // 2
     size = units // parts
     for part in range(parts):
         rows = slice(part * size, (part + 1) * size)
@@ -662,22 +591,79 @@
         out_refs[2 * part + 1][...] = both_ref[1 - mine, rows, :]
 
 
+def feed_grads_kernel(*refs):
+    feed_grads_into(refs[:4], refs[4:8], refs[8], refs[9], refs[10], refs[11:-1], refs[-1])
+
+
 def feed_grads(rows, grads, z, gu, place, parts):
     units, width = z.shape[-1], rows[0].shape[-1]
-    made = fetching_call(
-        functools.partial(feed_grads_kernel, parts),
+    made = kernel_call(
+        feed_grads_kernel,
         "feed_grads",
         [shape((units // parts, width), BF)] * (2 * parts),
         4_000_000_000,
-        [*rows, *grads, z, gu],
-        place,
-        [pltpu.VMEM((2, units, width), BF)],
+        *rows,
+        *grads,
+        z,
+        gu,
+        scalar(place),
+        scratch=[pltpu.VMEM((2, units, width), BF)],
     )
     return [made[2 * i : 2 * i + 2] for i in range(parts)]
+
+
+def both_kernel(layer, *refs):
+    rows_refs, grad_refs, (up_ref, bias_ref, down_ref, place_ref) = refs[:4], refs[4:8], refs[8:12]
+    out_refs, (z_ref, sums_ref, keep_ref, send_ref, gu_ref, both_ref) = refs[12:16], refs[16:]
+    sums_ref[...] = jnp.zeros(sums_ref.shape, F32)
+    for block in range(4):
+        gz = mxu(grad_refs[block][...], down_ref[layer], NT)
+        z, slope = up_rows(layer, rows_refs[block][...], up_ref, bias_ref)
+        z_ref[block] = z
+        gu = (gz * slope).astype(BF)
+        gu_ref[block] = gu
+        sums_ref[...] += fold_rows(gu.astype(F32))
+        out_refs[block][...] = mxu(gu, up_ref[layer], NT).astype(BF)
+    feed_grads_into(rows_refs, grad_refs, z_ref, gu_ref, place_ref, (keep_ref, send_ref), both_ref)
+
+
+def feed_both(layer, blocks, grads, w_up, up_bias, w_down, place):
+    size, units = blocks[0].shape[0], w_up.shape[2]
+    width = blocks[0].shape[1]
+    outs = [shape(blocks[0].shape, BF)] * 4 + [shape((4, size, units), BF), shape((8, units), F32)]
+    outs += [shape((units, width), BF)] * 2
+    made = kernel_call(
+        functools.partial(both_kernel, layer),
+        "feed_both",
+        outs,
+        10_000_000_000,
+        *blocks,
+        *grads,
+        w_up,
+        up_bias,
+        w_down,
+        scalar(place),
+        scratch=[pltpu.VMEM((4, size, units), BF), pltpu.VMEM((2, units, width), BF)],
+    )
+    return made[:4], made[4:6], made[6:]
 
 
 def partners(bits, bit):
     return [(i, i ^ (1 << bit)) for i in range(1 << len(bits))]
+
+
+def crossed(place, swapped):
+    other = (place & ~3) | ((place & 1) << 1) | ((place >> 1) & 1)
+    return jnp.where(swapped == 1, other, place)
+
+
+def crossed_partners(bits, bit, crossing):
+    pairs = []
+    for i in range(1 << len(bits)):
+        for t in range(4):
+            taken = bit ^ 1 if crossing and bit < 2 and t & 1 else bit
+            pairs.append((i * 4 + t, (i ^ (1 << taken)) * 4 + t))
+    return pairs
 
 
 def halve_kernel(bit, keep_ref, got_ref, place_ref, out_keep_ref, out_send_ref):
@@ -717,36 +703,36 @@
 
 
 class PageSum:
-    def __init__(self, halves, bits, place):
+    def __init__(self, halves, bits, places, crossing):
         self.own, send = halves
-        self.bits, self.place = bits, place
-        self.cuts = bits[1:3]
-        self.plan = [(self.down, bit) for bit in self.cuts] + [(self.turn, None)]
-        self.plan += [(self.up, bit) for bit in reversed(self.cuts)]
+        self.bits, self.place, self.crossing = bits, places[crossing], crossing
+        self.plan = [self.cut, self.add, self.turn, self.back]
         self.got = self.swap(send, 0)
 
     def swap(self, values, bit):
         self.sent = values
-        return lax.ppermute(values, "dp", partners(self.bits, bit))
-
-    def down(self, got, bit):
-        self.own, send = halve(self.own, got, bit, self.place)
-        return self.swap(send, bit)
-
-    def turn(self, got, unused):
+        return lax.ppermute(values, ("dp", "tensor"), crossed_partners(self.bits, bit, self.crossing))
+
+    def cut(self, got):
+        self.own, send = halve(self.own, got, 1, self.place)
+        return self.swap(send, 1)
+
+    def add(self, got):
+        self.own = self.own + got
+        return self.swap(self.own, 2)
+
+    def turn(self, got):
         self.own = self.own + got
         for bit in self.bits[3:]:
             self.own = self.own + self.swap(self.own, bit)
-        return self.swap(self.own, self.cuts[-1] if self.cuts else 0)
-
-    def up(self, got, bit):
-        self.own = join(self.own, got, bit, self.place)
-        index = self.bits.index(bit) - 1
-        return self.swap(self.own, self.bits[index])
+        return self.swap(self.own, 1)
+
+    def back(self, got):
+        self.own = join(self.own, got, 1, self.place)
+        return self.swap(self.own, 0)
 
     def step(self, token):
-        action, bit = self.plan.pop(0)
-        self.got = action(tied(self.got, token), bit)
+        self.got = self.plan.pop(0)(tied(self.got, token))
         return self.sent
 
     def ended(self):
@@ -914,7 +900,8 @@
     down_bias,
 ):
     member = lax.axis_index("tensor").reshape(1).astype(jnp.int32)
-    place = lax.axis_index("dp").reshape(1).astype(jnp.int32)
+    straight = lax.axis_index("dp").reshape(1).astype(jnp.int32)
+    places = [straight, crossed(straight, lax.axis_index("tensor") & 1)]
     bits = list(range(n_dp.bit_length() - 1))
     pages = patch_rows.shape[1]
     heads, entries = rel_table.shape[1:]
@@ -937,8 +924,10 @@
         middle, own = add_norm(hidden, near + [far], (layer, layer), out_bias, ln2_gain, ln2_bias)
         rows_two = spread(own)
         if layer == last:
-            partial, (z, gu, up_sums) = feed_both(layer, rows_two, last_blocks, w_up, up_bias, w_down)
-            kept.append((rows_one, before, saved, middle, rows_two, z, gu))
+            partial, (z, up_sums), mlp = feed_both(
+                layer, rows_two, last_blocks, w_up, up_bias, w_down, places[1]
+            )
+            kept.append((rows_one, before, saved, middle, rows_two, z, None))
         else:
             partial, (z, slope) = feed_forward(layer, rows_two, w_up, up_bias, w_down)
             kept.append((rows_one, before, saved, middle, rows_two, z, slope))
@@ -946,80 +935,89 @@
             hidden, own = add_norm(middle, near + [far], (layer, layer + 1), down_bias, ln1_gain, ln1_bias)
             blocks = spread(own)
 
-    rows_one, before, saved, middle, rows_two, z, gu = kept[last]
+    rows_one, before, saved, middle, rows_two, z, unused = kept[last]
     near, far, sent = collect(partial)
-    mlp = feed_grads(rows_two, last_blocks, tied(z, sent), gu, place, 1)
-    mlp1 = PageSum(mlp[0], bits, place)
-    far = tied(far, mlp)
+    mlp1 = PageSum(mlp, bits, places, 1)
     g1, low, twos1 = norm_back(last_own, near + [far], middle, last, ln2_gain)
     result_parts = down_product(last, tied(z, low), w_down)
-    out_blocks = spread(low, result_parts)
+    token = mlp1.step(result_parts[0])
+    out_blocks = spread(low, (result_parts, token))
     partial, (stack, totals, qv1) = attention_back(last, out_blocks, saved, w_qkv, w_out)
     near, far, sent = collect(partial)
-    mix = attention_grads(rows_one, out_blocks, tied(stack, sent), saved[-1], place)
-    mix1 = PageSum(mix, bits, place)
-    far = tied(far, mlp1.step(mix))
+    mix = attention_grads(rows_one, out_blocks, tied(stack, sent), saved[-1], places[1])
+    mix1 = PageSum(mix, bits, places, 1)
+    token = mlp1.step(mix)
+    far = tied(far, token)
     grad, low, ones1 = norm_back(g1, near + [far], before, last, ln1_gain)
     rel1 = sum_by_bucket(tied(totals, low), ordered)
-    token = mlp1.step(rel1)
+    token = mix1.step(rel1)
     grad_blocks = spread(low, (token,))
     up1 = up_sums
 
     rows_one, before, saved, middle, rows_two, z, slope = kept[0]
     partial, (gu, up0) = feed_back(0, grad_blocks, slope, w_up, w_down)
     near, far, sent = collect(partial)
-    mlp = feed_grads(rows_two, grad_blocks, tied(z, sent), gu, place, 2)
-    mlp0a = PageSum(mlp[0], bits, place)
+    mlp = feed_grads(rows_two, grad_blocks, tied(z, sent), gu, places[1], 2)
+    mlp0a, mlp0b = [PageSum(x, bits, places, 1) for x in mlp]
     token = mix1.step(mlp)
-    token = mlp1.step(token)
     far = tied(far, token)
     g1, low, twos0 = norm_back(grad, near + [far], middle, 0, ln2_gain)
-    token = mix1.step(low)
-    token = mlp1.step(token)
+    token = mlp1.step(low)
     token = mlp0a.step(token)
-    mlp0b = PageSum([mlp[1][0], tied(mlp[1][1], token)], bits, place)
     out_blocks = spread(low, (token,))
-    result_near, result_far, unused = collect([tied(p, out_blocks[3]) for p in result_parts])
     partial, (stack, totals, qv0) = attention_back(0, out_blocks, saved, w_qkv, w_out)
     near, far, sent = collect(partial)
-    mix = attention_grads(rows_one, out_blocks, tied(stack, sent), saved[-1], place)
-    mix0 = PageSum(mix, bits, place)
-    token = mlp0a.step(mix)
+    mix = attention_grads(rows_one, out_blocks, tied(stack, sent), saved[-1], places[1])
+    mix0 = PageSum(mix, bits, places, 1)
+    token = mlp1.step(mix)
     token = mlp0b.step(token)
     token = mix1.step(token)
-    token = mlp1.step(token)
     far = tied(far, token)
     grad, ones0 = last_norm_back(g1, near + [far], before, ln1_gain, masked)
 
+    def hop(values, axis, order, bit):
+        return lax.ppermute(values, axis, partners(order, bit))
+
     rows = pack_rows((ones0, ones1), (twos0, twos1), last_sum)
-    rows = rows + swap_core(rows)
-    rel0 = sum_by_bucket(tied(totals, rows), ordered)
-    token = mlp0a.step(rel0)
+    rows_got = hop(rows, "tensor", [0, 1], 0)
+    token = rows
+    token = mlp0a.step(token)
     token = mix0.step(token)
+    rows = token = rows + tied(rows_got, token)
+    rows_got = hop(rows, "tensor", [0, 1], 1)
+    rel0 = token = sum_by_bucket(tied(totals, token), ordered)
+    result_near, result_far, unused = collect([tied(p, rel0) for p in result_parts])
     token = mlp0b.step(token)
-    rows = rows + swap_chip(tied(rows, rel0))
-    small = pack_all(tied(rows, token), (qv0, qv1), (up0, up1), (rel0, rel1))
-    small_got = lax.ppermute(small, "dp", partners(bits, 0))
-    token = mix1.step(small)
-    result = last_result(kept[last][3], result_near + [tied(result_far, token)], last, down_bias, pages)
-    token = mlp0a.step((token, result))
+    small = pack_all(rows + tied(rows_got, token), (qv0, qv1), (up0, up1), (rel0, rel1))
+    small_got = hop(small, "dp", bits, 0)
+    token = small
+    token = mlp0a.step(token)
     token = mix0.step(token)
+    small = token = small + tied(small_got, token)
+    small_got = hop(small, "dp", bits, 1)
+    result = token = last_result(
+        kept[last][3], result_near + [tied(result_far, token)], last, down_bias, pages
+    )
+    token = mix1.step(token)
     token = mlp0b.step(token)
-    token = mix1.step(token)
+    small = token = small + tied(small_got, token)
+    small_got = hop(small, "dp", bits, 2)
+    token = mlp0a.step(token)
+    d_mlp = assemble_feed(last, 0, 1, mlp1, tied(places[1], token))
+    token = d_mlp[0]
+    token = mix0.step(token)
     small = small + tied(small_got, token)
-    small_got = lax.ppermute(small, "dp", partners(bits, bits[1])) if len(bits) > 1 else 0.0
-    token = mlp0a.step((token, small))
-    d_mlp = assemble_feed(last, 0, 1, mlp1, tied(place, token))
-    token = mix0.step((token, d_mlp))
+    small = token = sum_small(small, "dp", bits[3:], len(bits))
     token = mlp0b.step(token)
-    small = sum_small(small + tied(small_got, token), "dp", bits[2:], len(bits))
-    d_mix = assemble_attention(last, mix1, tied(place, token))
-    token = mix0.step((token, d_mix))
-    token = mlp0b.step(token)
-    d_mlp = assemble_feed(0, 0, 2, mlp0a, tied(place, token), d_mlp)
-    token = mix0.step((token, d_mlp))
-    d_mlp = assemble_feed(0, 1, 2, mlp0b, tied(place, token), d_mlp)
-    d_mix = assemble_attention(0, mix0, tied(place, token), d_mix)
+    d_mix = assemble_attention(last, mix1, tied(places[1], token))
+    token = d_mix[0]
+    token = mix0.step(token)
+    d_mlp = assemble_feed(0, 0, 2, mlp0a, tied(places[1], token), d_mlp)
+    token = d_mlp[0]
+    d_mlp = assemble_feed(0, 1, 2, mlp0b, tied(places[1], token), d_mlp)
+    token = d_mlp[0]
+    d_mix = assemble_attention(0, mix0, tied(places[1], token), d_mix)
+    token = d_mix[0]
     small = unpack(small, heads, entries)
     d_ln1_gain, d_ln1_bias, d_out_bias, d_ln2_gain, d_ln2_bias, d_down_bias, d_mask, d_up_bias, d_qv, d_rel = small
     return (

time: 389 us -> 369 us (0.949)
  local copies, waits for them, and re-layouts: 28.1 us -> 16.6 us
  Pallas kernels: 90.1 us -> 82.6 us
    pallas_call x4 -> x0, Pallas kernels: 17.8 us -> none  [fetching_call(): pl.pallas_call(body, out_shape=tuple(outs), in_specs=[pl.BlockSpec(memory...]
    unnamed x210 -> x174, local copies, waits for them, and re-layouts: 27.4 us -> 15.9 us
    ppermute x33 -> x30, waiting for transfers between devices: 102 us -> 91.6 us  [the longest x25 69.7 us: swap(): lax.ppermute(values, ('dp', 'tensor'), crossed_partners(self.bits, bit, s...]
    pallas_call x43 -> x36, Pallas kernels: 63.5 us -> 73.8 us  [kernel_call(): pl.pallas_call(body, out_shape=tuple(outs), in_specs=specs, out_specs=tup...]
    ppermute x17 -> x16, waiting for transfers between devices: 74.1 us -> 82.7 us  [swap_chip(): return lax.ppermute(values, 'tensor', CHIP)]
    ppermute x17 -> x16, starting transfers between devices: 22.4 us -> 24.1 us  [swap_chip(): return lax.ppermute(values, 'tensor', CHIP)]
    ppermute x33 -> x32, waiting for transfers between devices: 18.6 us -> 17.6 us  [swap_core(): return lax.ppermute(values, 'tensor', CORE)]
    ppermute x33 -> x30, starting transfers between devices: 41.8 us -> 41.6 us  [the longest x25 36.5 us: swap(): lax.ppermute(values, ('dp', 'tensor'), crossed_partners(self.bits, bit, s...]
  transfers between devices with their start and end apart: 83 -> 78, of which waited for: 43 -> 37; matrix products, arithmetic and copies ran while one was open for 0% -> 1% of each run, Pallas kernels for 16% -> 10%
where the time goes in v3:
time: 369 us; the launch traced here: 365 us
  waiting for transfers between devices  192 us (52%)
  Pallas kernels  82.6 us (22%)
  starting transfers between devices  69 us (19%)
  local copies, waits for them, and re-layouts  16.6 us (4%)
    ppermute x16, waiting for transfers between devices, swap_chip(): return lax.ppermute(values, 'tensor', CHIP)  82.7 us
    pallas_call x36, Pallas kernels, kernel_call(): pl.pallas_call(body, out_shape=tuple(outs), in_specs=specs, out_specs=tup...  73.8 us
    ppermute x25, waiting for transfers between devices, swap(): lax.ppermute(values, ('dp', 'tensor'), crossed_partners(self.bits, bit, s...  69.7 us
    ppermute x25, starting transfers between devices, swap(): lax.ppermute(values, ('dp', 'tensor'), crossed_partners(self.bits, bit, s...  36.5 us
    ppermute x16, starting transfers between devices, swap_chip(): return lax.ppermute(values, 'tensor', CHIP)  24.1 us
    ppermute x5, waiting for transfers between devices, hop(): return lax.ppermute(values, axis, partners(order, bit))  21.9 us
    ppermute x32, waiting for transfers between devices, swap_core(): return lax.ppermute(values, 'tensor', CORE)  17.6 us
    unnamed x174, local copies, waits for them, and re-layouts  15.9 us
  transfers between devices with their start and end apart: 78, of which 37 were waited for; matrix products, arithmetic and copies ran while one was open for 1% of the time, Pallas kernels for 10%

profile of v3, /device:TPU:0, one launch (start us, length us, event | category | flops | bytes accessed | tf_op | source)
XLA Modules:
  0.0 364.7 jit_solution(11131417643730679790)
XLA Ops:
  5.4 2.0 first_norm.1
  7.9 3.0 collective-permute-start.1
  13.3 5.0 %bias_of_buckets.1 = (bf16[2,3,256,256]{3,2,1,0:T(8,128)(2,1)S(1)}, s32[256,256]{1,0:T(8,128)S(1)}, f32[4,1,256]{2,1,0:T(1,128)S(1)}) custom-call(bf16[3,2,732]{2,1,0:T(2,128)(2,1)S(1)} %bitcast.13, s32[256,256]{1,0:T(8,128)S(1)} %copy-done.69, s32[4,256]{1,0:T(4,128)S(1)} %bitcast.16, s32[1]{0:T(128)} %bitcast.3.member_ref), custom_call_target="tpu_custom_call" | custom-call | flops 40000000 | bytes 13277 | tf_op jit(solution)/shard_map/bias_of_buckets/pallas_call | solution.py:42
  18.3 1.7 collective-permute-done.1.x2.refs_2_
  20.0 1.7 collective-permute-done.2.x3.refs_3_
  25.1 5.1 %attention.2 = (bf16[256,768]{1,0:T(8,128)(2,1)S(1)}, bf16[256,768]{1,0:T(8,128)(2,1)S(1)}, bf16[256,768]{1,0:T(8,128)(2,1)S(1)}, bf16[256,768]{1,0:T(8,128)(2,1...) custom-call(bf16[256,768]{1,0:T(8,128)(2,1)S(1)} %get-tuple-element., ...), custom_call_target="tpu_custom_call" | custom-call | flops 60000000 | bytes 94428 | tf_op jit(solution)/shard_map/attention/pallas_call | solution.py:42
  32.9 1.8 collective-permute-start.5
  34.8 9.4 %collective-permute-done.5.three_ref = bf16[256,768]{1,0:T(8,128)(2,1)S(1)} collective-permute-done((bf16[256,768]{1,0:T(8,128)(2,1)S(1)}, bf16[256,768]{1,0:T(8,128)(2,1)S(1)}, u32[]{:S(2)}, u32[]{:S(2)}) %collective-permute-start.5) | collective-permute-done | bytes 393248 | tf_op jit(solution)/shard_map/ppermute | solution.py:63
  44.7 1.8 collective-permute-start.7
  46.5 8.6 %collective-permute-done.7.c2.refs_2_ = bf16[256,768]{1,0:T(8,128)(2,1)S(1)} collective-permute-done((bf16[256,768]{1,0:T(8,128)(2,1)S(1)}, bf16[256,768]{1,0:T(8,128)(2,1)S(1)}, u32[]{:S(2)}, u32[]{:S(2)}) %collective-permute-start.7) | collective-permute-done | bytes 393248 | tf_op jit(solution)/shard_map/ppermute | solution.py:63
  56.9 3.7 %feed_forward.1 = (bf16[256,768]{1,0:T(8,128)(2,1)S(1)}, bf16[256,768]{1,0:T(8,128)(2,1)S(1)}, bf16[256,768]{1,0:T(8,128)(2,1)S(1)}, bf16[256,768]{1,0:T(8,128)(...) custom-call(bf16[256,768]{1,0:T(8,128)(2,1)S(1)} %get-tuple-element.193.c0.refs_0_, ...), custom_call_target="tpu_custom_call" | custom-call | flops 40000000 | bytes 110131 | tf_op jit(solution)/shard_map/feed_forward/pallas_call | solution.py:42
  63.6 1.8 collective-permute-start.11
  65.4 9.4 %collective-permute-done.11.three_ref = bf16[256,768]{1,0:T(8,128)(2,1)S(1)} collective-permute-done((bf16[256,768]{1,0:T(8,128)(2,1)S(1)}, bf16[256,768]{1,0:T(8,128)(2,1)S(1)}, u32[]{:S(2)}, u32[]{:S(2)}) %collective-permute-start.11) | collective-permute-done | bytes 393248 | tf_op jit(solution)/shard_map/ppermute | solution.py:63
  75.3 1.8 collective-permute-start.13
  77.1 8.6 %collective-permute-done.13.x2.refs_2_ = bf16[256,768]{1,0:T(8,128)(2,1)S(1)} collective-permute-done((bf16[256,768]{1,0:T(8,128)(2,1)S(1)}, bf16[256,768]{1,0:T(8,128)(2,1)S(1)}, u32[]{:S(2)}, u32[]{:S(2)}) %collective-permute-start.13) | collective-permute-done | bytes 393248 | tf_op jit(solution)/shard_map/ppermute | solution.py:63
  85.7 1.7 collective-permute-done.14.x3.refs_3_
  87.4 5.5 %attention.3 = (bf16[256,768]{1,0:T(8,128)(2,1)S(1)}, bf16[256,768]{1,0:T(8,128)(2,1)S(1)}, bf16[256,768]{1,0:T(8,128)(2,1)S(1)}, bf16[256,768]{1,0:T(8,128)(2,1...) custom-call(bf16[256,768]{1,0:T(8,128)(2,1)S(1)} %get-tuple-element., ...), custom_call_target="tpu_custom_call" | custom-call | flops 60000000 | bytes 94428 | tf_op jit(solution)/shard_map/attention/pallas_call | solution.py:42
  95.7 1.8 collective-permute-start.17
  97.8 9.9 %collective-permute-done.17.three_ref = bf16[256,768]{1,0:T(8,128)(2,1)S(1)} collective-permute-done((bf16[256,768]{1,0:T(8,128)(2,1)S(1)}, bf16[256,768]{1,0:T(8,128)(2,1)S(1)}, u32[]{:S(2)}, u32[]{:S(2)}) %collective-permute-start.17) | collective-permute-done | bytes 393248 | tf_op jit(solution)/shard_map/ppermute | solution.py:63
  109.8 1.7 collective-permute-start.19
  111.5 4.7 %collective-permute-done.22.refs_6_ = bf16[256,768]{1,0:T(8,128)(2,1)} collective-permute-done((bf16[256,768]{1,0:T(8,128)(2,1)S(1)}, bf16[256,768]{1,0:T(8,128)(2,1)}, u32[]{:S(2)}, u32[]{:S(2)}) %collective-permute-start.22) | collective-permute-done | bytes 393248 | tf_op jit(solution)/shard_map/ppermute | solution.py:63
  116.8 7.1 %collective-permute-done.19.refs_2_ = bf16[256,768]{1,0:T(8,128)(2,1)} collective-permute-done((bf16[256,768]{1,0:T(8,128)(2,1)}, bf16[256,768]{1,0:T(8,128)(2,1)}, u32[]{:S(2)}, u32[]{:S(2)}) %collective-permute-start.19) | collective-permute-done | bytes 393248 | tf_op jit(solution)/shard_map/ppermute | solution.py:63
  123.9 2.0 collective-permute-done.20.refs_3_
  127.6 10.4 %feed_both.1 = (bf16[256,768]{1,0:T(8,128)(2,1)S(1)}, bf16[256,768]{1,0:T(8,128)(2,1)S(1)}, bf16[256,768]{1,0:T(8,128)(2,1)S(1)}, bf16[256,768]{1,0:T(8,128)(2,1...) custom-call(bf16[256,768]{1,0:T(8,128)(2,1)} %get-tuple-element.205., ...), custom_call_target="tpu_custom_call" | custom-call | flops 100000000 | bytes 133969 | tf_op jit(solution)/shard_map/feed_both/pallas_call | solution.py:42
  138.2 1.7 collective-permute-start.29
  141.8 9.8 %collective-permute-done.26.three_ref = bf16[256,768]{1,0:T(8,128)(2,1)S(1)} collective-permute-done((bf16[256,768]{1,0:T(8,128)(2,1)S(1)}, bf16[256,768]{1,0:T(8,128)(2,1)S(1)}, u32[]{:S(2)}, u32[]{:S(2)}) %collective-permute-start.26) | collective-permute-done | bytes 393248 | tf_op jit(solution)/shard_map/ppermute | solution.py:63
  155.7 7.3 %collective-permute-done.28.g2.refs_6_ = bf16[256,768]{1,0:T(8,128)(2,1)S(1)} collective-permute-done((bf16[256,768]{1,0:T(8,128)(2,1)S(1)}, bf16[256,768]{1,0:T(8,128)(2,1)S(1)}, u32[]{:S(2)}, u32[]{:S(2)}) %collective-permute-start.28) | collective-permute-done | bytes 393248 | tf_op jit(solution)/shard_map/ppermute | solution.py:63
  163.0 1.7 collective-permute-done.30.g3.refs_7_
  164.8 6.6 %attention_back.2 = (bf16[256,768]{1,0:T(8,128)(2,1)S(1)}, bf16[256,768]{1,0:T(8,128)(2,1)S(1)}, bf16[256,768]{1,0:T(8,128)(2,1)S(1)}, bf16[256,768]{1,0:T(8,128...) custom-call(bf16[256,768]{1,0:T(8,128)(2,1)S(1)} %get-tuple-element.213.g0.re, ...), custom_call_target="tpu_custom_call" | custom-call | flops 90000000 | bytes 102359 | tf_op jit(solution)/shard_map/attention_back/pallas_call | solution.py:42
  171.5 1.7 collective-permute-start.34
  175.0 1.9 attention_grads.2
  177.9 4.8 %collective-permute-done.34 = bf16[384,768]{1,0:T(8,128)(2,1)S(1)} collective-permute-done((bf16[384,768]{1,0:T(8,128)(2,1)S(1)}, bf16[384,768]{1,0:T(8,128)(2,1)S(1)}, u32[]{:S(2)}, u32[]{:S(2)}) %collective-permute-start.34) | collective-permute-done | bytes 589856 | tf_op jit(solution)/shard_map/ppermute | solution.py:714
  186.8 4.0 %sum_by_bucket.2.rel1 = f32[72,32]{1,0:T(8,128)S(1)} custom-call(f32[3,256,256]{2,1,0:T(8,128)S(1)} %get-tuple-element.244.values_ref, s32[256,256]{1,0:T(8,128)S(1)} %copy-done.50), custom_call_target="tpu_custom_call" | custom-call | flops 60000000 | bytes 10577 | tf_op jit(solution)/shard_map/sum_by_bucket/pallas_call | solution.py:42
  191.0 4.4 %collective-permute-done.36.g2.refs_6_ = bf16[256,768]{1,0:T(8,128)(2,1)S(1)} collective-permute-done((bf16[256,768]{1,0:T(8,128)(2,1)S(1)}, bf16[256,768]{1,0:T(8,128)(2,1)S(1)}, u32[]{:S(2)}, u32[]{:S(2)}) %collective-permute-start.36) | collective-permute-done | bytes 393248 | tf_op jit(solution)/shard_map/ppermute | solution.py:63
  195.5 1.7 collective-permute-done.38.g3.refs_7_
  197.2 2.9 feed_back.1
  203.6 1.9 collective-permute-start.42
  205.5 2.6 collective-permute-start.46
  208.1 3.4 feed_grads.1
  215.6 17.9 %collective-permute-done.46 = bf16[384,768]{1,0:T(8,128)(2,1)S(1)} collective-permute-done((bf16[384,768]{1,0:T(8,128)(2,1)S(1)}, bf16[384,768]{1,0:T(8,128)(2,1)S(1)}, u32[]{:S(2)}, u32[]{:S(2)}) %collective-permute-start.46) | collective-permute-done | bytes 589856 | tf_op jit(solution)/shard_map/ppermute | solution.py:714
  235.8 6.4 %attention_back.3 = (bf16[256,768]{1,0:T(8,128)(2,1)S(1)}, bf16[256,768]{1,0:T(8,128)(2,1)S(1)}, bf16[256,768]{1,0:T(8,128)(2,1)S(1)}, bf16[256,768]{1,0:T(8,128...) custom-call(bf16[256,768]{1,0:T(8,128)(2,1)S(1)} %get-tuple-element.264.g0.re, ...), custom_call_target="tpu_custom_call" | custom-call | flops 90000000 | bytes 102359 | tf_op jit(solution)/shard_map/attention_back/pallas_call | solution.py:42
  243.1 3.4 collective-permute-start.51
  247.6 2.2 attention_grads.3
  251.5 11.7 %collective-permute-done.51 = bf16[192,768]{1,0:T(8,128)(2,1)S(1)} collective-permute-done((bf16[192,768]{1,0:T(8,128)(2,1)S(1)}, bf16[192,768]{1,0:T(8,128)(2,1)S(1)}, u32[]{:S(2)}, u32[]{:S(2)}) %collective-permute-start.51) | collective-permute-done | bytes 294944 | tf_op jit(solution)/shard_map/ppermute | solution.py:714
  263.4 3.3 collective-permute-start.56
  268.0 1.9 last_norm_back.1
  270.0 4.6 %collective-permute-done.56 = bf16[192,768]{1,0:T(8,128)(2,1)S(1)} collective-permute-done((bf16[192,768]{1,0:T(8,128)(2,1)S(1)}, bf16[192,768]{1,0:T(8,128)(2,1)S(1)}, u32[]{:S(2)}, u32[]{:S(2)}) %collective-permute-start.56) | collective-permute-done | bytes 294944 | tf_op jit(solution)/shard_map/ppermute | solution.py:714
  275.0 4.0 %sum_by_bucket.3.rel0 = f32[72,32]{1,0:T(8,128)S(1)} custom-call(f32[3,256,256]{2,1,0:T(8,128)S(1)} %get-tuple-element.299.values_ref, s32[256,256]{1,0:T(8,128)S(1)} %copy-done.50), custom_call_target="tpu_custom_call" | custom-call | flops 60000000 | bytes 10577 | tf_op jit(solution)/shard_map/sum_by_bucket/pallas_call | solution.py:42
  279.1 2.1 collective-permute-start.61
  281.1 2.2 collective-permute-start.64
  283.8 11.6 %collective-permute-done.61 = bf16[192,768]{1,0:T(8,128)(2,1)S(1)} collective-permute-done((bf16[192,768]{1,0:T(8,128)(2,1)S(1)}, bf16[192,768]{1,0:T(8,128)(2,1)S(1)}, u32[]{:S(2)}, u32[]{:S(2)}) %collective-permute-start.61) | collective-permute-done | bytes 294944 | tf_op jit(solution)/shard_map/ppermute | solution.py:714
  297.1 4.1 %collective-permute-done.62 = f32[48,768]{1,0:T(8,128)S(1)} collective-permute-done((f32[48,768]{1,0:T(8,128)S(1)}, f32[48,768]{1,0:T(8,128)S(1)}, u32[]{:S(2)}, u32[]{:S(2)}) %collective-permute-start.62) | collective-permute-done | bytes 147488 | tf_op jit(solution)/shard_map/ppermute | solution.py:979
  301.3 2.0 collective-permute-start.67
  304.7 2.4 collective-permute-start.71
  308.9 1.9 collective-permute-done.67.got_ref
  311.2 7.7 %collective-permute-done.66 = bf16[192,768]{1,0:T(8,128)(2,1)S(1)} collective-permute-done((bf16[192,768]{1,0:T(8,128)(2,1)S(1)}, bf16[192,768]{1,0:T(8,128)(2,1)S(1)}, u32[]{:S(2)}, u32[]{:S(2)}) %collective-permute-start.66) | collective-permute-done | bytes 294944 | tf_op jit(solution)/shard_map/ppermute | solution.py:714
  318.9 1.8 collective-permute-start.65
  320.8 9.5 %collective-permute-done.65 = f32[48,768]{1,0:T(8,128)S(1)} collective-permute-done((f32[48,768]{1,0:T(8,128)S(1)}, f32[48,768]{1,0:T(8,128)S(1)}, u32[]{:S(2)}, u32[]{:S(2)}) %collective-permute-start.65) | collective-permute-done | bytes 147488 | tf_op jit(solution)/shard_map/ppermute | solution.py:979
  330.3 2.5 collective-permute-start.74
  332.9 2.5 assemble_feed.3
  335.6 1.8 collective-permute-start.68
  338.2 8.3 %collective-permute-done.68 = f32[48,768]{1,0:T(8,128)S(1)} collective-permute-done((f32[48,768]{1,0:T(8,128)S(1)}, f32[48,768]{1,0:T(8,128)S(1)}, u32[]{:S(2)}, u32[]{:S(2)}) %collective-permute-start.68) | collective-permute-done | bytes 147488 | tf_op jit(solution)/shard_map/ppermute | solution.py:979
  353.4 3.1 collective-permute-done.76.got_ref
  358.1 4.7 %collective-permute-done.75.got_ref = bf16[384,768]{1,0:T(8,128)(2,1)S(1)} collective-permute-done((bf16[384,768]{1,0:T(8,128)(2,1)S(1)}, bf16[384,768]{1,0:T(8,128)(2,1)S(1)}, u32[]{:S(2)}, u32[]{:S(2)}) %collective-permute-start.75) | collective-permute-done | bytes 589856 | tf_op jit(solution)/shard_map/ppermute | solution.py:714
  (332 shorter events, 72.1 us)
Async XLA Ops:
  7.9 12.1 %collective-permute-start.1 = (bf16[256,768]{1,0:T(8,128)(2,1)S(1)}, bf16[256,768]{1,0:T(8,128)(2,1)S(1)}, u32[]{:S(2)}, u32[]{:S(2)}) collective-permute-start(bf16[256,768]{1,0:T(8,128)(2,1)S(1)} %get-tuple-element.184.x0.refs_0_), channel_id=1, source_target_pairs={{0,2},{1,3},{2,0},{3,1},{4,6},{5,7},{6,4},{7,5},{8,10},{9,11},{10,... | collective-permute-start | bytes 1179656 | tf_op jit(solution)/shard_map/ppermute | solution.py:63
  10.9 9.1 %collective-permute-start = (bf16[256,768]{1,0:T(8,128)(2,1)S(1)}, bf16[256,768]{1,0:T(8,128)(2,1)S(1)}, u32[]{:S(2)}, u32[]{:S(2)}) collective-permute-start(bf16[256,768]{1,0:T(8,128)(2,1)S(1)} %get-tuple-element.184.x0.refs_0_), channel_id=1, source_target_pairs={{0,1},{1,0},{2,3},{3,2},{4,5},{5,4},{6,7},{7,6},{8,9},{9,8},{10,11... | collective-permute-start | bytes 1179656 | tf_op jit(solution)/shard_map/ppermute | solution.py:59
  31.3 3.5 collective-permute-start.3
  32.9 11.2 %collective-permute-start.5 = (bf16[256,768]{1,0:T(8,128)(2,1)S(1)}, bf16[256,768]{1,0:T(8,128)(2,1)S(1)}, u32[]{:S(2)}, u32[]{:S(2)}) collective-permute-start(bf16[256,768]{1,0:T(8,128)(2,1)S(1)} %add.69), channel_id=1, source_target_pairs={{0,2},{1,3},{2,0},{3,1},{4,6},{5,7},{6,4},{7,5},{8,10},{9,11},{10,... | collective-permute-start | bytes 1179656 | tf_op jit(solution)/shard_map/ppermute | solution.py:63
  44.7 10.4 %collective-permute-start.7 = (bf16[256,768]{1,0:T(8,128)(2,1)S(1)}, bf16[256,768]{1,0:T(8,128)(2,1)S(1)}, u32[]{:S(2)}, u32[]{:S(2)}) collective-permute-start(bf16[256,768]{1,0:T(8,128)(2,1)S(1)} %get-tuple-element.193.c0.refs_0_), channel_id=1, source_target_pairs={{0,2},{1,3},{2,0},{3,1},{4,6},{5,7},{6,4},{7,5},{8,10},{9,11},{10,... | collective-permute-start | bytes 1179656 | tf_op jit(solution)/shard_map/ppermute | solution.py:63
  46.5 8.6 %collective-permute-start.6 = (bf16[256,768]{1,0:T(8,128)(2,1)S(1)}, bf16[256,768]{1,0:T(8,128)(2,1)S(1)}, u32[]{:S(2)}, u32[]{:S(2)}) collective-permute-start(bf16[256,768]{1,0:T(8,128)(2,1)S(1)} %get-tuple-element.193.c0.refs_0_), channel_id=1, source_target_pairs={{0,1},{1,0},{2,3},{3,2},{4,5},{5,4},{6,7},{7,6},{8,9},{9,8},{10,11... | collective-permute-start | bytes 1179656 | tf_op jit(solution)/shard_map/ppermute | solution.py:59
  61.9 3.5 collective-permute-start.9
  63.6 11.2 %collective-permute-start.11 = (bf16[256,768]{1,0:T(8,128)(2,1)S(1)}, bf16[256,768]{1,0:T(8,128)(2,1)S(1)}, u32[]{:S(2)}, u32[]{:S(2)}) collective-permute-start(bf16[256,768]{1,0:T(8,128)(2,1)S(1)} %add.70), channel_id=1, source_target_pairs={{0,2},{1,3},{2,0},{3,1},{4,6},{5,7},{6,4},{7,5},{8,10},{9,11},{10,... | collective-permute-start | bytes 1179656 | tf_op jit(solution)/shard_map/ppermute | solution.py:63
  75.3 10.4 %collective-permute-start.13 = (bf16[256,768]{1,0:T(8,128)(2,1)S(1)}, bf16[256,768]{1,0:T(8,128)(2,1)S(1)}, u32[]{:S(2)}, u32[]{:S(2)}) collective-permute-start(bf16[256,768]{1,0:T(8,128)(2,1)S(1)} %get-tuple-element.199.x0.refs_0_), channel_id=1, source_target_pairs={{0,2},{1,3},{2,0},{3,1},{4,6},{5,7},{6,4},{7,5},{8,10},{9,11},{10,... | collective-permute-start | bytes 1179656 | tf_op jit(solution)/shard_map/ppermute | solution.py:63
  77.1 8.6 %collective-permute-start.12 = (bf16[256,768]{1,0:T(8,128)(2,1)S(1)}, bf16[256,768]{1,0:T(8,128)(2,1)S(1)}, u32[]{:S(2)}, u32[]{:S(2)}) collective-permute-start(bf16[256,768]{1,0:T(8,128)(2,1)S(1)} %get-tuple-element.199.x0.refs_0_), channel_id=1, source_target_pairs={{0,1},{1,0},{2,3},{3,2},{4,5},{5,4},{6,7},{7,6},{8,9},{9,8},{10,11... | collective-permute-start | bytes 1179656 | tf_op jit(solution)/shard_map/ppermute | solution.py:59
  94.0 3.8 %collective-permute-start.15 = (bf16[256,768]{1,0:T(8,128)(2,1)S(1)}, bf16[256,768]{1,0:T(8,128)(2,1)S(1)}, u32[]{:S(2)}, u32[]{:S(2)}) collective-permute-start(bf16[256,768]{1,0:T(8,128)(2,1)S(1)} %get-tuple-element.201), channel_id=1, source_target_pairs={{0,1},{1,0},{2,3},{3,2},{4,5},{5,4},{6,7},{7,6},{8,9},{9,8},{10,11... | collective-permute-start | bytes 1179656 | tf_op jit(solution)/shard_map/ppermute | solution.py:59
  95.7 12.0 %collective-permute-start.17 = (bf16[256,768]{1,0:T(8,128)(2,1)S(1)}, bf16[256,768]{1,0:T(8,128)(2,1)S(1)}, u32[]{:S(2)}, u32[]{:S(2)}) collective-permute-start(bf16[256,768]{1,0:T(8,128)(2,1)S(1)} %add.71), channel_id=1, source_target_pairs={{0,2},{1,3},{2,0},{3,1},{4,6},{5,7},{6,4},{7,5},{8,10},{9,11},{10,... | collective-permute-start | bytes 1179656 | tf_op jit(solution)/shard_map/ppermute | solution.py:63
  97.5 18.8 %collective-permute-start.22 = (bf16[256,768]{1,0:T(8,128)(2,1)S(1)}, bf16[256,768]{1,0:T(8,128)(2,1)}, u32[]{:S(2)}, u32[]{:S(2)}) collective-permute-start(bf16[256,768]{1,0:T(8,128)(2,1)S(1)} %get-tuple-element.207.refs_4_.grad_ref), channel_id=1, source_target_pairs={{0,2},{1,3},{2,0},{3,1},{4,6},{5,7},{6,4},{7,5},{8,10},{9,11},{10,... | collective-permute-start | bytes 1179656 | tf_op jit(solution)/shard_map/ppermute | solution.py:63
  109.8 14.1 %collective-permute-start.19 = (bf16[256,768]{1,0:T(8,128)(2,1)}, bf16[256,768]{1,0:T(8,128)(2,1)}, u32[]{:S(2)}, u32[]{:S(2)}) collective-permute-start(bf16[256,768]{1,0:T(8,128)(2,1)} %get-tuple-element.205.refs_0_), channel_id=1, source_target_pairs={{0,2},{1,3},{2,0},{3,1},{4,6},{5,7},{6,4},{7,5},{8,10},{9,11},{10,... | collective-permute-start | bytes 1179656 | tf_op jit(solution)/shard_map/ppermute | solution.py:63
  111.5 12.4 %collective-permute-start.21 = (bf16[256,768]{1,0:T(8,128)(2,1)S(1)}, bf16[256,768]{1,0:T(8,128)(2,1)}, u32[]{:S(2)}, u32[]{:S(2)}) collective-permute-start(bf16[256,768]{1,0:T(8,128)(2,1)S(1)} %get-tuple-element.207.refs_4_.grad_ref), channel_id=1, source_target_pairs={{0,1},{1,0},{2,3},{3,2},{4,5},{5,4},{6,7},{7,6},{8,9},{9,8},{10,11... | collective-permute-start | bytes 1179656 | tf_op jit(solution)/shard_map/ppermute | solution.py:59
  116.3 7.6 %collective-permute-start.23 = (bf16[256,768]{1,0:T(8,128)(2,1)}, bf16[256,768]{1,0:T(8,128)(2,1)}, u32[]{:S(2)}, u32[]{:S(2)}) collective-permute-start(bf16[256,768]{1,0:T(8,128)(2,1)} %collective-permute-done.22.refs_6_), channel_id=1, source_target_pairs={{0,1},{1,0},{2,3},{3,2},{4,5},{5,4},{6,7},{7,6},{8,9},{9,8},{10,11... | collective-permute-start | bytes 1179656 | tf_op jit(solution)/shard_map/ppermute | solution.py:59
  116.3 7.6 %collective-permute-start.18 = (bf16[256,768]{1,0:T(8,128)(2,1)}, bf16[256,768]{1,0:T(8,128)(2,1)}, u32[]{:S(2)}, u32[]{:S(2)}) collective-permute-start(bf16[256,768]{1,0:T(8,128)(2,1)} %get-tuple-element.205.refs_0_), channel_id=1, source_target_pairs={{0,1},{1,0},{2,3},{3,2},{4,5},{5,4},{6,7},{7,6},{8,9},{9,8},{10,11... | collective-permute-start | bytes 1179656 | tf_op jit(solution)/shard_map/ppermute | solution.py:59
  138.2 17.2 %collective-permute-start.29 = (bf16[768,768]{1,0:T(8,128)(2,1)S(1)}, bf16[768,768]{1,0:T(8,128)(2,1)S(1)}, u32[]{:S(2)}, u32[]{:S(2)}) collective-permute-start(bf16[768,768]{1,0:T(8,128)(2,1)S(1)} %get-tuple-element.221), channel_id=1, source_target_pairs={{0,4},{1,9},{2,6},{3,11},{4,0},{5,13},{6,2},{7,15},{8,12},{9,1},{1... | collective-permute-start | bytes 3538952 | tf_op jit(solution)/shard_map/ppermute | solution.py:714
  140.2 11.4 %collective-permute-start.26 = (bf16[256,768]{1,0:T(8,128)(2,1)S(1)}, bf16[256,768]{1,0:T(8,128)(2,1)S(1)}, u32[]{:S(2)}, u32[]{:S(2)}) collective-permute-start(bf16[256,768]{1,0:T(8,128)(2,1)S(1)} %add.72), channel_id=1, source_target_pairs={{0,2},{1,3},{2,0},{3,1},{4,6},{5,7},{6,4},{7,5},{8,10},{9,11},{10,... | collective-permute-start | bytes 1179656 | tf_op jit(solution)/shard_map/ppermute | solution.py:63
  152.3 10.6 %collective-permute-start.28 = (bf16[256,768]{1,0:T(8,128)(2,1)S(1)}, bf16[256,768]{1,0:T(8,128)(2,1)S(1)}, u32[]{:S(2)}, u32[]{:S(2)}) collective-permute-start(bf16[256,768]{1,0:T(8,128)(2,1)S(1)} %get-tuple-element.213.g0.refs_4_), channel_id=1, source_target_pairs={{0,2},{1,3},{2,0},{3,1},{4,6},{5,7},{6,4},{7,5},{8,10},{9,11},{10,... | collective-permute-start | bytes 1179656 | tf_op jit(solution)/shard_map/ppermute | solution.py:63
  153.9 9.0 %collective-permute-start.27 = (bf16[256,768]{1,0:T(8,128)(2,1)S(1)}, bf16[256,768]{1,0:T(8,128)(2,1)S(1)}, u32[]{:S(2)}, u32[]{:S(2)}) collective-permute-start(bf16[256,768]{1,0:T(8,128)(2,1)S(1)} %get-tuple-element.213.g0.refs_4_), channel_id=1, source_target_pairs={{0,1},{1,0},{2,3},{3,2},{4,5},{5,4},{6,7},{7,6},{8,9},{9,8},{10,11... | collective-permute-start | bytes 1179656 | tf_op jit(solution)/shard_map/ppermute | solution.py:59
  171.5 11.1 %collective-permute-start.34 = (bf16[384,768]{1,0:T(8,128)(2,1)S(1)}, bf16[384,768]{1,0:T(8,128)(2,1)S(1)}, u32[]{:S(2)}, u32[]{:S(2)}) collective-permute-start(bf16[384,768]{1,0:T(8,128)(2,1)S(1)} %get-tuple-element.223), channel_id=1, source_target_pairs={{0,8},{1,5},{2,10},{3,7},{4,12},{5,1},{6,14},{7,3},{8,0},{9,13},{1... | collective-permute-start | bytes 1769480 | tf_op jit(solution)/shard_map/ppermute | solution.py:714
  173.4 11.1 %collective-permute-start.33 = (bf16[256,768]{1,0:T(8,128)(2,1)S(1)}, bf16[256,768]{1,0:T(8,128)(2,1)S(1)}, u32[]{:S(2)}, u32[]{:S(2)}) collective-permute-start(bf16[256,768]{1,0:T(8,128)(2,1)S(1)} %add.73), channel_id=1, source_target_pairs={{0,2},{1,3},{2,0},{3,1},{4,6},{5,7},{6,4},{7,5},{8,10},{9,11},{10,... | collective-permute-start | bytes 1179656 | tf_op jit(solution)/shard_map/ppermute | solution.py:63
  175.0 9.5 %collective-permute-start.31 = (bf16[256,768]{1,0:T(8,128)(2,1)S(1)}, bf16[256,768]{1,0:T(8,128)(2,1)S(1)}, u32[]{:S(2)}, u32[]{:S(2)}) collective-permute-start(bf16[256,768]{1,0:T(8,128)(2,1)S(1)} %get-tuple-element.230), channel_id=1, source_target_pairs={{0,1},{1,0},{2,3},{3,2},{4,5},{5,4},{6,7},{7,6},{8,9},{9,8},{10,11... | collective-permute-start | bytes 1179656 | tf_op jit(solution)/shard_map/ppermute | solution.py:59
  177.0 13.9 %collective-permute-start.37 = (bf16[384,768]{1,0:T(8,128)(2,1)S(1)}, bf16[384,768]{1,0:T(8,128)(2,1)S(1)}, u32[]{:S(2)}, u32[]{:S(2)}) collective-permute-start(bf16[384,768]{1,0:T(8,128)(2,1)S(1)} %get-tuple-element.238), channel_id=1, source_target_pairs={{0,4},{1,9},{2,6},{3,11},{4,0},{5,13},{6,2},{7,15},{8,12},{9,1},{1... | collective-permute-start | bytes 1769480 | tf_op jit(solution)/shard_map/ppermute | solution.py:714
  185.2 10.2 %collective-permute-start.36 = (bf16[256,768]{1,0:T(8,128)(2,1)S(1)}, bf16[256,768]{1,0:T(8,128)(2,1)S(1)}, u32[]{:S(2)}, u32[]{:S(2)}) collective-permute-start(bf16[256,768]{1,0:T(8,128)(2,1)S(1)} %get-tuple-element.242.g0.refs_4_), channel_id=1, source_target_pairs={{0,2},{1,3},{2,0},{3,1},{4,6},{5,7},{6,4},{7,5},{8,10},{9,11},{10,... | collective-permute-start | bytes 1179656 | tf_op jit(solution)/shard_map/ppermute | solution.py:63
  186.8 8.7 %collective-permute-start.35 = (bf16[256,768]{1,0:T(8,128)(2,1)S(1)}, bf16[256,768]{1,0:T(8,128)(2,1)S(1)}, u32[]{:S(2)}, u32[]{:S(2)}) collective-permute-start(bf16[256,768]{1,0:T(8,128)(2,1)S(1)} %get-tuple-element.242.g0.refs_4_), channel_id=1, source_target_pairs={{0,1},{1,0},{2,3},{3,2},{4,5},{5,4},{6,7},{7,6},{8,9},{9,8},{10,11... | collective-permute-start | bytes 1179656 | tf_op jit(solution)/shard_map/ppermute | solution.py:59
  202.0 11.8 %collective-permute-start.41 = (bf16[256,768]{1,0:T(8,128)(2,1)S(1)}, bf16[256,768]{1,0:T(8,128)(2,1)S(1)}, u32[]{:S(2)}, u32[]{:S(2)}) collective-permute-start(bf16[256,768]{1,0:T(8,128)(2,1)S(1)} %add.75), channel_id=1, source_target_pairs={{0,2},{1,3},{2,0},{3,1},{4,6},{5,7},{6,4},{7,5},{8,10},{9,11},{10,... | collective-permute-start | bytes 1179656 | tf_op jit(solution)/shard_map/ppermute | solution.py:63
  203.6 10.2 %collective-permute-start.39 = (bf16[256,768]{1,0:T(8,128)(2,1)S(1)}, bf16[256,768]{1,0:T(8,128)(2,1)S(1)}, u32[]{:S(2)}, u32[]{:S(2)}) collective-permute-start(bf16[256,768]{1,0:T(8,128)(2,1)S(1)} %get-tuple-element.251), channel_id=1, source_target_pairs={{0,1},{1,0},{2,3},{3,2},{4,5},{5,4},{6,7},{7,6},{8,9},{9,8},{10,11... | collective-permute-start | bytes 1179656 | tf_op jit(solution)/shard_map/ppermute | solution.py:59
  203.6 10.1 %collective-permute-start.42 = (bf16[192,768]{1,0:T(8,128)(2,1)S(1)}, bf16[192,768]{1,0:T(8,128)(2,1)S(1)}, u32[]{:S(2)}, u32[]{:S(2)}) collective-permute-start(bf16[192,768]{1,0:T(8,128)(2,1)S(1)} %get-tuple-element.247), channel_id=1, source_target_pairs={{0,8},{1,5},{2,10},{3,7},{4,12},{5,1},{6,14},{7,3},{8,0},{9,13},{1... | collective-permute-start | bytes 884744 | tf_op jit(solution)/shard_map/ppermute | solution.py:714
  205.5 28.1 %collective-permute-start.46 = (bf16[384,768]{1,0:T(8,128)(2,1)S(1)}, bf16[384,768]{1,0:T(8,128)(2,1)S(1)}, u32[]{:S(2)}, u32[]{:S(2)}) collective-permute-start(bf16[384,768]{1,0:T(8,128)(2,1)S(1)} %add.74), channel_id=1, source_target_pairs={{0,16},{1,17},{2,18},{3,19},{4,20},{5,21},{6,22},{7,23},{8,24},{9,... | collective-permute-start | bytes 1769480 | tf_op jit(solution)/shard_map/ppermute | solution.py:714
  211.5 22.2 %collective-permute-start.45 = (bf16[384,768]{1,0:T(8,128)(2,1)S(1)}, bf16[384,768]{1,0:T(8,128)(2,1)S(1)}, u32[]{:S(2)}, u32[]{:S(2)}) collective-permute-start(bf16[384,768]{1,0:T(8,128)(2,1)S(1)} %get-tuple-element.259), channel_id=1, source_target_pairs={{0,4},{1,9},{2,6},{3,11},{4,0},{5,13},{6,2},{7,15},{8,12},{9,1},{1... | collective-permute-start | bytes 1769480 | tf_op jit(solution)/shard_map/ppermute | solution.py:714
  214.6 19.3 %collective-permute-start.44 = (bf16[256,768]{1,0:T(8,128)(2,1)S(1)}, bf16[256,768]{1,0:T(8,128)(2,1)S(1)}, u32[]{:S(2)}, u32[]{:S(2)}) collective-permute-start(bf16[256,768]{1,0:T(8,128)(2,1)S(1)} %get-tuple-element.264.g0.refs_4_), channel_id=1, source_target_pairs={{0,2},{1,3},{2,0},{3,1},{4,6},{5,7},{6,4},{7,5},{8,10},{9,11},{10,... | collective-permute-start | bytes 1179656 | tf_op jit(solution)/shard_map/ppermute | solution.py:63
  215.6 18.4 %collective-permute-start.43 = (bf16[256,768]{1,0:T(8,128)(2,1)S(1)}, bf16[256,768]{1,0:T(8,128)(2,1)S(1)}, u32[]{:S(2)}, u32[]{:S(2)}) collective-permute-start(bf16[256,768]{1,0:T(8,128)(2,1)S(1)} %get-tuple-element.264.g0.refs_4_), channel_id=1, source_target_pairs={{0,1},{1,0},{2,3},{3,2},{4,5},{5,4},{6,7},{7,6},{8,9},{9,8},{10,11... | collective-permute-start | bytes 1179656 | tf_op jit(solution)/shard_map/ppermute | solution.py:59
  242.1 5.3 %collective-permute-start.49 = (bf16[256,768]{1,0:T(8,128)(2,1)S(1)}, bf16[256,768]{1,0:T(8,128)(2,1)S(1)}, u32[]{:S(2)}, u32[]{:S(2)}) collective-permute-start(bf16[256,768]{1,0:T(8,128)(2,1)S(1)} %get-tuple-element.278), channel_id=1, source_target_pairs={{0,1},{1,0},{2,3},{3,2},{4,5},{5,4},{6,7},{7,6},{8,9},{9,8},{10,11... | collective-permute-start | bytes 1179656 | tf_op jit(solution)/shard_map/ppermute | solution.py:59
  242.3 21.1 %collective-permute-start.53 = (bf16[384,768]{1,0:T(8,128)(2,1)S(1)}, bf16[384,768]{1,0:T(8,128)(2,1)S(1)}, u32[]{:S(2)}, u32[]{:S(2)}) collective-permute-start(bf16[384,768]{1,0:T(8,128)(2,1)S(1)} %add.77.own_ref), channel_id=1, source_target_pairs={{0,8},{1,5},{2,10},{3,7},{4,12},{5,1},{6,14},{7,3},{8,0},{9,13},{1... | collective-permute-start | bytes 1769480 | tf_op jit(solution)/shard_map/ppermute | solution.py:714
  243.1 20.0 %collective-permute-start.51 = (bf16[192,768]{1,0:T(8,128)(2,1)S(1)}, bf16[192,768]{1,0:T(8,128)(2,1)S(1)}, u32[]{:S(2)}, u32[]{:S(2)}) collective-permute-start(bf16[192,768]{1,0:T(8,128)(2,1)S(1)} %add.76), channel_id=1, source_target_pairs={{0,16},{1,17},{2,18},{3,19},{4,20},{5,21},{6,22},{7,23},{8,24},{9,... | collective-permute-start | bytes 884744 | tf_op jit(solution)/shard_map/ppermute | solution.py:714
  246.5 20.4 %collective-permute-start.52 = (bf16[384,768]{1,0:T(8,128)(2,1)S(1)}, bf16[384,768]{1,0:T(8,128)(2,1)S(1)}, u32[]{:S(2)}, u32[]{:S(2)}) collective-permute-start(bf16[384,768]{1,0:T(8,128)(2,1)S(1)} %get-tuple-element.261), channel_id=1, source_target_pairs={{0,4},{1,9},{2,6},{3,11},{4,0},{5,13},{6,2},{7,15},{8,12},{9,1},{1... | collective-permute-start | bytes 1769480 | tf_op jit(solution)/shard_map/ppermute | solution.py:714
  249.8 25.0 %collective-permute-start.55 = (bf16[384,768]{1,0:T(8,128)(2,1)S(1)}, bf16[384,768]{1,0:T(8,128)(2,1)S(1)}, u32[]{:S(2)}, u32[]{:S(2)}) collective-permute-start(bf16[384,768]{1,0:T(8,128)(2,1)S(1)} %get-tuple-element.283), channel_id=1, source_target_pairs={{0,4},{1,9},{2,6},{3,11},{4,0},{5,13},{6,2},{7,15},{8,12},{9,1},{1... | collective-permute-start | bytes 1769480 | tf_op jit(solution)/shard_map/ppermute | solution.py:714
  251.0 17.0 %collective-permute-start.50 = (bf16[256,768]{1,0:T(8,128)(2,1)S(1)}, bf16[256,768]{1,0:T(8,128)(2,1)S(1)}, u32[]{:S(2)}, u32[]{:S(2)}) collective-permute-start(bf16[256,768]{1,0:T(8,128)(2,1)S(1)} %add.78), channel_id=1, source_target_pairs={{0,2},{1,3},{2,0},{3,1},{4,6},{5,7},{6,4},{7,5},{8,10},{9,11},{10,... | collective-permute-start | bytes 1179656 | tf_op jit(solution)/shard_map/ppermute | solution.py:63
  263.2 4.8 %collective-permute-start.48 = (bf16[256,768]{1,0:T(8,128)(2,1)S(1)}, bf16[256,768]{1,0:T(8,128)(2,1)S(1)}, u32[]{:S(2)}, u32[]{:S(2)}) collective-permute-start(bf16[256,768]{1,0:T(8,128)(2,1)S(1)} %get-tuple-element.276), channel_id=1, source_target_pairs={{0,1},{1,0},{2,3},{3,2},{4,5},{5,4},{6,7},{7,6},{8,9},{9,8},{10,11... | collective-permute-start | bytes 1179656 | tf_op jit(solution)/shard_map/ppermute | solution.py:59
  263.4 11.2 %collective-permute-start.56 = (bf16[192,768]{1,0:T(8,128)(2,1)S(1)}, bf16[192,768]{1,0:T(8,128)(2,1)S(1)}, u32[]{:S(2)}, u32[]{:S(2)}) collective-permute-start(bf16[192,768]{1,0:T(8,128)(2,1)S(1)} %get-tuple-element.267), channel_id=1, source_target_pairs={{0,8},{1,5},{2,10},{3,7},{4,12},{5,1},{6,14},{7,3},{8,0},{9,13},{1... | collective-permute-start | bytes 884744 | tf_op jit(solution)/shard_map/ppermute | solution.py:714
  266.9 66.0 %collective-permute-start.70 = (bf16[768,768]{1,0:T(8,128)(2,1)S(1)}, bf16[768,768]{1,0:T(8,128)(2,1)S(1)}, u32[]{:S(2)}, u32[]{:S(2)}) collective-permute-start(bf16[768,768]{1,0:T(8,128)(2,1)S(1)} %join.5.own_ref), channel_id=1, source_target_pairs={{0,4},{1,9},{2,6},{3,11},{4,0},{5,13},{6,2},{7,15},{8,12},{9,1},{1... | collective-permute-start | bytes 3538952 | tf_op jit(solution)/shard_map/ppermute | solution.py:714
  270.0 5.0 %collective-permute-start.54 = (f32[16,768]{1,0:T(8,128)S(1)}, f32[16,768]{1,0:T(8,128)S(1)}, u32[]{:S(2)}, u32[]{:S(2)}) collective-permute-start(f32[16,768]{1,0:T(8,128)S(1)} %pack_rows.1), channel_id=1, source_target_pairs={{0,1},{1,0},{2,3},{3,2},{4,5},{5,4},{6,7},{7,6},{8,9},{9,8},{10,11... | collective-permute-start | bytes 147464 | tf_op jit(solution)/shard_map/ppermute | solution.py:979
  279.0 17.4 %collective-permute-start.58 = (bf16[256,768]{1,0:T(8,128)(2,1)S(1)}, bf16[256,768]{1,0:T(8,128)(2,1)S(1)}, u32[]{:S(2)}, u32[]{:S(2)}) collective-permute-start(bf16[256,768]{1,0:T(8,128)(2,1)S(1)} %get-tuple-element.303), channel_id=1, source_target_pairs={{0,1},{1,0},{2,3},{3,2},{4,5},{5,4},{6,7},{7,6},{8,9},{9,8},{10,11... | collective-permute-start | bytes 1179656 | tf_op jit(solution)/shard_map/ppermute | solution.py:59
  279.1 16.3 %collective-permute-start.61 = (bf16[192,768]{1,0:T(8,128)(2,1)S(1)}, bf16[192,768]{1,0:T(8,128)(2,1)S(1)}, u32[]{:S(2)}, u32[]{:S(2)}) collective-permute-start(bf16[192,768]{1,0:T(8,128)(2,1)S(1)} %get-tuple-element.286), channel_id=1, source_target_pairs={{0,8},{1,5},{2,10},{3,7},{4,12},{5,1},{6,14},{7,3},{8,0},{9,13},{1... | collective-permute-start | bytes 884744 | tf_op jit(solution)/shard_map/ppermute | solution.py:714
  281.1 16.0 %collective-permute-start.64 = (bf16[192,768]{1,0:T(8,128)(2,1)S(1)}, bf16[192,768]{1,0:T(8,128)(2,1)S(1)}, u32[]{:S(2)}, u32[]{:S(2)}) collective-permute-start(bf16[192,768]{1,0:T(8,128)(2,1)S(1)} %add.80), channel_id=1, source_target_pairs={{0,16},{1,17},{2,18},{3,19},{4,20},{5,21},{6,22},{7,23},{8,24},{9,... | collective-permute-start | bytes 884744 | tf_op jit(solution)/shard_map/ppermute | solution.py:714
  283.3 12.2 %collective-permute-start.60 = (f32[16,768]{1,0:T(8,128)S(1)}, f32[16,768]{1,0:T(8,128)S(1)}, u32[]{:S(2)}, u32[]{:S(2)}) collective-permute-start(f32[16,768]{1,0:T(8,128)S(1)} %add.81), channel_id=1, source_target_pairs={{0,2},{1,3},{2,0},{3,1},{4,6},{5,7},{6,4},{7,5},{8,10},{9,11},{10,... | collective-permute-start | bytes 147464 | tf_op jit(solution)/shard_map/ppermute | solution.py:979
  295.4 7.9 %collective-permute-start.63 = (bf16[192,768]{1,0:T(8,128)(2,1)S(1)}, bf16[192,768]{1,0:T(8,128)(2,1)S(1)}, u32[]{:S(2)}, u32[]{:S(2)}) collective-permute-start(bf16[192,768]{1,0:T(8,128)(2,1)S(1)} %get-tuple-element.297), channel_id=1, source_target_pairs={{0,8},{1,5},{2,10},{3,7},{4,12},{5,1},{6,14},{7,3},{8,0},{9,13},{1... | collective-permute-start | bytes 884744 | tf_op jit(solution)/shard_map/ppermute | solution.py:714
  295.6 5.7 %collective-permute-start.62 = (f32[48,768]{1,0:T(8,128)S(1)}, f32[48,768]{1,0:T(8,128)S(1)}, u32[]{:S(2)}, u32[]{:S(2)}) collective-permute-start(f32[48,768]{1,0:T(8,128)S(1)} %pack_all.1), channel_id=1, source_target_pairs={{0,4},{4,0},{8,12},{12,8},{16,20},{20,16},{24,28},{28,24},{1,5},{5... | collective-permute-start | bytes 442376 | tf_op jit(solution)/shard_map/ppermute | solution.py:979
  296.5 8.2 %collective-permute-start.59 = (bf16[256,768]{1,0:T(8,128)(2,1)S(1)}, bf16[256,768]{1,0:T(8,128)(2,1)S(1)}, u32[]{:S(2)}, u32[]{:S(2)}) collective-permute-start(bf16[256,768]{1,0:T(8,128)(2,1)S(1)} %add.82), channel_id=1, source_target_pairs={{0,2},{1,3},{2,0},{3,1},{4,6},{5,7},{6,4},{7,5},{8,10},{9,11},{10,... | collective-permute-start | bytes 1179656 | tf_op jit(solution)/shard_map/ppermute | solution.py:63
  297.1 10.0 %collective-permute-start.57 = (bf16[256,768]{1,0:T(8,128)(2,1)S(1)}, bf16[256,768]{1,0:T(8,128)(2,1)S(1)}, u32[]{:S(2)}, u32[]{:S(2)}) collective-permute-start(bf16[256,768]{1,0:T(8,128)(2,1)S(1)} %get-tuple-element.301), channel_id=1, source_target_pairs={{0,1},{1,0},{2,3},{3,2},{4,5},{5,4},{6,7},{7,6},{8,9},{9,8},{10,11... | collective-permute-start | bytes 1179656 | tf_op jit(solution)/shard_map/ppermute | solution.py:59
  301.3 9.5 %collective-permute-start.67 = (bf16[192,768]{1,0:T(8,128)(2,1)S(1)}, bf16[192,768]{1,0:T(8,128)(2,1)S(1)}, u32[]{:S(2)}, u32[]{:S(2)}) collective-permute-start(bf16[192,768]{1,0:T(8,128)(2,1)S(1)} %add.79.own_ref), channel_id=1, source_target_pairs={{0,8},{1,5},{2,10},{3,7},{4,12},{5,1},{6,14},{7,3},{8,0},{9,13},{1... | collective-permute-start | bytes 884744 | tf_op jit(solution)/shard_map/ppermute | solution.py:714
  303.3 15.6 %collective-permute-start.66 = (bf16[192,768]{1,0:T(8,128)(2,1)S(1)}, bf16[192,768]{1,0:T(8,128)(2,1)S(1)}, u32[]{:S(2)}, u32[]{:S(2)}) collective-permute-start(bf16[192,768]{1,0:T(8,128)(2,1)S(1)} %add.83), channel_id=1, source_target_pairs={{0,16},{1,17},{2,18},{3,19},{4,20},{5,21},{6,22},{7,23},{8,24},{9,... | collective-permute-start | bytes 884744 | tf_op jit(solution)/shard_map/ppermute | solution.py:714
  304.7 28.1 %collective-permute-start.71 = (bf16[192,768]{1,0:T(8,128)(2,1)S(1)}, bf16[192,768]{1,0:T(8,128)(2,1)S(1)}, u32[]{:S(2)}, u32[]{:S(2)}) collective-permute-start(bf16[192,768]{1,0:T(8,128)(2,1)S(1)} %add.85.own_ref), channel_id=1, source_target_pairs={{0,8},{1,5},{2,10},{3,7},{4,12},{5,1},{6,14},{7,3},{8,0},{9,13},{1... | collective-permute-start | bytes 884744 | tf_op jit(solution)/shard_map/ppermute | solution.py:714
  307.1 28.3 %collective-permute-start.69 = (bf16[192,768]{1,0:T(8,128)(2,1)S(1)}, bf16[192,768]{1,0:T(8,128)(2,1)S(1)}, u32[]{:S(2)}, u32[]{:S(2)}) collective-permute-start(bf16[192,768]{1,0:T(8,128)(2,1)S(1)} %add.86), channel_id=1, source_target_pairs={{0,16},{1,17},{2,18},{3,19},{4,20},{5,21},{6,22},{7,23},{8,24},{9,... | collective-permute-start | bytes 884744 | tf_op jit(solution)/shard_map/ppermute | solution.py:714
  310.8 36.9 %collective-permute-start.73 = (bf16[384,768]{1,0:T(8,128)(2,1)S(1)}, bf16[384,768]{1,0:T(8,128)(2,1)S(1)}, u32[]{:S(2)}, u32[]{:S(2)}) collective-permute-start(bf16[384,768]{1,0:T(8,128)(2,1)S(1)} %join.6.own_ref), channel_id=1, source_target_pairs={{0,4},{1,9},{2,6},{3,11},{4,0},{5,13},{6,2},{7,15},{8,12},{9,1},{1... | collective-permute-start | bytes 1769480 | tf_op jit(solution)/shard_map/ppermute | solution.py:714
  318.9 11.4 %collective-permute-start.65 = (f32[48,768]{1,0:T(8,128)S(1)}, f32[48,768]{1,0:T(8,128)S(1)}, u32[]{:S(2)}, u32[]{:S(2)}) collective-permute-start(f32[48,768]{1,0:T(8,128)S(1)} %add.87), channel_id=1, source_target_pairs={{0,8},{4,12},{8,0},{12,4},{16,24},{20,28},{24,16},{28,20},{1,9},{5... | collective-permute-start | bytes 442376 | tf_op jit(solution)/shard_map/ppermute | solution.py:979
  330.3 16.2 %collective-permute-start.74 = (bf16[192,768]{1,0:T(8,128)(2,1)S(1)}, bf16[192,768]{1,0:T(8,128)(2,1)S(1)}, u32[]{:S(2)}, u32[]{:S(2)}) collective-permute-start(bf16[192,768]{1,0:T(8,128)(2,1)S(1)} %add.88.own_ref), channel_id=1, source_target_pairs={{0,8},{1,5},{2,10},{3,7},{4,12},{5,1},{6,14},{7,3},{8,0},{9,13},{1... | collective-permute-start | bytes 884744 | tf_op jit(solution)/shard_map/ppermute | solution.py:714
  335.5 13.8 %collective-permute-start.72 = (bf16[192,768]{1,0:T(8,128)(2,1)S(1)}, bf16[192,768]{1,0:T(8,128)(2,1)S(1)}, u32[]{:S(2)}, u32[]{:S(2)}) collective-permute-start(bf16[192,768]{1,0:T(8,128)(2,1)S(1)} %add.90.own_ref), channel_id=1, source_target_pairs={{0,8},{1,5},{2,10},{3,7},{4,12},{5,1},{6,14},{7,3},{8,0},{9,13},{1... | collective-permute-start | bytes 884744 | tf_op jit(solution)/shard_map/ppermute | solution.py:714
  335.6 10.9 %collective-permute-start.68 = (f32[48,768]{1,0:T(8,128)S(1)}, f32[48,768]{1,0:T(8,128)S(1)}, u32[]{:S(2)}, u32[]{:S(2)}) collective-permute-start(f32[48,768]{1,0:T(8,128)S(1)} %add.89), channel_id=1, source_target_pairs={{0,16},{4,20},{8,24},{12,28},{16,0},{20,4},{24,8},{28,12},{1,17},{... | collective-permute-start | bytes 442376 | tf_op jit(solution)/shard_map/ppermute | solution.py:979
  337.3 14.4 %collective-permute-start.77 = (bf16[384,768]{1,0:T(8,128)(2,1)S(1)}, bf16[384,768]{1,0:T(8,128)(2,1)S(1)}, u32[]{:S(2)}, u32[]{:S(2)}) collective-permute-start(bf16[384,768]{1,0:T(8,128)(2,1)S(1)} %join.7.own_ref), channel_id=1, source_target_pairs={{0,4},{1,9},{2,6},{3,11},{4,0},{5,13},{6,2},{7,15},{8,12},{9,1},{1... | collective-permute-start | bytes 1769480 | tf_op jit(solution)/shard_map/ppermute | solution.py:714
  346.6 9.9 %collective-permute-start.76 = (bf16[384,768]{1,0:T(8,128)(2,1)S(1)}, bf16[384,768]{1,0:T(8,128)(2,1)S(1)}, u32[]{:S(2)}, u32[]{:S(2)}) collective-permute-start(bf16[384,768]{1,0:T(8,128)(2,1)S(1)} %join.8.own_ref), channel_id=1, source_target_pairs={{0,4},{1,9},{2,6},{3,11},{4,0},{5,13},{6,2},{7,15},{8,12},{9,1},{1... | collective-permute-start | bytes 1769480 | tf_op jit(solution)/shard_map/ppermute | solution.py:714
  349.4 13.4 %collective-permute-start.75 = (bf16[384,768]{1,0:T(8,128)(2,1)S(1)}, bf16[384,768]{1,0:T(8,128)(2,1)S(1)}, u32[]{:S(2)}, u32[]{:S(2)}) collective-permute-start(bf16[384,768]{1,0:T(8,128)(2,1)S(1)} %join.9.own_ref), channel_id=1, source_target_pairs={{0,4},{1,9},{2,6},{3,11},{4,0},{5,13},{6,2},{7,15},{8,12},{9,1},{1... | collective-permute-start | bytes 1769480 | tf_op jit(solution)/shard_map/ppermute | solution.py:714
  (101 other events, 1059.3 us)

commit v4 on v3

--- a/solution.py
+++ b/solution.py
@@ -368,53 +368,120 @@
     return [jnp.where((lane // HEAD_DIM) == h, 1.0, 0.0).astype(kind) for h in range(heads)]
 
 
-def attention_kernel(
-    layer, x0, x1, x2, x3, w_ref, bias_ref, rel_ref, pad_ref, wo_ref, p0, p1, p2, p3, q_ref, k_ref, v_ref, pb_ref, o_ref
-):
-    pages = pad_ref.shape[0]
-    heads = rel_ref.shape[1]
-    size = x0.shape[0] // pages
+def project_rows(layer, rows, w_ref, bias_ref):
+    q = ((mxu(rows, w_ref[layer, 0], NT) + bias_ref[layer, 0:1, :].astype(F32)) * HEAD_DIM**-0.5).astype(BF)
+    k = mxu(rows, w_ref[layer, 1], NT).astype(BF)
+    v = (mxu(rows, w_ref[layer, 2], NT) + bias_ref[layer, 1:2, :].astype(F32)).astype(BF)
+    return q, k, v
+
+
+def project_pair(layer, x0, x1, w_ref, bias_ref, outs):
+    size = x0.shape[0]
+    rows = jnp.concatenate([x0[...], x1[...]], axis=0)
+    for out_ref, made in zip(outs, project_rows(layer, rows, w_ref, bias_ref)):
+        out_ref[0], out_ref[1] = made[:size], made[size:]
+
+
+def project_kernel(layer, x0, x1, w_ref, bias_ref, q_ref, k_ref, v_ref):
+    project_pair(layer, x0, x1, w_ref, bias_ref, (q_ref, k_ref, v_ref))
+
+
+def project(layer, pair, w_qkv, qv_bias):
+    outs = [shape((2, pair[0].shape[0], w_qkv.shape[2]), BF)] * 3
+    return kernel_call(
+        functools.partial(project_kernel, layer), "project", outs, 1_000_000_000, *pair, w_qkv, qv_bias
+    )
+
+
+def rows_of_page(refs, page, size):
+    at = pl.ds(pl.multiple_of(page * size, size), size)
+    return jnp.concatenate([ref[i, at, :] for ref in refs for i in range(2)], axis=0)
+
+
+def attend(layer, start, q_ref, k_refs, v_refs, rel_ref, pad_ref, wo_ref, out_refs, pb_ref, o_ref):
+    pages, heads, count = pb_ref.shape[:3]
+    size = count // 2
 
     def step(page, carry):
         masks = head_masks(heads, BF)
-        rows = page_rows((x0, x1, x2, x3), page, size)
-        q = ((mxu(rows, w_ref[layer, 0], NT) + bias_ref[layer, 0:1, :].astype(F32)) * HEAD_DIM**-0.5).astype(BF)
-        k = mxu(rows, w_ref[layer, 1], NT).astype(BF)
-        v = (mxu(rows, w_ref[layer, 2], NT) + bias_ref[layer, 1:2, :].astype(F32)).astype(BF)
-        q_ref[page], k_ref[page], v_ref[page] = q, k, v
+        q = rows_of_page((q_ref,), page, size)
+        k, v = rows_of_page(k_refs, page, size), rows_of_page(v_refs, page, size)
         o = jnp.zeros(q.shape, F32)
         for h in range(heads):
-            s = mxu(q * masks[h], k, NT) + (rel_ref[layer, h].astype(F32) + pad_ref[page])
+            rel = rel_ref[layer, h, start : start + count, :].astype(F32)
+            s = mxu(q * masks[h], k, NT) + (rel + pad_ref[page])
             e = jnp.exp(s - jnp.max(s, axis=-1, keepdims=True))
             pb = (e * (1.0 / jnp.sum(e, axis=-1, keepdims=True))).astype(BF)
             pb_ref[page, h] = pb
             o = o + mxu(pb, v * masks[h], NN)
         o = o.astype(BF)
         o_ref[page] = o
-        put_page((p0, p1, p2, p3), page, size, mxu(o, wo_ref[layer], NN).astype(BF))
+        mixed = mxu(o, wo_ref[layer], NN).astype(BF)
+        at = pl.ds(pl.multiple_of(page * size, size), size)
+        out_refs[0][at, :], out_refs[1][at, :] = mixed[:size], mixed[size:]
         return carry
 
     lax.fori_loop(0, pages, step, 0, unroll=2)
 
 
-def attention(layer, blocks, w_qkv, qv_bias, rel_bias, pad_bias, w_out):
+def attention_far_kernel(
+    layer, x2, x3, kn, vn, w_ref, bias_ref, rel_ref, pad_ref, wo_ref, p2, p3, qf, kf, vf, pb_ref, o_ref
+):
+    project_pair(layer, x2, x3, w_ref, bias_ref, (qf, kf, vf))
+    start = rel_ref.shape[2] // 2
+    attend(layer, start, qf, (kn, kf), (vn, vf), rel_ref, pad_ref, wo_ref, (p2, p3), pb_ref, o_ref)
+
+
+def attention_near_kernel(layer, qn, kn, vn, kf, vf, rel_ref, pad_ref, wo_ref, p0, p1, pb_ref, o_ref):
+    attend(layer, 0, qn, (kn, kf), (vn, vf), rel_ref, pad_ref, wo_ref, (p0, p1), pb_ref, o_ref)
+
+
+def attention_outs(block, pad_bias, rel_bias):
     pages, unused, length = pad_bias.shape
     heads = rel_bias.shape[1]
-    local = heads * HEAD_DIM
-    outs = [shape(blocks[0].shape, BF)] * 4 + [shape((pages, length, local), BF)] * 3
-    outs += [shape((pages, heads, length, length), BF), shape((pages, length, local), BF)]
+    outs = [shape((pages, heads, length // 2, length), BF), shape((pages, length // 2, heads * HEAD_DIM), BF)]
+    return [shape(block, BF)] * 2, outs
+
+
+def attention_far(layer, pair, near, w_qkv, qv_bias, rel_bias, pad_bias, w_out):
+    sums, saved = attention_outs(pair[0].shape, pad_bias, rel_bias)
     made = kernel_call(
-        functools.partial(attention_kernel, layer), "attention", outs, 6_000_000_000, *blocks, w_qkv, qv_bias, rel_bias, pad_bias, w_out
-    )
-    return made[:4], made[4:]
+        functools.partial(attention_far_kernel, layer),
+        "attention_far",
+        sums + [shape(near[0].shape, BF)] * 3 + saved,
+        4_000_000_000,
+        *pair,
+        *near[1:],
+        w_qkv,
+        qv_bias,
+        rel_bias,
+        pad_bias,
+        w_out,
+    )
+    return made[:2], made[2:5], made[5:]
+
+
+def attention_near(layer, block, near, far, rel_bias, pad_bias, w_out):
+    sums, saved = attention_outs(block, pad_bias, rel_bias)
+    made = kernel_call(
+        functools.partial(attention_near_kernel, layer),
+        "attention_near",
+        sums + saved,
+        3_000_000_000,
+        *near,
+        *far[1:],
+        rel_bias,
+        pad_bias,
+        w_out,
+    )
+    return made[:2], made[2:]
 
 
 def attention_back_kernel(
-    layer, g0, g1, g2, g3, q_ref, k_ref, v_ref, pb_ref, w_ref, wo_ref, p0, p1, p2, p3, stack_ref, total_ref, sums_ref
+    layer, g0, g1, g2, g3, qn, kn, vn, qf, kf, vf, pbn, pbf, w_ref, wo_ref, p0, p1, p2, p3, stack_ref, total_ref, sums_ref
 ):
-    pages, heads = pb_ref.shape[:2]
+    pages, heads = pbn.shape[:2]
     size = g0.shape[0] // pages
-    local = heads * HEAD_DIM
     total_ref[...] = jnp.zeros(total_ref.shape, F32)
     sums_ref[...] = jnp.zeros(sums_ref.shape, F32)
 
@@ -422,10 +489,10 @@
         masks = head_masks(heads, BF)
         rows = page_rows((g0, g1, g2, g3), page, size)
         go = mxu(rows, wo_ref[layer], NT).astype(BF)
-        q, k, v = q_ref[page], k_ref[page], v_ref[page]
+        q, k, v = [rows_of_page(refs, page, size) for refs in ((qn, qf), (kn, kf), (vn, vf))]
         gq = gk = gv = jnp.zeros(q.shape, F32)
         for h in range(heads):
-            pb = pb_ref[page, h]
+            pb = jnp.concatenate([pbn[page, h], pbf[page, h]], axis=0)
             go_h = go * masks[h]
             gv = gv + mxu(pb, go_h, TN)
             gp = mxu(go_h, v, NT)
@@ -447,19 +514,30 @@
 
 
 def attention_back(layer, blocks, kept, w_qkv, w_out):
-    q, k, v, pb, unused = kept
-    pages, length, local = q.shape
-    heads = pb.shape[1]
+    near, far, (pbn, unused), (pbf, unused) = kept
+    pages, heads, unused, length = pbn.shape
+    local = heads * HEAD_DIM
     outs = [shape(blocks[0].shape, BF)] * 4
     outs += [shape((pages, 3, length, local), BF), shape((heads, length, length), F32), shape((2, 8, local), F32)]
     made = kernel_call(
-        functools.partial(attention_back_kernel, layer), "attention_back", outs, 9_000_000_000, *blocks, q, k, v, pb, w_qkv, w_out
+        functools.partial(attention_back_kernel, layer),
+        "attention_back",
+        outs,
+        9_000_000_000,
+        *blocks,
+        *near,
+        *far,
+        pbn,
+        pbf,
+        w_qkv,
+        w_out,
     )
     return made[:4], made[4:]
 
 
 def attention_grads_kernel(*refs):
-    rows_refs, grad_refs, (stack_ref, o_ref, place_ref, keep_ref, send_ref, acc_ref) = refs[:4], refs[4:8], refs[8:]
+    rows_refs, grad_refs, refs = refs[:4], refs[4:8], refs[8:]
+    stack_ref, on_ref, of_ref, place_ref, keep_ref, send_ref, acc_ref = refs
     pages, parts, length, local = stack_ref.shape
     size = rows_refs[0].shape[0] // pages
     acc_ref[...] = jnp.zeros(acc_ref.shape, F32)
@@ -467,7 +545,7 @@
     def step(page, carry):
         rows = page_rows(rows_refs, page, size)
         grad = page_rows(grad_refs, page, size)
-        acc_ref[:local] += mxu(o_ref[page], grad, TN)
+        acc_ref[:local] += mxu(jnp.concatenate([on_ref[page], of_ref[page]], axis=0), grad, TN)
         for t in range(parts):
             acc_ref[(t + 1) * local : (t + 2) * local] += mxu(stack_ref[page, t], rows, TN)
         return carry
@@ -480,7 +558,7 @@
 
 
 def attention_grads(rows, grads, stack, o, place):
-    local, width = o.shape[-1], rows[0].shape[-1]
+    local, width = o[0].shape[-1], rows[0].shape[-1]
     return kernel_call(
         attention_grads_kernel,
         "attention_grads",
@@ -489,7 +567,7 @@
         *rows,
         *grads,
         stack,
-        o,
+        *o,
         scalar(place),
         scratch=[pltpu.VMEM((4 * local, width), F32)],
     )
@@ -509,78 +587,60 @@
     return z.astype(BF), slope
 
 
-def forward_kernel(layer, c0, c1, c2, c3, up_ref, bias_ref, down_ref, p0, p1, p2, p3, z_ref, slope_ref):
-    size = 256
-    for block, (rows_ref, out_ref) in enumerate(zip((c0, c1, c2, c3), (p0, p1, p2, p3))):
-
-        def step(i, carry):
-            at = pl.ds(pl.multiple_of(i * size, size), size)
-            z, slope = up_rows(layer, rows_ref[at, :], up_ref, bias_ref)
-            z_ref[block, at, :] = z
-            slope_ref[block, at, :] = slope.astype(BF)
-            out_ref[at, :] = mxu(z, down_ref[layer], NN).astype(BF)
-            return carry
-
-        lax.fori_loop(0, rows_ref.shape[0] // size, step, 0)
-
-
-def feed_forward(layer, blocks, w_up, up_bias, w_down):
+def forward_kernel(layer, c0, c1, up_ref, bias_ref, down_ref, p0, p1, z_ref, slope_ref):
+    for block, (rows_ref, out_ref) in enumerate(((c0, p0), (c1, p1))):
+        z, slope = up_rows(layer, rows_ref[...], up_ref, bias_ref)
+        z_ref[block], slope_ref[block] = z, slope.astype(BF)
+        out_ref[...] = mxu(z, down_ref[layer], NN).astype(BF)
+
+
+def feed_forward(layer, pair, w_up, up_bias, w_down):
     units = w_up.shape[2]
-    size = blocks[0].shape[0]
-    outs = [shape(blocks[0].shape, BF)] * 4 + [shape((4, size, units), BF)] * 2
-    made = kernel_call(functools.partial(forward_kernel, layer), "feed_forward", outs, 4_000_000_000, *blocks, w_up, up_bias, w_down)
-    return made[:4], made[4:]
-
-
-def down_kernel(layer, z_ref, down_ref, p0, p1, p2, p3):
-    size = 256
-    for block, out_ref in enumerate((p0, p1, p2, p3)):
-
-        def step(i, carry):
-            at = pl.ds(pl.multiple_of(i * size, size), size)
-            out_ref[at, :] = mxu(z_ref[block, at, :], down_ref[layer], NN).astype(BF)
-            return carry
-
-        lax.fori_loop(0, out_ref.shape[0] // size, step, 0)
+    size = pair[0].shape[0]
+    outs = [shape(pair[0].shape, BF)] * 2 + [shape((2, size, units), BF)] * 2
+    made = kernel_call(
+        functools.partial(forward_kernel, layer), "feed_forward", outs, 2_000_000_000, *pair, w_up, up_bias, w_down
+    )
+    return made[:2], made[2], made[3]
+
+
+def down_kernel(layer, zn_ref, zf_ref, down_ref, *out_refs):
+    for block, out_ref in enumerate(out_refs):
+        out_ref[...] = mxu((zn_ref, zf_ref)[block // 2][block % 2], down_ref[layer], NN).astype(BF)
 
 
 def down_product(layer, z, w_down):
-    outs = [shape((z.shape[1], w_down.shape[2]), BF)] * 4
-    return kernel_call(functools.partial(down_kernel, layer), "down_product", outs, 1_500_000_000, z, w_down)
-
-
-def back_kernel(layer, g0, g1, g2, g3, slope_ref, up_ref, down_ref, p0, p1, p2, p3, gu_ref, sums_ref):
-    size = 256
+    outs = [shape((z[0].shape[1], w_down.shape[2]), BF)] * 4
+    return kernel_call(functools.partial(down_kernel, layer), "down_product", outs, 1_500_000_000, *z, w_down)
+
+
+def back_kernel(layer, g0, g1, g2, g3, sn_ref, sf_ref, up_ref, down_ref, p0, p1, p2, p3, gu_ref, sums_ref):
     sums_ref[...] = jnp.zeros(sums_ref.shape, F32)
     for block, (grad_ref, out_ref) in enumerate(zip((g0, g1, g2, g3), (p0, p1, p2, p3))):
-
-        def step(i, carry):
-            at = pl.ds(pl.multiple_of(i * size, size), size)
-            gz = mxu(grad_ref[at, :], down_ref[layer], NT)
-            gu = (gz * slope_ref[block, at, :].astype(F32)).astype(BF)
-            gu_ref[block, at, :] = gu
-            sums_ref[...] += fold_rows(gu.astype(F32))
-            out_ref[at, :] = mxu(gu, up_ref[layer], NT).astype(BF)
-            return carry
-
-        lax.fori_loop(0, grad_ref.shape[0] // size, step, 0)
+        gz = mxu(grad_ref[...], down_ref[layer], NT)
+        gu = (gz * (sn_ref, sf_ref)[block // 2][block % 2].astype(F32)).astype(BF)
+        gu_ref[block] = gu
+        sums_ref[...] += fold_rows(gu.astype(F32))
+        out_ref[...] = mxu(gu, up_ref[layer], NT).astype(BF)
 
 
 def feed_back(layer, blocks, slope, w_up, w_down):
     size, units = blocks[0].shape[0], w_up.shape[2]
     outs = [shape(blocks[0].shape, BF)] * 4 + [shape((4, size, units), BF), shape((8, units), F32)]
-    made = kernel_call(functools.partial(back_kernel, layer), "feed_back", outs, 4_000_000_000, *blocks, slope, w_up, w_down)
+    made = kernel_call(
+        functools.partial(back_kernel, layer), "feed_back", outs, 4_000_000_000, *blocks, *slope, w_up, w_down
+    )
     return made[:4], made[4:]
 
 
-def feed_grads_into(rows_refs, grad_refs, z_ref, gu_ref, place_ref, out_refs, both_ref):
+def feed_grads_into(rows_refs, grad_refs, z_of, gu_of, place_ref, out_refs, both_ref):
     unused, units, width = both_ref.shape
     step = 256
     for start in range(0, units, step):
         rows = slice(start, start + step)
-        down = sum(mxu(z_ref[i, :, rows], g[...], TN) for i, g in enumerate(grad_refs))
+        down = sum(mxu(z_of(i, rows), g[...], TN) for i, g in enumerate(grad_refs))
         both_ref[0, rows, :] = down.astype(BF)
-        up = sum(mxu(c[:, rows], gu_ref[i], TN) for i, c in enumerate(rows_refs))
+        up = sum(mxu(c[:, rows], gu_of(i), TN) for i, c in enumerate(rows_refs))
         both_ref[1, rows, :] = up.astype(BF)
     mine = place_ref[0] & 1
     parts = len(out_refs) // 2
@@ -592,11 +652,16 @@
 
 
 def feed_grads_kernel(*refs):
-    feed_grads_into(refs[:4], refs[4:8], refs[8], refs[9], refs[10], refs[11:-1], refs[-1])
+    zn, zf, gu, place_ref = refs[8:12]
+
+    def z_of(i, rows):
+        return (zn, zf)[i // 2][i % 2, :, rows]
+
+    feed_grads_into(refs[:4], refs[4:8], z_of, lambda i: gu[i], place_ref, refs[12:-1], refs[-1])
 
 
 def feed_grads(rows, grads, z, gu, place, parts):
-    units, width = z.shape[-1], rows[0].shape[-1]
+    units, width = gu.shape[-1], rows[0].shape[-1]
     made = kernel_call(
         feed_grads_kernel,
         "feed_grads",
@@ -604,7 +669,7 @@
         4_000_000_000,
         *rows,
         *grads,
-        z,
+        *z,
         gu,
         scalar(place),
         scratch=[pltpu.VMEM((2, units, width), BF)],
@@ -612,11 +677,8 @@
     return [made[2 * i : 2 * i + 2] for i in range(parts)]
 
 
-def both_kernel(layer, *refs):
-    rows_refs, grad_refs, (up_ref, bias_ref, down_ref, place_ref) = refs[:4], refs[4:8], refs[8:12]
-    out_refs, (z_ref, sums_ref, keep_ref, send_ref, gu_ref, both_ref) = refs[12:16], refs[16:]
-    sums_ref[...] = jnp.zeros(sums_ref.shape, F32)
-    for block in range(4):
+def both_pair(layer, rows_refs, grad_refs, up_ref, bias_ref, down_ref, out_refs, z_ref, gu_ref, sums_ref):
+    for block in range(2):
         gz = mxu(grad_refs[block][...], down_ref[layer], NT)
         z, slope = up_rows(layer, rows_refs[block][...], up_ref, bias_ref)
         z_ref[block] = z
@@ -624,28 +686,68 @@
         gu_ref[block] = gu
         sums_ref[...] += fold_rows(gu.astype(F32))
         out_refs[block][...] = mxu(gu, up_ref[layer], NT).astype(BF)
-    feed_grads_into(rows_refs, grad_refs, z_ref, gu_ref, place_ref, (keep_ref, send_ref), both_ref)
-
-
-def feed_both(layer, blocks, grads, w_up, up_bias, w_down, place):
-    size, units = blocks[0].shape[0], w_up.shape[2]
-    width = blocks[0].shape[1]
-    outs = [shape(blocks[0].shape, BF)] * 4 + [shape((4, size, units), BF), shape((8, units), F32)]
-    outs += [shape((units, width), BF)] * 2
+
+
+def both_near_kernel(layer, c0, c1, g0, g1, up_ref, bias_ref, down_ref, p0, p1, z_ref, gu_ref, sums_ref):
+    sums_ref[...] = jnp.zeros(sums_ref.shape, F32)
+    weights = (up_ref, bias_ref, down_ref)
+    both_pair(layer, (c0, c1), (g0, g1), *weights, (p0, p1), z_ref, gu_ref, sums_ref)
+
+
+def both_far_kernel(layer, *refs):
+    rows_refs, grad_refs, refs = refs[:4], refs[4:8], refs[8:]
+    zn, gun, sums_near, up_ref, bias_ref, down_ref, place_ref, p2, p3, z_ref, sums_ref, keep_ref, send_ref = refs[:13]
+    gu_ref, both_ref = refs[13:]
+    sums_ref[...] = sums_near[...]
+    weights = (up_ref, bias_ref, down_ref)
+    both_pair(layer, rows_refs[2:], grad_refs[2:], *weights, (p2, p3), z_ref, gu_ref, sums_ref)
+
+    def z_of(i, rows):
+        return (zn, z_ref)[i // 2][i % 2, :, rows]
+
+    def gu_of(i):
+        return (gun, gu_ref)[i // 2][i % 2]
+
+    feed_grads_into(rows_refs, grad_refs, z_of, gu_of, place_ref, (keep_ref, send_ref), both_ref)
+
+
+def both_near(layer, rows, grads, w_up, up_bias, w_down):
+    size, units = rows[0].shape[0], w_up.shape[2]
+    outs = [shape(rows[0].shape, BF)] * 2 + [shape((2, size, units), BF)] * 2 + [shape((8, units), F32)]
     made = kernel_call(
-        functools.partial(both_kernel, layer),
-        "feed_both",
+        functools.partial(both_near_kernel, layer),
+        "both_near",
         outs,
-        10_000_000_000,
-        *blocks,
+        3_000_000_000,
+        *rows,
         *grads,
         w_up,
         up_bias,
         w_down,
+    )
+    return made[:2], made[2:]
+
+
+def both_far(layer, rows, grads, near, w_up, up_bias, w_down, place):
+    size, units = rows[0].shape[0], w_up.shape[2]
+    width = rows[0].shape[1]
+    outs = [shape(rows[0].shape, BF)] * 2 + [shape((2, size, units), BF), shape((8, units), F32)]
+    outs += [shape((units, width), BF)] * 2
+    made = kernel_call(
+        functools.partial(both_far_kernel, layer),
+        "both_far",
+        outs,
+        7_000_000_000,
+        *rows,
+        *grads,
+        *near,
+        w_up,
+        up_bias,
+        w_down,
         scalar(place),
-        scratch=[pltpu.VMEM((4, size, units), BF), pltpu.VMEM((2, units, width), BF)],
-    )
-    return made[:4], made[4:6], made[6:]
+        scratch=[pltpu.VMEM((2, size, units), BF), pltpu.VMEM((2, units, width), BF)],
+    )
+    return made[:2], made[2], made[3], made[4:]
 
 
 def partners(bits, bit):
@@ -913,41 +1015,60 @@
         patch_rows, cotangent, masked, mask_emb.reshape(1, -1), ln1_gain, ln1_bias
     )
     rel_bias, ordered, pad_bias = bias_of_buckets(jnp.swapaxes(rel_table, 0, 1), buckets, pad_flags.T, member)
-    blocks = spread(own, (rel_bias,))
-    last_blocks = spread(tied(last_own, blocks[3]))
-
+    last_blocks = None
     kept = []
     for layer in range(LAYERS):
-        rows_one, before = blocks, hidden
-        partial, saved = attention(layer, rows_one, w_qkv, qv_bias, rel_bias, pad_bias, w_out)
-        near, far, unused = collect(partial)
-        middle, own = add_norm(hidden, near + [far], (layer, layer), out_bias, ln2_gain, ln2_bias)
-        rows_two = spread(own)
+        before = hidden
+        near, far = swap_core(own), swap_chip(own)
+        q_near = project(layer, (own, near), w_qkv, qv_bias)
+        far = tied(far, (q_near, rel_bias))
+        rows_one = [own, near, far, swap_core(far)]
+        if last_blocks is None:
+            last_blocks = spread(tied(last_own, rows_one[3]))
+        other, q_far, saved_far = attention_far(
+            layer, rows_one[2:], q_near, w_qkv, qv_bias, rel_bias, pad_bias, w_out
+        )
+        sent = other[0] + swap_core(other[1])
+        arriving = swap_chip(sent)
+        mine, saved_near = attention_near(
+            layer, own.shape, [tied(q_near[0], sent), *q_near[1:]], q_far, rel_bias, pad_bias, w_out
+        )
+        terms = [mine[0], swap_core(mine[1]), tied(arriving, mine)]
+        middle, own = add_norm(hidden, terms, (layer, layer), out_bias, ln2_gain, ln2_bias)
+        saved = (q_near, q_far, saved_near, saved_far)
+        near, far = swap_core(own), swap_chip(own)
         if layer == last:
-            partial, (z, up_sums), mlp = feed_both(
-                layer, rows_two, last_blocks, w_up, up_bias, w_down, places[1]
+            partial, near_made = both_near(layer, (own, near), last_blocks[:2], w_up, up_bias, w_down)
+            far = tied(far, near_made)
+            rows_two = [own, near, far, swap_core(far)]
+            other, z, up_sums, mlp = both_far(
+                layer, rows_two, last_blocks, near_made, w_up, up_bias, w_down, places[1]
             )
-            kept.append((rows_one, before, saved, middle, rows_two, z, None))
+            partial = [*partial, *other]
+            kept.append((rows_one, before, saved, middle, rows_two, (near_made[0], z), None))
         else:
-            partial, (z, slope) = feed_forward(layer, rows_two, w_up, up_bias, w_down)
+            partial, *near_made = feed_forward(layer, (own, near), w_up, up_bias, w_down)
+            far = tied(far, near_made)
+            rows_two = [own, near, far, swap_core(far)]
+            other, *far_made = feed_forward(layer, rows_two[2:], w_up, up_bias, w_down)
+            z, slope = zip(near_made, far_made)
             kept.append((rows_one, before, saved, middle, rows_two, z, slope))
-            near, far, unused = collect(partial)
+            near, far, unused = collect([*partial, *other])
             hidden, own = add_norm(middle, near + [far], (layer, layer + 1), down_bias, ln1_gain, ln1_bias)
-            blocks = spread(own)
 
     rows_one, before, saved, middle, rows_two, z, unused = kept[last]
     near, far, sent = collect(partial)
     mlp1 = PageSum(mlp, bits, places, 1)
     g1, low, twos1 = norm_back(last_own, near + [far], middle, last, ln2_gain)
-    result_parts = down_product(last, tied(z, low), w_down)
+    result_parts = down_product(last, (tied(z[0], low), z[1]), w_down)
     token = mlp1.step(result_parts[0])
     out_blocks = spread(low, (result_parts, token))
     partial, (stack, totals, qv1) = attention_back(last, out_blocks, saved, w_qkv, w_out)
     near, far, sent = collect(partial)
-    mix = attention_grads(rows_one, out_blocks, tied(stack, sent), saved[-1], places[1])
-    mix1 = PageSum(mix, bits, places, 1)
+    mix = attention_grads(rows_one, out_blocks, tied(stack, sent), (saved[2][1], saved[3][1]), places[0])
+    mix1 = PageSum(mix, bits, places, 0)
     token = mlp1.step(mix)
-    far = tied(far, token)
+    far = tied(far, (token,))
     grad, low, ones1 = norm_back(g1, near + [far], before, last, ln1_gain)
     rel1 = sum_by_bucket(tied(totals, low), ordered)
     token = mix1.step(rel1)
@@ -957,22 +1078,22 @@
     rows_one, before, saved, middle, rows_two, z, slope = kept[0]
     partial, (gu, up0) = feed_back(0, grad_blocks, slope, w_up, w_down)
     near, far, sent = collect(partial)
-    mlp = feed_grads(rows_two, grad_blocks, tied(z, sent), gu, places[1], 2)
+    mlp = feed_grads(rows_two, grad_blocks, z, tied(gu, sent), places[1], 2)
     mlp0a, mlp0b = [PageSum(x, bits, places, 1) for x in mlp]
     token = mix1.step(mlp)
-    far = tied(far, token)
+    far = tied(far, (token,))
     g1, low, twos0 = norm_back(grad, near + [far], middle, 0, ln2_gain)
     token = mlp1.step(low)
     token = mlp0a.step(token)
     out_blocks = spread(low, (token,))
     partial, (stack, totals, qv0) = attention_back(0, out_blocks, saved, w_qkv, w_out)
     near, far, sent = collect(partial)
-    mix = attention_grads(rows_one, out_blocks, tied(stack, sent), saved[-1], places[1])
+    mix = attention_grads(rows_one, out_blocks, tied(stack, sent), (saved[2][1], saved[3][1]), places[1])
     mix0 = PageSum(mix, bits, places, 1)
     token = mlp1.step(mix)
     token = mlp0b.step(token)
     token = mix1.step(token)
-    far = tied(far, token)
+    far = tied(far, (token,))
     grad, ones0 = last_norm_back(g1, near + [far], before, ln1_gain, masked)
 
     def hop(values, axis, order, bit):
@@ -982,38 +1103,38 @@
     rows_got = hop(rows, "tensor", [0, 1], 0)
     token = rows
     token = mlp0a.step(token)
+    token = mlp0b.step(token)
     token = mix0.step(token)
     rows = token = rows + tied(rows_got, token)
     rows_got = hop(rows, "tensor", [0, 1], 1)
     rel0 = token = sum_by_bucket(tied(totals, token), ordered)
     result_near, result_far, unused = collect([tied(p, rel0) for p in result_parts])
-    token = mlp0b.step(token)
     small = pack_all(rows + tied(rows_got, token), (qv0, qv1), (up0, up1), (rel0, rel1))
     small_got = hop(small, "dp", bits, 0)
     token = small
     token = mlp0a.step(token)
+    token = mlp0b.step(token)
     token = mix0.step(token)
     small = token = small + tied(small_got, token)
     small_got = hop(small, "dp", bits, 1)
+    token = mix1.step(token)
     result = token = last_result(
         kept[last][3], result_near + [tied(result_far, token)], last, down_bias, pages
     )
-    token = mix1.step(token)
-    token = mlp0b.step(token)
+    token = mlp0a.step(token)
     small = token = small + tied(small_got, token)
     small_got = hop(small, "dp", bits, 2)
-    token = mlp0a.step(token)
+    token = mlp0b.step(token)
     d_mlp = assemble_feed(last, 0, 1, mlp1, tied(places[1], token))
     token = d_mlp[0]
     token = mix0.step(token)
     small = small + tied(small_got, token)
     small = token = sum_small(small, "dp", bits[3:], len(bits))
-    token = mlp0b.step(token)
-    d_mix = assemble_attention(last, mix1, tied(places[1], token))
+    d_mlp = assemble_feed(0, 0, 2, mlp0a, tied(places[1], token), d_mlp)
+    token = d_mlp[0]
+    d_mix = assemble_attention(last, mix1, tied(places[0], token))
     token = d_mix[0]
     token = mix0.step(token)
-    d_mlp = assemble_feed(0, 0, 2, mlp0a, tied(places[1], token), d_mlp)
-    token = d_mlp[0]
     d_mlp = assemble_feed(0, 1, 2, mlp0b, tied(places[1], token), d_mlp)
     token = d_mlp[0]
     d_mix = assemble_attention(0, mix0, tied(places[1], token), d_mix)

time: 369 us -> 351 us (0.951)
  waiting for transfers between devices: 192 us -> 163 us
  local copies, waits for them, and re-layouts: 16.6 us -> 26.7 us
  Pallas kernels: 82.6 us -> 86.9 us
    ppermute x5, waiting for transfers between devices: 21.9 us -> 6.74 us  [hop(): return lax.ppermute(values, axis, partners(order, bit))]
    ppermute x16, waiting for transfers between devices: 82.7 us -> 69.3 us  [swap_chip(): return lax.ppermute(values, 'tensor', CHIP)]
    unnamed x174 -> x246, local copies, waits for them, and re-layouts: 15.9 us -> 26 us
    ppermute x32, starting transfers between devices: 3.33 us -> 12.3 us  [swap_core(): return lax.ppermute(values, 'tensor', CORE)]
    ppermute x25, starting transfers between devices: 36.5 us -> 29.1 us  [swap(): lax.ppermute(values, ('dp', 'tensor'), crossed_partners(self.bits, bit, s...]
    ppermute x16, starting transfers between devices: 24.1 us -> 16.8 us  [swap_chip(): return lax.ppermute(values, 'tensor', CHIP)]
    pallas_call x36 -> x42, Pallas kernels: 73.8 us -> 78.1 us  [kernel_call(): pl.pallas_call(body, out_shape=tuple(outs), in_specs=specs, out_specs=tup...]
  transfers between devices with their start and end apart: 78 -> 78, of which waited for: 37 -> 43; matrix products, arithmetic and copies ran while one was open for 1% -> 1% of each run, Pallas kernels for 10% -> 16%
where the time goes in v4:
time: 351 us; the launch traced here: 348 us
  waiting for transfers between devices  163 us (46%)
  Pallas kernels  86.9 us (25%)
  starting transfers between devices  66 us (19%)
  local copies, waits for them, and re-layouts  26.7 us (8%)
    pallas_call x42, Pallas kernels, kernel_call(): pl.pallas_call(body, out_shape=tuple(outs), in_specs=specs, out_specs=tup...  78.1 us
    ppermute x16, waiting for transfers between devices, swap_chip(): return lax.ppermute(values, 'tensor', CHIP)  69.3 us
    ppermute x25, waiting for transfers between devices, swap(): lax.ppermute(values, ('dp', 'tensor'), crossed_partners(self.bits, bit, s...  66.4 us
    ppermute x25, starting transfers between devices, swap(): lax.ppermute(values, ('dp', 'tensor'), crossed_partners(self.bits, bit, s...  29.1 us
    unnamed x246, local copies, waits for them, and re-layouts  26 us
    ppermute x32, waiting for transfers between devices, swap_core(): return lax.ppermute(values, 'tensor', CORE)  20.4 us
    ppermute x16, starting transfers between devices, swap_chip(): return lax.ppermute(values, 'tensor', CHIP)  16.8 us
    ppermute x32, starting transfers between devices, swap_core(): return lax.ppermute(values, 'tensor', CORE)  12.3 us
  transfers between devices with their start and end apart: 78, of which 43 were waited for; matrix products, arithmetic and copies ran while one was open for 1% of the time, Pallas kernels for 16%

profile of v4, /device:TPU:0, one launch (start us, length us, event | category | flops | bytes accessed | tf_op | source)
XLA Modules:
  0.0 347.6 jit_solution(7965307633458673218)
XLA Ops:
  5.4 2.0 first_norm.1
  8.7 2.5 collective-permute-start.1
  13.5 5.0 %bias_of_buckets.1 = (bf16[2,3,256,256]{3,2,1,0:T(8,128)(2,1)S(1)}, s32[256,256]{1,0:T(8,128)S(1)}, f32[4,1,256]{2,1,0:T(1,128)S(1)}) custom-call(bf16[3,2,732]{2,1,0:T(2,128)(2,1)S(1)} %bitcast.15, s32[256,256]{1,0:T(8,128)S(1)} %copy-done.97, s32[4,256]{1,0:T(4,128)S(1)} %bitcast.18, s32[1]{0:T(128)} %bitcast.4.member_ref), custom_call_target="tpu_custom_call" | custom-call | flops 40000000 | bytes 13277 | tf_op jit(solution)/shard_map/bias_of_buckets/pallas_call | solution.py:42
  18.6 1.7 copy-done.1
  23.6 3.7 %attention_far.2 = (bf16[256,768]{1,0:T(8,128)(2,1)S(1)}, bf16[256,768]{1,0:T(8,128)(2,1)S(1)}, bf16[2,256,192]{2,1,0:T(8,128)(2,1)S(1)}, bf16[2,256,192]{2,1,0:...) custom-call(bf16[256,768]{1,0:T(8,128)(2,1)S(1)} %collective-permute, ...), custom_call_target="tpu_custom_call" | custom-call | flops 40000000 | bytes 66903 | tf_op jit(solution)/shard_map/attention_far/pallas_call | solution.py:42
  30.9 2.9 attention_near.2
  35.4 5.9 %collective-permute-done.5.three_ref = bf16[256,768]{1,0:T(8,128)(2,1)S(1)} collective-permute-done((bf16[256,768]{1,0:T(8,128)(2,1)S(1)}, bf16[256,768]{1,0:T(8,128)(2,1)S(1)}, u32[]{:S(2)}, u32[]{:S(2)}) %collective-permute-start.5) | collective-permute-done | bytes 393248 | tf_op jit(solution)/shard_map/ppermute | solution.py:63
  43.6 2.0 feed_forward.2
  47.5 5.9 %collective-permute-done.8.c0.refs_2_ = bf16[256,768]{1,0:T(8,128)(2,1)S(1)} collective-permute-done((bf16[256,768]{1,0:T(8,128)(2,1)S(1)}, bf16[256,768]{1,0:T(8,128)(2,1)S(1)}, u32[]{:S(2)}, u32[]{:S(2)}) %collective-permute-start.8) | collective-permute-done | bytes 393248 | tf_op jit(solution)/shard_map/ppermute | solution.py:63
  53.5 1.7 collective-permute-done.9.c1.refs_3_
  55.2 2.0 feed_forward.3
  60.0 10.4 %collective-permute-done.11.three_ref = bf16[256,768]{1,0:T(8,128)(2,1)S(1)} collective-permute-done((bf16[256,768]{1,0:T(8,128)(2,1)S(1)}, bf16[256,768]{1,0:T(8,128)(2,1)S(1)}, u32[]{:S(2)}, u32[]{:S(2)}) %collective-permute-start.11) | collective-permute-done | bytes 393248 | tf_op jit(solution)/shard_map/ppermute | solution.py:63
  73.5 9.0 %collective-permute-done.13.x2.refs_2_ = bf16[256,768]{1,0:T(8,128)(2,1)S(1)} collective-permute-done((bf16[256,768]{1,0:T(8,128)(2,1)S(1)}, bf16[256,768]{1,0:T(8,128)(2,1)S(1)}, u32[]{:S(2)}, u32[]{:S(2)}) %collective-permute-start.13) | collective-permute-done | bytes 393248 | tf_op jit(solution)/shard_map/ppermute | solution.py:63
  82.5 1.7 collective-permute-done.14.x3.refs_3_
  84.2 3.7 %attention_far.3 = (bf16[256,768]{1,0:T(8,128)(2,1)S(1)}, bf16[256,768]{1,0:T(8,128)(2,1)S(1)}, bf16[2,256,192]{2,1,0:T(8,128)(2,1)S(1)}, bf16[2,256,192]{2,1,0:...) custom-call(bf16[256,768]{1,0:T(8,128)(2,1)S(1)} %collective-permute, ...), custom_call_target="tpu_custom_call" | custom-call | flops 40000000 | bytes 66903 | tf_op jit(solution)/shard_map/attention_far/pallas_call | solution.py:42
  90.7 3.3 attention_near.3
  96.4 5.5 %collective-permute-done.17.three_ref = bf16[256,768]{1,0:T(8,128)(2,1)S(1)} collective-permute-done((bf16[256,768]{1,0:T(8,128)(2,1)S(1)}, bf16[256,768]{1,0:T(8,128)(2,1)S(1)}, u32[]{:S(2)}, u32[]{:S(2)}) %collective-permute-start.17) | collective-permute-done | bytes 393248 | tf_op jit(solution)/shard_map/ppermute | solution.py:63
  104.0 6.5 %collective-permute-done.23.refs_6_ = bf16[256,768]{1,0:T(8,128)(2,1)} collective-permute-done((bf16[256,768]{1,0:T(8,128)(2,1)S(1)}, bf16[256,768]{1,0:T(8,128)(2,1)}, u32[]{:S(2)}, u32[]{:S(2)}) %collective-permute-start.23) | collective-permute-done | bytes 393248 | tf_op jit(solution)/shard_map/ppermute | solution.py:63
  110.5 2.9 both_near.1
  118.1 2.1 collective-permute-done.22.refs_3_
  120.1 1.7 copy-done.5
  127.0 7.6 %both_far.1 = (bf16[256,768]{1,0:T(8,128)(2,1)S(1)}, bf16[256,768]{1,0:T(8,128)(2,1)S(1)}, bf16[2,256,768]{2,1,0:T(8,128)(2,1)S(1)}, f32[8,768]{1,0:T(8,128)S(1)...) custom-call(bf16[256,768]{1,0:T(8,128)(2,1)S(1)} %copy-done.30, bf16[256,768]{1,0:T(8,128)(2,1)S(1)} %copy-done.32, ...), custom_call_target="tpu_custom_call" | custom-call | flops 70000000 | bytes 134215 | tf_op jit(solution)/shard_map/both_far/pallas_call | solution.py:42
  138.1 10.0 %collective-permute-done.26.three_ref = bf16[256,768]{1,0:T(8,128)(2,1)S(1)} collective-permute-done((bf16[256,768]{1,0:T(8,128)(2,1)S(1)}, bf16[256,768]{1,0:T(8,128)(2,1)S(1)}, u32[]{:S(2)}, u32[]{:S(2)}) %collective-permute-start.26) | collective-permute-done | bytes 393248 | tf_op jit(solution)/shard_map/ppermute | solution.py:63
  151.4 8.0 %collective-permute-done.28.g2.refs_6_ = bf16[256,768]{1,0:T(8,128)(2,1)S(1)} collective-permute-done((bf16[256,768]{1,0:T(8,128)(2,1)S(1)}, bf16[256,768]{1,0:T(8,128)(2,1)S(1)}, u32[]{:S(2)}, u32[]{:S(2)}) %collective-permute-start.28) | collective-permute-done | bytes 393248 | tf_op jit(solution)/shard_map/ppermute | solution.py:63
  159.4 1.7 collective-permute-done.30.g3.refs_7_
  161.3 6.5 %attention_back.2 = (bf16[256,768]{1,0:T(8,128)(2,1)S(1)}, bf16[256,768]{1,0:T(8,128)(2,1)S(1)}, bf16[256,768]{1,0:T(8,128)(2,1)S(1)}, bf16[256,768]{1,0:T(8,128...) custom-call(bf16[256,768]{1,0:T(8,128)(2,1)S(1)} %get-tuple-element.256.g0.re, ...), custom_call_target="tpu_custom_call" | custom-call | flops 90000000 | bytes 102359 | tf_op jit(solution)/shard_map/attention_back/pallas_call | solution.py:42
  168.0 1.7 collective-permute-start.34
  170.7 2.0 attention_grads.2
  173.7 4.2 %collective-permute-done.34 = bf16[384,768]{1,0:T(8,128)(2,1)S(1)} collective-permute-done((bf16[384,768]{1,0:T(8,128)(2,1)S(1)}, bf16[384,768]{1,0:T(8,128)(2,1)S(1)}, u32[]{:S(2)}, u32[]{:S(2)}) %collective-permute-start.34) | collective-permute-done | bytes 589856 | tf_op jit(solution)/shard_map/ppermute | solution.py:816
  178.1 2.9 collective-permute-done.33.three_ref
  182.6 4.0 %sum_by_bucket.2.rel1 = f32[72,32]{1,0:T(8,128)S(1)} custom-call(f32[3,256,256]{2,1,0:T(8,128)S(1)} %get-tuple-element.288.values_ref, s32[256,256]{1,0:T(8,128)S(1)} %copy-done.70), custom_call_target="tpu_custom_call" | custom-call | flops 60000000 | bytes 10577 | tf_op jit(solution)/shard_map/sum_by_bucket/pallas_call | solution.py:42
  186.6 2.5 collective-permute-done.37.got_ref
  189.2 2.7 collective-permute-done.36.g2.refs_6_
  191.9 1.7 collective-permute-done.38.g3.refs_7_
  193.7 2.9 feed_back.1
  199.4 1.8 collective-permute-start.42
  201.2 2.6 collective-permute-start.46
  203.8 3.4 feed_grads.1
  208.2 7.0 %collective-permute-done.42 = bf16[192,768]{1,0:T(8,128)(2,1)S(1)} collective-permute-done((bf16[192,768]{1,0:T(8,128)(2,1)S(1)}, bf16[192,768]{1,0:T(8,128)(2,1)S(1)}, u32[]{:S(2)}, u32[]{:S(2)}) %collective-permute-start.42) | collective-permute-done | bytes 294944 | tf_op jit(solution)/shard_map/ppermute | solution.py:816
  217.5 12.7 %collective-permute-done.46 = bf16[384,768]{1,0:T(8,128)(2,1)S(1)} collective-permute-done((bf16[384,768]{1,0:T(8,128)(2,1)S(1)}, bf16[384,768]{1,0:T(8,128)(2,1)S(1)}, u32[]{:S(2)}, u32[]{:S(2)}) %collective-permute-start.46) | collective-permute-done | bytes 589856 | tf_op jit(solution)/shard_map/ppermute | solution.py:816
  230.8 1.6 collective-permute-done.47.g3.refs_7_
  232.5 6.4 %attention_back.3 = (bf16[256,768]{1,0:T(8,128)(2,1)S(1)}, bf16[256,768]{1,0:T(8,128)(2,1)S(1)}, bf16[256,768]{1,0:T(8,128)(2,1)S(1)}, bf16[256,768]{1,0:T(8,128...) custom-call(bf16[256,768]{1,0:T(8,128)(2,1)S(1)} %get-tuple-element.308.g0.re, ...), custom_call_target="tpu_custom_call" | custom-call | flops 90000000 | bytes 102359 | tf_op jit(solution)/shard_map/attention_back/pallas_call | solution.py:42
  241.3 2.2 attention_grads.3
  246.2 2.8 collective-permute-done.52.got_ref
  249.4 4.5 %collective-permute-done.51 = bf16[192,768]{1,0:T(8,128)(2,1)S(1)} collective-permute-done((bf16[192,768]{1,0:T(8,128)(2,1)S(1)}, bf16[192,768]{1,0:T(8,128)(2,1)S(1)}, u32[]{:S(2)}, u32[]{:S(2)}) %collective-permute-start.51) | collective-permute-done | bytes 294944 | tf_op jit(solution)/shard_map/ppermute | solution.py:816
  255.4 1.9 last_norm_back.1
  257.3 3.1 collective-permute-start.54
  261.4 4.1 %collective-permute-done.56 = bf16[192,768]{1,0:T(8,128)(2,1)S(1)} collective-permute-done((bf16[192,768]{1,0:T(8,128)(2,1)S(1)}, bf16[192,768]{1,0:T(8,128)(2,1)S(1)}, u32[]{:S(2)}, u32[]{:S(2)}) %collective-permute-start.56) | collective-permute-done | bytes 294944 | tf_op jit(solution)/shard_map/ppermute | solution.py:816
  267.0 4.0 %sum_by_bucket.3.rel0 = f32[72,32]{1,0:T(8,128)S(1)} custom-call(f32[3,256,256]{2,1,0:T(8,128)S(1)} %get-tuple-element.345.values_ref, s32[256,256]{1,0:T(8,128)S(1)} %copy-done.70), custom_call_target="tpu_custom_call" | custom-call | flops 60000000 | bytes 10577 | tf_op jit(solution)/shard_map/sum_by_bucket/pallas_call | solution.py:42
  271.7 2.5 collective-permute-start.66
  275.4 2.8 collective-permute-done.62
  278.7 1.9 collective-permute-done.65
  282.5 6.2 %collective-permute-done.66 = bf16[192,768]{1,0:T(8,128)(2,1)S(1)} collective-permute-done((bf16[192,768]{1,0:T(8,128)(2,1)S(1)}, bf16[192,768]{1,0:T(8,128)(2,1)S(1)}, u32[]{:S(2)}, u32[]{:S(2)}) %collective-permute-start.66) | collective-permute-done | bytes 294944 | tf_op jit(solution)/shard_map/ppermute | solution.py:816
  290.0 8.3 %collective-permute-start.58 = (bf16[256,768]{1,0:T(8,128)(2,1)S(1)}, bf16[256,768]{1,0:T(8,128)(2,1)S(1)}, u32[]{:S(2)}, u32[]{:S(2)}) collective-permute-start(bf16[256,768]{1,0:T(8,128)(2,1)S(1)} %get-tuple-element.347), channel_id=1, source_target_pairs={{0,1},{1,0},{2,3},{3,2},{4,5},{5,4},{6,7},{7,6},{8,9},{9,8},{10,11... | collective-permute-start | bytes 1179656 | tf_op jit(solution)/shard_map/ppermute | solution.py:59
  298.4 2.9 collective-permute-start.68
  301.6 2.1 collective-permute-start.72
  305.0 2.3 collective-permute-done.68.got_ref
  308.2 2.3 collective-permute-start.70
  311.7 9.2 %collective-permute-done.72.got_ref = bf16[192,768]{1,0:T(8,128)(2,1)S(1)} collective-permute-done((bf16[192,768]{1,0:T(8,128)(2,1)S(1)}, bf16[192,768]{1,0:T(8,128)(2,1)S(1)}, u32[]{:S(2)}, u32[]{:S(2)}) %collective-permute-start.72) | collective-permute-done | bytes 294944 | tf_op jit(solution)/shard_map/ppermute | solution.py:816
  321.0 2.5 assemble_feed.3
  323.7 2.3 collective-permute-start.69
  326.4 3.9 %collective-permute-done.69 = f32[48,768]{1,0:T(8,128)S(1)} collective-permute-done((f32[48,768]{1,0:T(8,128)S(1)}, f32[48,768]{1,0:T(8,128)S(1)}, u32[]{:S(2)}, u32[]{:S(2)}) %collective-permute-start.69) | collective-permute-done | bytes 147488 | tf_op jit(solution)/shard_map/ppermute | solution.py:1100
  336.8 2.6 collective-permute-done.77.got_ref
  341.0 4.7 %collective-permute-done.76.got_ref = bf16[384,768]{1,0:T(8,128)(2,1)S(1)} collective-permute-done((bf16[384,768]{1,0:T(8,128)(2,1)S(1)}, bf16[384,768]{1,0:T(8,128)(2,1)S(1)}, u32[]{:S(2)}, u32[]{:S(2)}) %collective-permute-start.76) | collective-permute-done | bytes 589856 | tf_op jit(solution)/shard_map/ppermute | solution.py:816
  (410 shorter events, 90.0 us)
Async XLA Ops:
  8.2 10.3 %collective-permute-start = (bf16[256,768]{1,0:T(8,128)(2,1)S(1)}, bf16[256,768]{1,0:T(8,128)(2,1)S(1)}, u32[]{:S(2)}, u32[]{:S(2)}) collective-permute-start(bf16[256,768]{1,0:T(8,128)(2,1)S(1)} %get-tuple-element.206.x0.refs_0_), channel_id=1, source_target_pairs={{0,1},{1,0},{2,3},{3,2},{4,5},{5,4},{6,7},{7,6},{8,9},{9,8},{10,11... | collective-permute-start | bytes 1179656 | tf_op jit(solution)/shard_map/ppermute | solution.py:59
  8.7 13.1 %collective-permute-start.1 = (bf16[256,768]{1,0:T(8,128)(2,1)S(1)}, bf16[256,768]{1,0:T(8,128)(2,1)S(1)}, u32[]{:S(2)}, u32[]{:S(2)}) collective-permute-start(bf16[256,768]{1,0:T(8,128)(2,1)S(1)} %get-tuple-element.206.x0.refs_0_), channel_id=1, source_target_pairs={{0,2},{1,3},{2,0},{3,1},{4,6},{5,7},{6,4},{7,5},{8,10},{9,11},{10,... | collective-permute-start | bytes 1179656 | tf_op jit(solution)/shard_map/ppermute | solution.py:63
  30.0 11.3 %collective-permute-start.5 = (bf16[256,768]{1,0:T(8,128)(2,1)S(1)}, bf16[256,768]{1,0:T(8,128)(2,1)S(1)}, u32[]{:S(2)}, u32[]{:S(2)}) collective-permute-start(bf16[256,768]{1,0:T(8,128)(2,1)S(1)} %add.69), channel_id=1, source_target_pairs={{0,2},{1,3},{2,0},{3,1},{4,6},{5,7},{6,4},{7,5},{8,10},{9,11},{10,... | collective-permute-start | bytes 1179656 | tf_op jit(solution)/shard_map/ppermute | solution.py:63
  35.4 5.9 %collective-permute-start.4 = (bf16[256,768]{1,0:T(8,128)(2,1)S(1)}, bf16[256,768]{1,0:T(8,128)(2,1)S(1)}, u32[]{:S(2)}, u32[]{:S(2)}) collective-permute-start(bf16[256,768]{1,0:T(8,128)(2,1)S(1)} %get-tuple-element.219), channel_id=1, source_target_pairs={{0,1},{1,0},{2,3},{3,2},{4,5},{5,4},{6,7},{7,6},{8,9},{9,8},{10,11... | collective-permute-start | bytes 1179656 | tf_op jit(solution)/shard_map/ppermute | solution.py:59
  41.9 11.5 %collective-permute-start.8 = (bf16[256,768]{1,0:T(8,128)(2,1)S(1)}, bf16[256,768]{1,0:T(8,128)(2,1)S(1)}, u32[]{:S(2)}, u32[]{:S(2)}) collective-permute-start(bf16[256,768]{1,0:T(8,128)(2,1)S(1)} %get-tuple-element.222.c0.refs_0_), channel_id=1, source_target_pairs={{0,2},{1,3},{2,0},{3,1},{4,6},{5,7},{6,4},{7,5},{8,10},{9,11},{10,... | collective-permute-start | bytes 1179656 | tf_op jit(solution)/shard_map/ppermute | solution.py:63
  57.5 2.5 collective-permute-start.7
  59.2 11.2 %collective-permute-start.11 = (bf16[256,768]{1,0:T(8,128)(2,1)S(1)}, bf16[256,768]{1,0:T(8,128)(2,1)S(1)}, u32[]{:S(2)}, u32[]{:S(2)}) collective-permute-start(bf16[256,768]{1,0:T(8,128)(2,1)S(1)} %add.70), channel_id=1, source_target_pairs={{0,2},{1,3},{2,0},{3,1},{4,6},{5,7},{6,4},{7,5},{8,10},{9,11},{10,... | collective-permute-start | bytes 1179656 | tf_op jit(solution)/shard_map/ppermute | solution.py:63
  71.0 11.5 %collective-permute-start.13 = (bf16[256,768]{1,0:T(8,128)(2,1)S(1)}, bf16[256,768]{1,0:T(8,128)(2,1)S(1)}, u32[]{:S(2)}, u32[]{:S(2)}) collective-permute-start(bf16[256,768]{1,0:T(8,128)(2,1)S(1)} %get-tuple-element.231.x0.refs_0_), channel_id=1, source_target_pairs={{0,2},{1,3},{2,0},{3,1},{4,6},{5,7},{6,4},{7,5},{8,10},{9,11},{10,... | collective-permute-start | bytes 1179656 | tf_op jit(solution)/shard_map/ppermute | solution.py:63
  89.9 12.0 %collective-permute-start.17 = (bf16[256,768]{1,0:T(8,128)(2,1)S(1)}, bf16[256,768]{1,0:T(8,128)(2,1)S(1)}, u32[]{:S(2)}, u32[]{:S(2)}) collective-permute-start(bf16[256,768]{1,0:T(8,128)(2,1)S(1)} %add.71), channel_id=1, source_target_pairs={{0,2},{1,3},{2,0},{3,1},{4,6},{5,7},{6,4},{7,5},{8,10},{9,11},{10,... | collective-permute-start | bytes 1179656 | tf_op jit(solution)/shard_map/ppermute | solution.py:63
  94.9 7.0 %collective-permute-start.16 = (bf16[256,768]{1,0:T(8,128)(2,1)S(1)}, bf16[256,768]{1,0:T(8,128)(2,1)S(1)}, u32[]{:S(2)}, u32[]{:S(2)}) collective-permute-start(bf16[256,768]{1,0:T(8,128)(2,1)S(1)} %get-tuple-element.242), channel_id=1, source_target_pairs={{0,1},{1,0},{2,3},{3,2},{4,5},{5,4},{6,7},{7,6},{8,9},{9,8},{10,11... | collective-permute-start | bytes 1179656 | tf_op jit(solution)/shard_map/ppermute | solution.py:59
  94.9 15.5 %collective-permute-start.23 = (bf16[256,768]{1,0:T(8,128)(2,1)S(1)}, bf16[256,768]{1,0:T(8,128)(2,1)}, u32[]{:S(2)}, u32[]{:S(2)}) collective-permute-start(bf16[256,768]{1,0:T(8,128)(2,1)S(1)} %get-tuple-element.247.g0.refs_4_.grad_ref), channel_id=1, source_target_pairs={{0,2},{1,3},{2,0},{3,1},{4,6},{5,7},{6,4},{7,5},{8,10},{9,11},{10,... | collective-permute-start | bytes 1179656 | tf_op jit(solution)/shard_map/ppermute | solution.py:63
  96.2 14.2 %collective-permute-start.19 = (bf16[256,768]{1,0:T(8,128)(2,1)S(1)}, bf16[256,768]{1,0:T(8,128)(2,1)S(1)}, u32[]{:S(2)}, u32[]{:S(2)}) collective-permute-start(bf16[256,768]{1,0:T(8,128)(2,1)S(1)} %get-tuple-element.247.g0.refs_4_.grad_ref), channel_id=1, source_target_pairs={{0,1},{1,0},{2,3},{3,2},{4,5},{5,4},{6,7},{7,6},{8,9},{9,8},{10,11... | collective-permute-start | bytes 1179656 | tf_op jit(solution)/shard_map/ppermute | solution.py:59
  103.2 7.2 %collective-permute-start.18 = (bf16[256,768]{1,0:T(8,128)(2,1)S(1)}, bf16[256,768]{1,0:T(8,128)(2,1)S(1)}, u32[]{:S(2)}, u32[]{:S(2)}) collective-permute-start(bf16[256,768]{1,0:T(8,128)(2,1)S(1)} %get-tuple-element.245.c0.refs_0_), channel_id=1, source_target_pairs={{0,1},{1,0},{2,3},{3,2},{4,5},{5,4},{6,7},{7,6},{8,9},{9,8},{10,11... | collective-permute-start | bytes 1179656 | tf_op jit(solution)/shard_map/ppermute | solution.py:59
  103.2 14.8 %collective-permute-start.21 = (bf16[256,768]{1,0:T(8,128)(2,1)S(1)}, bf16[256,768]{1,0:T(8,128)(2,1)}, u32[]{:S(2)}, u32[]{:S(2)}) collective-permute-start(bf16[256,768]{1,0:T(8,128)(2,1)S(1)} %get-tuple-element.245.c0.refs_0_), channel_id=1, source_target_pairs={{0,2},{1,3},{2,0},{3,1},{4,6},{5,7},{6,4},{7,5},{8,10},{9,11},{10,... | collective-permute-start | bytes 1179656 | tf_op jit(solution)/shard_map/ppermute | solution.py:63
  110.4 7.6 %collective-permute-start.24 = (bf16[256,768]{1,0:T(8,128)(2,1)}, bf16[256,768]{1,0:T(8,128)(2,1)}, u32[]{:S(2)}, u32[]{:S(2)}) collective-permute-start(bf16[256,768]{1,0:T(8,128)(2,1)} %collective-permute-done.23.refs_6_), channel_id=1, source_target_pairs={{0,1},{1,0},{2,3},{3,2},{4,5},{5,4},{6,7},{7,6},{8,9},{9,8},{10,11... | collective-permute-start | bytes 1179656 | tf_op jit(solution)/shard_map/ppermute | solution.py:59
  118.1 2.1 collective-permute-start.22
  134.9 16.2 %collective-permute-start.29 = (bf16[768,768]{1,0:T(8,128)(2,1)S(1)}, bf16[768,768]{1,0:T(8,128)(2,1)S(1)}, u32[]{:S(2)}, u32[]{:S(2)}) collective-permute-start(bf16[768,768]{1,0:T(8,128)(2,1)S(1)} %get-tuple-element.265), channel_id=1, source_target_pairs={{0,4},{1,9},{2,6},{3,11},{4,0},{5,13},{6,2},{7,15},{8,12},{9,1},{1... | collective-permute-start | bytes 3538952 | tf_op jit(solution)/shard_map/ppermute | solution.py:816
  136.7 11.4 %collective-permute-start.26 = (bf16[256,768]{1,0:T(8,128)(2,1)S(1)}, bf16[256,768]{1,0:T(8,128)(2,1)S(1)}, u32[]{:S(2)}, u32[]{:S(2)}) collective-permute-start(bf16[256,768]{1,0:T(8,128)(2,1)S(1)} %add.72), channel_id=1, source_target_pairs={{0,2},{1,3},{2,0},{3,1},{4,6},{5,7},{6,4},{7,5},{8,10},{9,11},{10,... | collective-permute-start | bytes 1179656 | tf_op jit(solution)/shard_map/ppermute | solution.py:63
  148.8 10.6 %collective-permute-start.28 = (bf16[256,768]{1,0:T(8,128)(2,1)S(1)}, bf16[256,768]{1,0:T(8,128)(2,1)S(1)}, u32[]{:S(2)}, u32[]{:S(2)}) collective-permute-start(bf16[256,768]{1,0:T(8,128)(2,1)S(1)} %get-tuple-element.256.g0.refs_4_), channel_id=1, source_target_pairs={{0,2},{1,3},{2,0},{3,1},{4,6},{5,7},{6,4},{7,5},{8,10},{9,11},{10,... | collective-permute-start | bytes 1179656 | tf_op jit(solution)/shard_map/ppermute | solution.py:63
  149.6 9.8 %collective-permute-start.27 = (bf16[256,768]{1,0:T(8,128)(2,1)S(1)}, bf16[256,768]{1,0:T(8,128)(2,1)S(1)}, u32[]{:S(2)}, u32[]{:S(2)}) collective-permute-start(bf16[256,768]{1,0:T(8,128)(2,1)S(1)} %get-tuple-element.256.g0.refs_4_), channel_id=1, source_target_pairs={{0,1},{1,0},{2,3},{3,2},{4,5},{5,4},{6,7},{7,6},{8,9},{9,8},{10,11... | collective-permute-start | bytes 1179656 | tf_op jit(solution)/shard_map/ppermute | solution.py:59
  167.8 1.9 collective-permute-start.32
  168.0 9.9 %collective-permute-start.34 = (bf16[384,768]{1,0:T(8,128)(2,1)S(1)}, bf16[384,768]{1,0:T(8,128)(2,1)S(1)}, u32[]{:S(2)}, u32[]{:S(2)}) collective-permute-start(bf16[384,768]{1,0:T(8,128)(2,1)S(1)} %get-tuple-element.267), channel_id=1, source_target_pairs={{0,8},{1,5},{2,10},{3,7},{4,12},{5,1},{6,14},{7,3},{8,0},{9,13},{1... | collective-permute-start | bytes 1769480 | tf_op jit(solution)/shard_map/ppermute | solution.py:816
  169.9 11.1 %collective-permute-start.33 = (bf16[256,768]{1,0:T(8,128)(2,1)S(1)}, bf16[256,768]{1,0:T(8,128)(2,1)S(1)}, u32[]{:S(2)}, u32[]{:S(2)}) collective-permute-start(bf16[256,768]{1,0:T(8,128)(2,1)S(1)} %add.73), channel_id=1, source_target_pairs={{0,2},{1,3},{2,0},{3,1},{4,6},{5,7},{6,4},{7,5},{8,10},{9,11},{10,... | collective-permute-start | bytes 1179656 | tf_op jit(solution)/shard_map/ppermute | solution.py:63
  170.7 10.3 %collective-permute-start.31 = (bf16[256,768]{1,0:T(8,128)(2,1)S(1)}, bf16[256,768]{1,0:T(8,128)(2,1)S(1)}, u32[]{:S(2)}, u32[]{:S(2)}) collective-permute-start(bf16[256,768]{1,0:T(8,128)(2,1)S(1)} %get-tuple-element.273), channel_id=1, source_target_pairs={{0,1},{1,0},{2,3},{3,2},{4,5},{5,4},{6,7},{7,6},{8,9},{9,8},{10,11... | collective-permute-start | bytes 1179656 | tf_op jit(solution)/shard_map/ppermute | solution.py:59
  172.7 16.3 %collective-permute-start.37 = (bf16[384,768]{1,0:T(8,128)(2,1)S(1)}, bf16[384,768]{1,0:T(8,128)(2,1)S(1)}, u32[]{:S(2)}, u32[]{:S(2)}) collective-permute-start(bf16[384,768]{1,0:T(8,128)(2,1)S(1)} %get-tuple-element.282), channel_id=1, source_target_pairs={{0,4},{1,5},{2,6},{3,7},{4,0},{5,1},{6,2},{7,3},{8,12},{9,13},{10,... | collective-permute-start | bytes 1769480 | tf_op jit(solution)/shard_map/ppermute | solution.py:816
  181.7 10.2 %collective-permute-start.36 = (bf16[256,768]{1,0:T(8,128)(2,1)S(1)}, bf16[256,768]{1,0:T(8,128)(2,1)S(1)}, u32[]{:S(2)}, u32[]{:S(2)}) collective-permute-start(bf16[256,768]{1,0:T(8,128)(2,1)S(1)} %get-tuple-element.286.g0.refs_4_), channel_id=1, source_target_pairs={{0,2},{1,3},{2,0},{3,1},{4,6},{5,7},{6,4},{7,5},{8,10},{9,11},{10,... | collective-permute-start | bytes 1179656 | tf_op jit(solution)/shard_map/ppermute | solution.py:63
  182.5 9.4 %collective-permute-start.35 = (bf16[256,768]{1,0:T(8,128)(2,1)S(1)}, bf16[256,768]{1,0:T(8,128)(2,1)S(1)}, u32[]{:S(2)}, u32[]{:S(2)}) collective-permute-start(bf16[256,768]{1,0:T(8,128)(2,1)S(1)} %get-tuple-element.286.g0.refs_4_), channel_id=1, source_target_pairs={{0,1},{1,0},{2,3},{3,2},{4,5},{5,4},{6,7},{7,6},{8,9},{9,8},{10,11... | collective-permute-start | bytes 1179656 | tf_op jit(solution)/shard_map/ppermute | solution.py:59
  198.5 16.8 %collective-permute-start.41 = (bf16[256,768]{1,0:T(8,128)(2,1)S(1)}, bf16[256,768]{1,0:T(8,128)(2,1)S(1)}, u32[]{:S(2)}, u32[]{:S(2)}) collective-permute-start(bf16[256,768]{1,0:T(8,128)(2,1)S(1)} %add.75), channel_id=1, source_target_pairs={{0,2},{1,3},{2,0},{3,1},{4,6},{5,7},{6,4},{7,5},{8,10},{9,11},{10,... | collective-permute-start | bytes 1179656 | tf_op jit(solution)/shard_map/ppermute | solution.py:63
  199.3 15.9 %collective-permute-start.39 = (bf16[256,768]{1,0:T(8,128)(2,1)S(1)}, bf16[256,768]{1,0:T(8,128)(2,1)S(1)}, u32[]{:S(2)}, u32[]{:S(2)}) collective-permute-start(bf16[256,768]{1,0:T(8,128)(2,1)S(1)} %get-tuple-element.295), channel_id=1, source_target_pairs={{0,1},{1,0},{2,3},{3,2},{4,5},{5,4},{6,7},{7,6},{8,9},{9,8},{10,11... | collective-permute-start | bytes 1179656 | tf_op jit(solution)/shard_map/ppermute | solution.py:59
  199.4 15.8 %collective-permute-start.42 = (bf16[192,768]{1,0:T(8,128)(2,1)S(1)}, bf16[192,768]{1,0:T(8,128)(2,1)S(1)}, u32[]{:S(2)}, u32[]{:S(2)}) collective-permute-start(bf16[192,768]{1,0:T(8,128)(2,1)S(1)} %get-tuple-element.291), channel_id=1, source_target_pairs={{0,8},{1,9},{2,10},{3,11},{4,12},{5,13},{6,14},{7,15},{8,0},{9,1},... | collective-permute-start | bytes 884744 | tf_op jit(solution)/shard_map/ppermute | solution.py:816
  201.2 29.0 %collective-permute-start.46 = (bf16[384,768]{1,0:T(8,128)(2,1)S(1)}, bf16[384,768]{1,0:T(8,128)(2,1)S(1)}, u32[]{:S(2)}, u32[]{:S(2)}) collective-permute-start(bf16[384,768]{1,0:T(8,128)(2,1)S(1)} %add.74), channel_id=1, source_target_pairs={{0,16},{1,17},{2,18},{3,19},{4,20},{5,21},{6,22},{7,23},{8,24},{9,... | collective-permute-start | bytes 1769480 | tf_op jit(solution)/shard_map/ppermute | solution.py:816
  207.3 23.1 %collective-permute-start.45 = (bf16[384,768]{1,0:T(8,128)(2,1)S(1)}, bf16[384,768]{1,0:T(8,128)(2,1)S(1)}, u32[]{:S(2)}, u32[]{:S(2)}) collective-permute-start(bf16[384,768]{1,0:T(8,128)(2,1)S(1)} %get-tuple-element.303), channel_id=1, source_target_pairs={{0,4},{1,9},{2,6},{3,11},{4,0},{5,13},{6,2},{7,15},{8,12},{9,1},{1... | collective-permute-start | bytes 1769480 | tf_op jit(solution)/shard_map/ppermute | solution.py:816
  216.1 14.5 %collective-permute-start.44 = (bf16[256,768]{1,0:T(8,128)(2,1)S(1)}, bf16[256,768]{1,0:T(8,128)(2,1)S(1)}, u32[]{:S(2)}, u32[]{:S(2)}) collective-permute-start(bf16[256,768]{1,0:T(8,128)(2,1)S(1)} %get-tuple-element.308.g0.refs_4_), channel_id=1, source_target_pairs={{0,2},{1,3},{2,0},{3,1},{4,6},{5,7},{6,4},{7,5},{8,10},{9,11},{10,... | collective-permute-start | bytes 1179656 | tf_op jit(solution)/shard_map/ppermute | solution.py:63
  217.5 13.3 %collective-permute-start.43 = (bf16[256,768]{1,0:T(8,128)(2,1)S(1)}, bf16[256,768]{1,0:T(8,128)(2,1)S(1)}, u32[]{:S(2)}, u32[]{:S(2)}) collective-permute-start(bf16[256,768]{1,0:T(8,128)(2,1)S(1)} %get-tuple-element.308.g0.refs_4_), channel_id=1, source_target_pairs={{0,1},{1,0},{2,3},{3,2},{4,5},{5,4},{6,7},{7,6},{8,9},{9,8},{10,11... | collective-permute-start | bytes 1179656 | tf_op jit(solution)/shard_map/ppermute | solution.py:59
  230.7 15.4 %collective-permute-start.53 = (bf16[384,768]{1,0:T(8,128)(2,1)S(1)}, bf16[384,768]{1,0:T(8,128)(2,1)S(1)}, u32[]{:S(2)}, u32[]{:S(2)}) collective-permute-start(bf16[384,768]{1,0:T(8,128)(2,1)S(1)} %add.77.own_ref), channel_id=1, source_target_pairs={{0,8},{1,5},{2,10},{3,7},{4,12},{5,1},{6,14},{7,3},{8,0},{9,13},{1... | collective-permute-start | bytes 1769480 | tf_op jit(solution)/shard_map/ppermute | solution.py:816
  238.9 2.3 collective-permute-start.49
  239.1 9.9 %collective-permute-start.52 = (bf16[384,768]{1,0:T(8,128)(2,1)S(1)}, bf16[384,768]{1,0:T(8,128)(2,1)S(1)}, u32[]{:S(2)}, u32[]{:S(2)}) collective-permute-start(bf16[384,768]{1,0:T(8,128)(2,1)S(1)} %get-tuple-element.305), channel_id=1, source_target_pairs={{0,4},{1,9},{2,6},{3,11},{4,0},{5,13},{6,2},{7,15},{8,12},{9,1},{1... | collective-permute-start | bytes 1769480 | tf_op jit(solution)/shard_map/ppermute | solution.py:816
  239.9 14.0 %collective-permute-start.51 = (bf16[192,768]{1,0:T(8,128)(2,1)S(1)}, bf16[192,768]{1,0:T(8,128)(2,1)S(1)}, u32[]{:S(2)}, u32[]{:S(2)}) collective-permute-start(bf16[192,768]{1,0:T(8,128)(2,1)S(1)} %add.76), channel_id=1, source_target_pairs={{0,16},{1,17},{2,18},{3,19},{4,20},{5,21},{6,22},{7,23},{8,24},{9,... | collective-permute-start | bytes 884744 | tf_op jit(solution)/shard_map/ppermute | solution.py:816
  243.5 23.4 %collective-permute-start.55 = (bf16[384,768]{1,0:T(8,128)(2,1)S(1)}, bf16[384,768]{1,0:T(8,128)(2,1)S(1)}, u32[]{:S(2)}, u32[]{:S(2)}) collective-permute-start(bf16[384,768]{1,0:T(8,128)(2,1)S(1)} %get-tuple-element.327), channel_id=1, source_target_pairs={{0,4},{1,9},{2,6},{3,11},{4,0},{5,13},{6,2},{7,15},{8,12},{9,1},{1... | collective-permute-start | bytes 1769480 | tf_op jit(solution)/shard_map/ppermute | solution.py:816
  244.7 10.6 %collective-permute-start.50 = (bf16[256,768]{1,0:T(8,128)(2,1)S(1)}, bf16[256,768]{1,0:T(8,128)(2,1)S(1)}, u32[]{:S(2)}, u32[]{:S(2)}) collective-permute-start(bf16[256,768]{1,0:T(8,128)(2,1)S(1)} %add.78), channel_id=1, source_target_pairs={{0,2},{1,3},{2,0},{3,1},{4,6},{5,7},{6,4},{7,5},{8,10},{9,11},{10,... | collective-permute-start | bytes 1179656 | tf_op jit(solution)/shard_map/ppermute | solution.py:63
  246.1 9.3 %collective-permute-start.48 = (bf16[256,768]{1,0:T(8,128)(2,1)S(1)}, bf16[256,768]{1,0:T(8,128)(2,1)S(1)}, u32[]{:S(2)}, u32[]{:S(2)}) collective-permute-start(bf16[256,768]{1,0:T(8,128)(2,1)S(1)} %get-tuple-element.319), channel_id=1, source_target_pairs={{0,1},{1,0},{2,3},{3,2},{4,5},{5,4},{6,7},{7,6},{8,9},{9,8},{10,11... | collective-permute-start | bytes 1179656 | tf_op jit(solution)/shard_map/ppermute | solution.py:59
  248.9 12.4 %collective-permute-start.57 = (bf16[192,768]{1,0:T(8,128)(2,1)S(1)}, bf16[192,768]{1,0:T(8,128)(2,1)S(1)}, u32[]{:S(2)}, u32[]{:S(2)}) collective-permute-start(bf16[192,768]{1,0:T(8,128)(2,1)S(1)} %get-tuple-element.311), channel_id=1, source_target_pairs={{0,8},{1,5},{2,10},{3,7},{4,12},{5,1},{6,14},{7,3},{8,0},{9,13},{1... | collective-permute-start | bytes 884744 | tf_op jit(solution)/shard_map/ppermute | solution.py:816
  253.9 11.6 %collective-permute-start.56 = (bf16[192,768]{1,0:T(8,128)(2,1)S(1)}, bf16[192,768]{1,0:T(8,128)(2,1)S(1)}, u32[]{:S(2)}, u32[]{:S(2)}) collective-permute-start(bf16[192,768]{1,0:T(8,128)(2,1)S(1)} %get-tuple-element.330), channel_id=1, source_target_pairs={{0,8},{1,5},{2,10},{3,7},{4,12},{5,1},{6,14},{7,3},{8,0},{9,13},{1... | collective-permute-start | bytes 884744 | tf_op jit(solution)/shard_map/ppermute | solution.py:816
  257.3 9.7 %collective-permute-start.54 = (f32[16,768]{1,0:T(8,128)S(1)}, f32[16,768]{1,0:T(8,128)S(1)}, u32[]{:S(2)}, u32[]{:S(2)}) collective-permute-start(f32[16,768]{1,0:T(8,128)S(1)} %pack_rows.1), channel_id=1, source_target_pairs={{0,1},{1,0},{2,3},{3,2},{4,5},{5,4},{6,7},{7,6},{8,9},{9,8},{10,11... | collective-permute-start | bytes 147464 | tf_op jit(solution)/shard_map/ppermute | solution.py:1100
  260.5 60.5 %collective-permute-start.71 = (bf16[768,768]{1,0:T(8,128)(2,1)S(1)}, bf16[768,768]{1,0:T(8,128)(2,1)S(1)}, u32[]{:S(2)}, u32[]{:S(2)}) collective-permute-start(bf16[768,768]{1,0:T(8,128)(2,1)S(1)} %join.5.own_ref), channel_id=1, source_target_pairs={{0,4},{1,9},{2,6},{3,11},{4,0},{5,13},{6,2},{7,15},{8,12},{9,1},{1... | collective-permute-start | bytes 3538952 | tf_op jit(solution)/shard_map/ppermute | solution.py:816
  265.5 15.0 %collective-permute-start.65 = (bf16[192,768]{1,0:T(8,128)(2,1)S(1)}, bf16[192,768]{1,0:T(8,128)(2,1)S(1)}, u32[]{:S(2)}, u32[]{:S(2)}) collective-permute-start(bf16[192,768]{1,0:T(8,128)(2,1)S(1)} %add.81), channel_id=1, source_target_pairs={{0,16},{1,17},{2,18},{3,19},{4,20},{5,21},{6,22},{7,23},{8,24},{9,... | collective-permute-start | bytes 884744 | tf_op jit(solution)/shard_map/ppermute | solution.py:816
  271.1 10.6 %collective-permute-start.59 = (bf16[256,768]{1,0:T(8,128)(2,1)S(1)}, bf16[256,768]{1,0:T(8,128)(2,1)S(1)}, u32[]{:S(2)}, u32[]{:S(2)}) collective-permute-start(bf16[256,768]{1,0:T(8,128)(2,1)S(1)} %get-tuple-element.349), channel_id=1, source_target_pairs={{0,1},{1,0},{2,3},{3,2},{4,5},{5,4},{6,7},{7,6},{8,9},{9,8},{10,11... | collective-permute-start | bytes 1179656 | tf_op jit(solution)/shard_map/ppermute | solution.py:59
  271.7 17.0 %collective-permute-start.66 = (bf16[192,768]{1,0:T(8,128)(2,1)S(1)}, bf16[192,768]{1,0:T(8,128)(2,1)S(1)}, u32[]{:S(2)}, u32[]{:S(2)}) collective-permute-start(bf16[192,768]{1,0:T(8,128)(2,1)S(1)} %add.80), channel_id=1, source_target_pairs={{0,16},{1,17},{2,18},{3,19},{4,20},{5,21},{6,22},{7,23},{8,24},{9,... | collective-permute-start | bytes 884744 | tf_op jit(solution)/shard_map/ppermute | solution.py:816
  274.1 4.1 %collective-permute-start.62 = (f32[16,768]{1,0:T(8,128)S(1)}, f32[16,768]{1,0:T(8,128)S(1)}, u32[]{:S(2)}, u32[]{:S(2)}) collective-permute-start(f32[16,768]{1,0:T(8,128)S(1)} %add.82), channel_id=1, source_target_pairs={{0,2},{1,3},{2,0},{3,1},{4,6},{5,7},{6,4},{7,5},{8,10},{9,11},{10,... | collective-permute-start | bytes 147464 | tf_op jit(solution)/shard_map/ppermute | solution.py:1100
  278.2 20.1 %collective-permute-start.64 = (bf16[192,768]{1,0:T(8,128)(2,1)S(1)}, bf16[192,768]{1,0:T(8,128)(2,1)S(1)}, u32[]{:S(2)}, u32[]{:S(2)}) collective-permute-start(bf16[192,768]{1,0:T(8,128)(2,1)S(1)} %get-tuple-element.343), channel_id=1, source_target_pairs={{0,8},{1,5},{2,10},{3,7},{4,12},{5,1},{6,14},{7,3},{8,0},{9,13},{1... | collective-permute-start | bytes 884744 | tf_op jit(solution)/shard_map/ppermute | solution.py:816
  280.6 9.4 %collective-permute-start.63 = (f32[48,768]{1,0:T(8,128)S(1)}, f32[48,768]{1,0:T(8,128)S(1)}, u32[]{:S(2)}, u32[]{:S(2)}) collective-permute-start(f32[48,768]{1,0:T(8,128)S(1)} %pack_all.1), channel_id=1, source_target_pairs={{0,4},{4,0},{8,12},{12,8},{16,20},{20,16},{24,28},{28,24},{1,5},{5... | collective-permute-start | bytes 442376 | tf_op jit(solution)/shard_map/ppermute | solution.py:1100
  281.6 19.8 %collective-permute-start.61 = (bf16[192,768]{1,0:T(8,128)(2,1)S(1)}, bf16[192,768]{1,0:T(8,128)(2,1)S(1)}, u32[]{:S(2)}, u32[]{:S(2)}) collective-permute-start(bf16[192,768]{1,0:T(8,128)(2,1)S(1)} %add.79.own_ref), channel_id=1, source_target_pairs={{0,8},{1,9},{2,10},{3,11},{4,12},{5,13},{6,14},{7,15},{8,0},{9,1},... | collective-permute-start | bytes 884744 | tf_op jit(solution)/shard_map/ppermute | solution.py:816
  288.6 12.9 %collective-permute-start.60 = (bf16[256,768]{1,0:T(8,128)(2,1)S(1)}, bf16[256,768]{1,0:T(8,128)(2,1)S(1)}, u32[]{:S(2)}, u32[]{:S(2)}) collective-permute-start(bf16[256,768]{1,0:T(8,128)(2,1)S(1)} %add.83), channel_id=1, source_target_pairs={{0,2},{1,3},{2,0},{3,1},{4,6},{5,7},{6,4},{7,5},{8,10},{9,11},{10,... | collective-permute-start | bytes 1179656 | tf_op jit(solution)/shard_map/ppermute | solution.py:63
  290.0 13.7 %collective-permute-start.58 = (bf16[256,768]{1,0:T(8,128)(2,1)S(1)}, bf16[256,768]{1,0:T(8,128)(2,1)S(1)}, u32[]{:S(2)}, u32[]{:S(2)}) collective-permute-start(bf16[256,768]{1,0:T(8,128)(2,1)S(1)} %get-tuple-element.347), channel_id=1, source_target_pairs={{0,1},{1,0},{2,3},{3,2},{4,5},{5,4},{6,7},{7,6},{8,9},{9,8},{10,11... | collective-permute-start | bytes 1179656 | tf_op jit(solution)/shard_map/ppermute | solution.py:59
  298.4 8.9 %collective-permute-start.68 = (bf16[192,768]{1,0:T(8,128)(2,1)S(1)}, bf16[192,768]{1,0:T(8,128)(2,1)S(1)}, u32[]{:S(2)}, u32[]{:S(2)}) collective-permute-start(bf16[192,768]{1,0:T(8,128)(2,1)S(1)} %add.85.own_ref), channel_id=1, source_target_pairs={{0,8},{1,5},{2,10},{3,7},{4,12},{5,1},{6,14},{7,3},{8,0},{9,13},{1... | collective-permute-start | bytes 884744 | tf_op jit(solution)/shard_map/ppermute | solution.py:816
  301.4 9.1 %collective-permute-start.67 = (f32[48,768]{1,0:T(8,128)S(1)}, f32[48,768]{1,0:T(8,128)S(1)}, u32[]{:S(2)}, u32[]{:S(2)}) collective-permute-start(f32[48,768]{1,0:T(8,128)S(1)} %add.88), channel_id=1, source_target_pairs={{0,8},{4,12},{8,0},{12,4},{16,24},{20,28},{24,16},{28,20},{1,9},{5... | collective-permute-start | bytes 442376 | tf_op jit(solution)/shard_map/ppermute | solution.py:1100
  301.6 19.4 %collective-permute-start.72 = (bf16[192,768]{1,0:T(8,128)(2,1)S(1)}, bf16[192,768]{1,0:T(8,128)(2,1)S(1)}, u32[]{:S(2)}, u32[]{:S(2)}) collective-permute-start(bf16[192,768]{1,0:T(8,128)(2,1)S(1)} %add.86.own_ref), channel_id=1, source_target_pairs={{0,8},{1,5},{2,10},{3,7},{4,12},{5,1},{6,14},{7,3},{8,0},{9,13},{1... | collective-permute-start | bytes 884744 | tf_op jit(solution)/shard_map/ppermute | solution.py:816
  307.3 23.0 %collective-permute-start.75 = (bf16[384,768]{1,0:T(8,128)(2,1)S(1)}, bf16[384,768]{1,0:T(8,128)(2,1)S(1)}, u32[]{:S(2)}, u32[]{:S(2)}) collective-permute-start(bf16[384,768]{1,0:T(8,128)(2,1)S(1)} %join.7.own_ref), channel_id=1, source_target_pairs={{0,4},{1,9},{2,6},{3,11},{4,0},{5,13},{6,2},{7,15},{8,12},{9,1},{1... | collective-permute-start | bytes 1769480 | tf_op jit(solution)/shard_map/ppermute | solution.py:816
  308.2 15.3 %collective-permute-start.70 = (bf16[192,768]{1,0:T(8,128)(2,1)S(1)}, bf16[192,768]{1,0:T(8,128)(2,1)S(1)}, u32[]{:S(2)}, u32[]{:S(2)}) collective-permute-start(bf16[192,768]{1,0:T(8,128)(2,1)S(1)} %add.87), channel_id=1, source_target_pairs={{0,16},{1,17},{2,18},{3,19},{4,20},{5,21},{6,22},{7,23},{8,24},{9,... | collective-permute-start | bytes 884744 | tf_op jit(solution)/shard_map/ppermute | solution.py:816
  310.5 22.0 %collective-permute-start.74 = (bf16[384,768]{1,0:T(8,128)(2,1)S(1)}, bf16[384,768]{1,0:T(8,128)(2,1)S(1)}, u32[]{:S(2)}, u32[]{:S(2)}) collective-permute-start(bf16[384,768]{1,0:T(8,128)(2,1)S(1)} %join.6.own_ref), channel_id=1, source_target_pairs={{0,4},{1,5},{2,6},{3,7},{4,0},{5,1},{6,2},{7,3},{8,12},{9,13},{10,... | collective-permute-start | bytes 1769480 | tf_op jit(solution)/shard_map/ppermute | solution.py:816
  323.6 11.7 %collective-permute-start.73 = (bf16[192,768]{1,0:T(8,128)(2,1)S(1)}, bf16[192,768]{1,0:T(8,128)(2,1)S(1)}, u32[]{:S(2)}, u32[]{:S(2)}) collective-permute-start(bf16[192,768]{1,0:T(8,128)(2,1)S(1)} %add.90.own_ref), channel_id=1, source_target_pairs={{0,8},{1,5},{2,10},{3,7},{4,12},{5,1},{6,14},{7,3},{8,0},{9,13},{1... | collective-permute-start | bytes 884744 | tf_op jit(solution)/shard_map/ppermute | solution.py:816
  323.7 6.6 %collective-permute-start.69 = (f32[48,768]{1,0:T(8,128)S(1)}, f32[48,768]{1,0:T(8,128)S(1)}, u32[]{:S(2)}, u32[]{:S(2)}) collective-permute-start(f32[48,768]{1,0:T(8,128)S(1)} %add.89), channel_id=1, source_target_pairs={{0,16},{4,20},{8,24},{12,28},{16,0},{20,4},{24,8},{28,12},{1,17},{... | collective-permute-start | bytes 442376 | tf_op jit(solution)/shard_map/ppermute | solution.py:1100
  326.0 13.4 %collective-permute-start.77 = (bf16[384,768]{1,0:T(8,128)(2,1)S(1)}, bf16[384,768]{1,0:T(8,128)(2,1)S(1)}, u32[]{:S(2)}, u32[]{:S(2)}) collective-permute-start(bf16[384,768]{1,0:T(8,128)(2,1)S(1)} %join.8.own_ref), channel_id=1, source_target_pairs={{0,4},{1,9},{2,6},{3,11},{4,0},{5,13},{6,2},{7,15},{8,12},{9,1},{1... | collective-permute-start | bytes 1769480 | tf_op jit(solution)/shard_map/ppermute | solution.py:816
  335.3 10.4 %collective-permute-start.76 = (bf16[384,768]{1,0:T(8,128)(2,1)S(1)}, bf16[384,768]{1,0:T(8,128)(2,1)S(1)}, u32[]{:S(2)}, u32[]{:S(2)}) collective-permute-start(bf16[384,768]{1,0:T(8,128)(2,1)S(1)} %join.9.own_ref), channel_id=1, source_target_pairs={{0,4},{1,9},{2,6},{3,11},{4,0},{5,13},{6,2},{7,15},{8,12},{9,1},{1... | collective-permute-start | bytes 1769480 | tf_op jit(solution)/shard_map/ppermute | solution.py:816
  (137 other events, 1105.0 us)
